TPU v7x, 256 devices: a whole 4x4x8 slice. The times are simulated.
256 devices in a mesh: seq: 32 (over y_lo, z, core), head: 8 (over x, y_hi).
Axes of the slice: x: 4, y: 4 (y_hi: 2, y_lo: 2; y = y_hi * 2 + y_lo), z: 8, core: 2. Of those that a mesh axis runs over, the one named last changes fastest.
Arguments:
- queries: bfloat16 [12288, 5120], P('seq', 'head'), may hold values from -256 to 256
- keys: bfloat16 [12288, 5120], P('seq', 'head'), may hold values from -10 to 10
- values: bfloat16 [12288, 5120], P('seq', 'head'), may hold values from -18 to 18
- ref_keys: bfloat16 [1536, 5120], P('seq', 'head'), may hold values from -9 to 9
- ref_values: bfloat16 [1536, 5120], P('seq', 'head'), may hold values from -18 to 18
- out_weight: bfloat16 [5120, 5120], P('head'), may hold values from -0.078125 to 0.078125
Outputs:
- projected: bfloat16 [12288, 5120], P('seq', 'head')
All inputs are finite; a program needn't handle non-finite values.
Results may differ from a plain program's by a relative error of at most 0.018.
Values may be sent and summed in bfloat16 or wider, within the bound.
No kernel may reach another device: no remote copies, remote signals or barrier semaphores. Data moves between devices by JAX's collectives and lax.ppermute only.
A program may use at most 128 MiB of HBM per device.

v0:
```python
import math

import jax
import jax.numpy as jnp
from jax import lax
from jax.sharding import PartitionSpec as P

HD = 128


def partner(value, axis, apart):
    return lax.ppermute(value, axis, [(i, i ^ 1 << apart) for i in range(lax.axis_size(axis))])


def attend(query_heads, key_rows, value_rows):
    heads = query_heads.shape[1]
    width = query_heads.shape[2]
    key_heads = key_rows.reshape(key_rows.shape[0], heads, width)
    value_heads = value_rows.reshape(value_rows.shape[0], heads, width)
    scores = jnp.einsum(
        "thd,shd->hts", query_heads, key_heads, preferred_element_type=jnp.float32
    ) * (1.0 / math.sqrt(width))
    maxima = jnp.max(scores, axis=2)
    weights = jnp.exp(scores - maxima[:, :, None])
    totals = jnp.sum(weights, axis=2)
    summed = jnp.einsum(
        "hts,shd->htd",
        weights.astype(jnp.bfloat16),
        value_heads,
        preferred_element_type=jnp.float32,
    )
    return (maxima, totals, summed)


def combine(first, second):
    maxima = jnp.maximum(first[0], second[0])
    first_factor = jnp.exp(first[0] - maxima)
    second_factor = jnp.exp(second[0] - maxima)
    totals = first[1] * first_factor + second[1] * second_factor
    summed = first[2] * first_factor[:, :, None] + second[2] * second_factor[:, :, None]
    return (maxima, totals, summed)


def body(queries, keys, values, ref_keys, ref_values, out_weight):
    tok_rows = queries.shape[0]
    heads = out_weight.shape[0] // HD
    query_heads = queries.reshape(tok_rows, heads, HD)
    state = attend(query_heads, keys, values)
    held_keys = keys
    held_values = values
    for bit_number in range(2):
        got_keys, got_values = partner((held_keys, held_values), "seq", bit_number)
        state = combine(state, attend(query_heads, got_keys, got_values))
        held_keys = jnp.concatenate([held_keys, got_keys], axis=0)
        held_values = jnp.concatenate([held_values, got_values], axis=0)
    state = combine(
        state,
        attend(
            query_heads,
            lax.all_gather(ref_keys, "seq", axis=0, tiled=True),
            lax.all_gather(ref_values, "seq", axis=0, tiled=True),
        ),
    )
    attended = (state[2] / state[1][:, :, None]).astype(jnp.bfloat16)
    attended = attended.transpose(1, 0, 2).reshape(tok_rows, heads * HD)
    flipped = lax.psum_scatter(
        lax.dot_general(
            out_weight, attended, (((0,), (1,)), ((), ())), preferred_element_type=jnp.float32
        ).astype(jnp.bfloat16),
        "head",
        scatter_dimension=0,
        tiled=True,
    ).astype(jnp.float32)
    return flipped.T.astype(jnp.bfloat16)


def solution(mesh):
    placed = (
        P("seq", "head"),
        P("seq", "head"),
        P("seq", "head"),
        P("seq", "head"),
        P("seq", "head"),
        P("head", None),
    )
    return jax.shard_map(
        body, mesh=mesh, in_specs=placed, out_specs=P("seq", "head"), check_vma=False
    )
```

profile of v0, /device:TPU:8, one launch (start us, length us, event | category | flops | bytes accessed | tf_op | source)
XLA Modules:
  0.0 263.5 jit_solution(7759311872670865399)
XLA Ops:
  6.5 0.0 copy-start.7
  6.5 0.0 all-gather.3.cloned.1.call-start
  6.5 0.7 all-gather.3.cloned.1.call-update
  7.3 0.0 all-gather.5.cloned.1.call-start
  7.3 1.3 copy.40
  8.6 0.0 copy-start.4
  8.6 0.1 collective-permute-start
  8.7 0.5 collective-permute-start.1
  9.2 0.0 all-gather.5.cloned.1.call-update
  9.2 0.0 reduce-scatter.4.cloned.1.call-start
  9.3 2.0 copy.43
  11.3 1.3 copy.39
  12.6 0.0 collective-permute-done
  12.6 0.0 copy-start.8
  12.6 1.1 pad_maximum_fusion
  13.7 1.9 collective-permute-start.2
  15.7 0.0 collective-permute-done.1
  15.7 0.0 copy-done.7
  15.7 1.1 pad_maximum_fusion.1
  16.8 0.0 copy-done.4
  16.8 0.1 collective-permute-start.3
  16.9 0.0 copy-done.8
  16.9 0.0 copy-done.9
  16.9 1.6 multiply_reduce_fusion.2
  18.6 2.0 copy.48
  20.6 1.6 multiply_reduce_fusion.1
  22.2 0.0 copy-start.2
  22.2 1.0 fusion.14
  23.2 0.6 copy-done.2
  23.8 44.4 %collective-permute-done.3 = bf16[768,640]{1,0:T(8,128)(2,1)} collective-permute-done((bf16[768,640]{1,0:T(8,128)(2,1)}, bf16[768,640]{1,0:T(8,128)(2,1)}, u32[]{:S(2)}, u32[]{:S(2)}) %collective-permute-start.3) | collective-permute-done | bytes 983072 | tf_op jit(solution)/shard_map/ppermute | solution.py:12
  68.2 2.3 copy.53
  70.5 0.0 collective-permute-done.2
  70.5 2.2 bitcast_reduce_fusion
  72.6 0.0 copy-start.1
  72.7 2.5 copy-done.1
  75.1 1.0 fusion.8
  76.1 1.1 all-gather.3.cloned.1.call-done
  77.2 4.0 %copy.55 = bf16[1536,640]{0,1:T(8,128)(2,1)} copy(bf16[1536,640]{1,0:T(8,128)(2,1)} %all-gather.3.cloned.1.call-done) | data formatting | bytes 3932160 | tf_op jit(solution)/shard_map/all_gather | solution.py:60
  81.2 3.4 %multiply_reduce_fusion = (f32[5,384]{1,0:T(8,128)S(1)}, f32[5,384,1536]{2,1,0:T(8,128)S(1)}) fusion(bf16[384,5,128]{0,2,1:T(8,128)(2,1)S(1)} %bitcast.144, bf16[1536,5,128]{0,2,1:T(8,128)(2,1)} %bitcast.145), kind=kOutput, calls=%fused_computation.1 | convolution fusion | flops 760871040 | bytes 14261760 | tf_op jit(solution)/shard_map/thd,shd->hts/dot_general | solution.py:20
  84.6 0.0 slice-start
  84.6 0.0 copy-start.6
  84.6 0.0 slice-start.1
  84.6 2.3 fusion
  87.0 3.6 %copy-done = f32[5,384,1536]{2,1,0:T(8,128)} copy-done((f32[5,384,1536]{2,1,0:T(8,128)}, f32[5,384,1536]{2,1,0:T(8,128)S(1)}, u32[]{:S(2)}) %copy-start) | copy-done | bytes 11796504
  90.6 0.0 copy-done.6
  90.6 1.7 fusion.35
  92.3 0.0 slice-done
  92.3 0.0 slice-done.1
  92.3 0.0 copy-done.5
  92.3 1.1 fusion.62
  93.4 49.3 %all-gather.5.cloned.1.call-done = bf16[1536,640]{1,0:T(8,128)(2,1)} async-done(((bf16[48,640]{1,0:T(8,128)(2,1)}), bf16[1536,640]{1,0:T(8,128)(2,1)}) %all-gather.5.cloned.1.call-update) | async-done | bytes 1966096 | tf_op jit(solution)/shard_map/all_gather | solution.py:61
  142.7 4.2 %copy.58 = bf16[1536,640]{0,1:T(8,128)(2,1)} copy(bf16[1536,640]{1,0:T(8,128)(2,1)} %all-gather.5.cloned.1.call-done) | data formatting | bytes 3932160 | tf_op jit(solution)/shard_map/all_gather | solution.py:61
  146.9 7.2 %fusion.59 = f32[384,5,128]{0,2,1:T(8,128)S(1)} fusion(bf16[1536,5,128]{0,2,1:T(8,128)(2,1)} %bitcast.150, f32[5,384,1536]{2,1,0:T(8,128)} %copy-done, f32[5,384]{1,0:T(8,128)S(1)} %get-tuple-element.12, f32[384,5]{0,1:T(8,128)S(1)} %get-tuple-element.11), kind=kOutput, calls=%fused_computation.42 | convolution fusion | flops 764067840 | bytes 14760960 | tf_op jit(solution)/shard_map/hts,shd->htd/dot_general | solution.py:26
  154.2 0.0 copy-done.3
  154.2 0.0 copy-done.10
  154.2 0.0 copy-done.11
  154.2 0.9 fusion.68
  155.1 0.0 slice-done.2
  155.1 0.0 slice-done.3
  155.1 4.8 %fusion.2 = bf16[5120,384]{0,1:T(8,128)(2,1)} fusion(bf16[384,640]{0,1:T(8,128)(2,1)S(1)} %bitcast.153, bf16[640,5120]{1,0:T(8,128)(2,1)S(1)} %bitcast.147), kind=kOutput, calls=%fused_computation.5 | convolution fusion | flops 2518548480 | bytes 10977280 | tf_op jit(solution)/shard_map/dot_general | solution.py:67
  159.9 6.3 %copy.70 = bf16[5120,384]{1,0:T(8,128)(2,1)} copy(bf16[5120,384]{0,1:T(8,128)(2,1)} %fusion.2) | data formatting | bytes 7864320
  166.2 0.0 reduce-scatter.4.cloned.1.call-update
  166.2 88.7 %reduce-scatter.4.cloned.1.call-done = bf16[640,384]{1,0:T(8,128)(2,1)} async-done(((bf16[5120,384]{1,0:T(8,128)(2,1)}), bf16[640,384]{1,0:T(8,128)(2,1)}) %reduce-scatter.4.cloned.1.call-update) | async-done | bytes 491536
  254.9 2.0 copy.71
  (11 shorter events, 0.0 us)
Async XLA Ops:
  6.5 9.1 %copy-start.7 = (bf16[384,640]{1,0:T(8,128)(2,1)S(1)}, bf16[384,640]{1,0:T(8,128)(2,1)}, u32[]{:S(2)}) copy-start(bf16[384,640]{1,0:T(8,128)(2,1)} %param.8) | copy-start | bytes 1474564
  6.5 70.7 %all-gather.3.cloned.1.call-start = ((), (), s32[]{:S(2)}) async-start(), calls=%async_computation.1 | async-start | bytes 2027520 | tf_op jit(solution)/shard_map/all_gather | solution.py:60
  7.3 135.5 %all-gather.5.cloned.1.call-start = ((), (), s32[]{:S(2)}) async-start(), calls=%async_computation.2 | async-start | bytes 2027520 | tf_op jit(solution)/shard_map/all_gather | solution.py:61
  8.6 8.2 %copy-start.4 = (bf16[384,640]{0,1:T(8,128)(2,1)}, bf16[384,640]{0,1:T(8,128)(2,1)S(1)}, u32[]{:S(2)}) copy-start(bf16[384,640]{0,1:T(8,128)(2,1)S(1)} %copy.40) | copy-start | bytes 1474564
  8.6 4.0 %collective-permute-start = (bf16[384,640]{0,1:T(8,128)(2,1)S(1)}, bf16[384,640]{0,1:T(8,128)(2,1)S(1)}, u32[]{:S(2)}, u32[]{:S(2)}) collective-permute-start(bf16[384,640]{0,1:T(8,128)(2,1)S(1)} %copy.40), channel_id=1, source_target_pairs={{0,8},{8,0},{16,24},{24,16},{32,40},{40,32},{48,56},{56,48},{64,72... | collective-permute-start | bytes 1474568 | tf_op jit(solution)/shard_map/ppermute | solution.py:12
  8.7 7.0 %collective-permute-start.1 = (bf16[384,640]{1,0:T(8,128)(2,1)}, bf16[384,640]{1,0:T(8,128)(2,1)S(1)}, u32[]{:S(2)}, u32[]{:S(2)}) collective-permute-start(bf16[384,640]{1,0:T(8,128)(2,1)} %param.8), channel_id=1, source_target_pairs={{0,8},{8,0},{16,24},{24,16},{32,40},{40,32},{48,56},{56,48},{64,72... | collective-permute-start | bytes 1474568 | tf_op jit(solution)/shard_map/ppermute | solution.py:12
  9.2 245.7 %reduce-scatter.4.cloned.1.call-start = ((), (), s32[]{:S(2)}) async-start(), calls=%async_computation.3 | async-start | bytes 4423680
  12.6 4.3 %copy-start.8 = (bf16[384,640]{0,1:T(8,128)(2,1)}, bf16[384,640]{0,1:T(8,128)(2,1)S(1)}, u32[]{:S(2)}) copy-start(bf16[384,640]{0,1:T(8,128)(2,1)S(1)} %collective-permute-done) | copy-start | bytes 1474564
  13.7 56.7 %collective-permute-start.2 = (bf16[768,640]{0,1:T(8,128)(2,1)}, bf16[768,640]{0,1:T(8,128)(2,1)}, u32[]{:S(2)}, u32[]{:S(2)}) collective-permute-start(bf16[768,640]{0,1:T(8,128)(2,1)} %pad_maximum_fusion), channel_id=1, source_target_pairs={{0,16},{8,24},{16,0},{24,8},{32,48},{40,56},{48,32},{56,40},{64,80... | collective-permute-start | bytes 2949128 | tf_op jit(solution)/shard_map/ppermute | solution.py:12
  15.7 1.3 copy-start.9
  16.8 51.4 %collective-permute-start.3 = (bf16[768,640]{1,0:T(8,128)(2,1)}, bf16[768,640]{1,0:T(8,128)(2,1)}, u32[]{:S(2)}, u32[]{:S(2)}) collective-permute-start(bf16[768,640]{1,0:T(8,128)(2,1)} %pad_maximum_fusion.1), channel_id=1, source_target_pairs={{0,16},{8,24},{16,0},{24,8},{32,48},{40,56},{48,32},{56,40},{64,80... | collective-permute-start | bytes 2949128 | tf_op jit(solution)/shard_map/ppermute | solution.py:12
  22.2 1.6 copy-start.2
  72.6 2.5 copy-start.1
  84.6 6.0 %copy-start = (f32[5,384,1536]{2,1,0:T(8,128)}, f32[5,384,1536]{2,1,0:T(8,128)S(1)}, u32[]{:S(2)}) copy-start(f32[5,384,1536]{2,1,0:T(8,128)S(1)} %get-tuple-element.13) | copy-start | bytes 35389444
  84.6 7.7 %slice-start = ((s8[5898240]{0:T(1024)(128)(4,1)}), s8[4194304]{0:T(1024)(128)(4,1)S(1)}, s32[]{:S(2)}) async-start(s8[5898240]{0:T(1024)(128)(4,1)} %bitcast.139), calls=%async_computation.4 | async-start | bytes 8388608
  84.6 6.0 %copy-start.6 = (bf16[384,640]{0,1:T(8,128)(2,1)S(1)}, bf16[384,640]{0,1:T(8,128)(2,1)}, u32[]{:S(2)}) copy-start(bf16[384,640]{0,1:T(8,128)(2,1)} %copy.43) | copy-start | bytes 1474564
  84.6 7.7 %slice-start.1 = ((s8[5898240]{0:T(1024)(128)(4,1)}), s8[1703936]{0:T(1024)(128)(4,1)S(1)}, s32[]{:S(2)}) async-start(s8[5898240]{0:T(1024)(128)(4,1)} %bitcast.139), calls=%async_computation.5 | async-start | bytes 3407872
  90.6 1.7 copy-start.5
  142.7 12.4 %slice-start.2 = ((s8[6553600]{0:T(1024)(128)(4,1)}), s8[2359296]{0:T(1024)(128)(4,1)S(1)}, s32[]{:S(2)}) async-start(s8[6553600]{0:T(1024)(128)(4,1)} %bitcast.146), calls=%async_computation.6 | async-start | bytes 4718592
  146.9 7.3 %copy-start.3 = (f32[5,384,384]{1,2,0:T(8,128)S(1)}, f32[5,384,384]{1,2,0:T(8,128)}, u32[]{:S(2)}) copy-start(f32[5,384,384]{1,2,0:T(8,128)} %copy-done.2) | copy-start | bytes 8847364
  146.9 7.3 %copy-start.10 = (f32[384,5,128]{0,2,1:T(8,128)S(1)}, f32[384,5,128]{0,2,1:T(8,128)}, u32[]{:S(2)}) copy-start(f32[384,5,128]{0,2,1:T(8,128)} %fusion.35) | copy-start | bytes 2949124
  146.9 7.3 %copy-start.11 = (bf16[384,640]{0,1:T(8,128)(2,1)S(1)}, bf16[384,640]{0,1:T(8,128)(2,1)}, u32[]{:S(2)}) copy-start(bf16[384,640]{0,1:T(8,128)(2,1)} %copy.48) | copy-start | bytes 1474564
  146.9 8.2 %slice-start.3 = ((s8[6553600]{0:T(1024)(128)(4,1)}), s8[4194304]{0:T(1024)(128)(4,1)S(1)}, s32[]{:S(2)}) async-start(s8[6553600]{0:T(1024)(128)(4,1)} %bitcast.146), calls=%async_computation.7 | async-start | bytes 8388608
Sparse Core Ops, SparseCore 0:
  9.2 67.9 all-gather.2
  79.0 63.6 all-gather.4
  166.4 88.5 reduce-scatter.3
where the time goes:
time: 265 us; the launch traced here: 263 us
  waiting for transfers between devices  184 us (69%)
  local copies, waits for them, and re-layouts  32.1 us (12%)
  matrix products  24.6 us (9%)
  between operations  13.3 us (5%)
  other arithmetic  6.6 us (2%)
  starting transfers between devices  2.7 us (1%)
    unnamed x4, waiting for transfers between devices  89.4 us
    all_gather x1, waiting for transfers between devices, body(): lax.all_gather(ref_values, 'seq', axis=0, tiled=True)  49.3 us
    ppermute x4, waiting for transfers between devices, partner(): lax.ppermute(value, axis, [(i, i ^ 1 << apart) for i in range(lax.axis_si...  44.4 us
    unnamed x37, local copies, waits for them, and re-layouts  19.6 us
    dot_general x4, matrix products, attend(): jnp.einsum('hts,shd->htd', weights.astype(jnp.bfloat16), value_heads, pre...  10.9 us
    dot_general x4, matrix products, attend(): jnp.einsum('thd,shd->hts', query_heads, key_heads, preferred_element_type...  8.84 us
  transfers between devices with their start and end apart: 7, of which 4 were waited for; matrix products, arithmetic and copies ran while one was open for 12% of the time, Pallas kernels for 0%

commit v1 on v0

v1 whole, which is shorter than its diff:
```python
import functools
import math

import jax
import jax.numpy as jnp
from jax import lax
from jax.experimental import pallas as pl
from jax.experimental.pallas import tpu as pltpu
from jax.sharding import PartitionSpec as P

HD = 128
Z = 8
X = 4
BASE2 = math.log2(math.e) / math.sqrt(HD)
F32 = jnp.float32
BF16 = jnp.bfloat16
VMEM_LIMIT = 48 << 20


def seq_place(i):
    return i // (2 * Z), (i // 2) % Z, i % 2


def along_z(step):
    pairs = []
    for i in range(4 * Z):
        y, z, core = seq_place(i)
        pairs.append((i, (y * Z + (z + step) % Z) * 2 + core))
    return pairs


def between_frames():
    pairs = []
    for i in range(4 * Z):
        y, z, core = seq_place(i)
        other = (z + 1) % Z if z % 2 else (z - 1) % Z
        pairs.append((i, (y * Z + other) * 2 + core))
    return pairs


def along_x(step):
    return [(i, (i // 2 + step) % X * 2 + i % 2) for i in range(2 * X)]


def swap(value, axis, bit):
    return lax.ppermute(value, axis, [(i, i ^ bit) for i in range(lax.axis_size(axis))])


def scores_of(rows, keys):
    return lax.dot_general(rows, keys, (((1,), (1,)), ((), ())), preferred_element_type=F32)


def softmax_part(rows, keys, values_and_ones):
    scores = scores_of(rows, keys)
    peak = jnp.max(scores, axis=1, keepdims=True)
    weights = jnp.exp2((scores - peak) * BASE2).astype(BF16)
    both = jnp.dot(weights, values_and_ones, preferred_element_type=F32)
    return both[:, :HD], both[:, HD:], peak * BASE2


def fill_keys(key_ref, value_ref, layout, pieces):
    at = 0
    for piece, kind in zip(pieces, layout):
        if kind[0] == "key":
            key_ref[at : at + kind[1], :] = piece[...]
        elif kind[0] == "value":
            value_ref[at : at + kind[1], :HD] = piece[...]
            at += kind[1]
        else:
            half = kind[1]
            for group in range(kind[2]):
                low = group * 2 * half
                key_ref[at : at + half, :] = piece[low : low + half, :]
                value_ref[at : at + half, :HD] = piece[low + half : low + 2 * half, :]
                at += half
    value_ref[:, HD:] = jnp.ones((at, HD), BF16)


def first_kernel(layout, *refs):
    queries = refs[:2]
    pieces = refs[2 : 2 + len(layout)]
    part_ref, log_ref, key_ref, value_ref = refs[2 + len(layout) :]
    fill_keys(key_ref, value_ref, layout, pieces)
    rows = queries[0].shape[0]
    for place, query in enumerate(queries):
        summed, total, peak = softmax_part(query[...], key_ref[...], value_ref[...])
        part_ref[place * rows : (place + 1) * rows, :] = summed / total
        log_ref[place * rows : (place + 1) * rows, :] = peak + jnp.log2(total)


def last_kernel(layout, low, high, *refs):
    queries = refs[:2]
    states = refs[2:6]
    pieces = refs[6 : 6 + len(layout)]
    own_ref, own_log, other_ref, other_log, key_ref, value_ref, query_ref = refs[6 + len(layout) :]
    rows = high - low
    head = pl.program_id(0)
    fill_keys(key_ref, value_ref, layout, pieces)
    query_ref[:rows, :] = queries[0][low:high, :]
    query_ref[rows:, :] = queries[1][low:high, :]
    summed, total, peak = softmax_part(query_ref[...], key_ref[...], value_ref[...])
    lane = lax.broadcasted_iota(jnp.int32, (rows, HD), 1)
    for place, (out_ref, log_ref) in enumerate(((own_ref, own_log), (other_ref, other_log))):
        part = slice(place * rows, (place + 1) * rows)
        before = states[2 * place][low:high, :]
        before_log = states[2 * place + 1][low:high, :]
        top = jnp.maximum(before_log, peak[part])
        before_factor = jnp.exp2(before_log - top)
        factor = jnp.exp2(peak[part] - top)
        whole = before_factor + total[part] * factor
        out_ref[...] = ((before * before_factor + summed[part] * factor) / whole).astype(BF16)
        logs = top + jnp.log2(whole)
        log_ref[...] = jnp.where(lane == head, logs, jnp.where(head == 0, 0.0, log_ref[...]))


def piece_keys(layout):
    return sum(
        kind[1] if kind[0] == "value" else kind[1] * kind[2] if kind[0] == "both" else 0
        for kind in layout
    )


def by_head(array, place=0, rows=None):
    return pl.BlockSpec((rows or array.shape[0], HD), lambda head: (place, head))


def estimate(rows, keys, heads):
    return pl.CostEstimate(
        flops=4 * rows * keys * heads * HD,
        bytes_accessed=4 * (rows + keys) * heads * HD,
        transcendentals=rows * keys * heads,
    )


def attend_first(queries, other_queries, layout, pieces):
    rows, width = queries.shape
    heads = width // HD
    keys = piece_keys(layout)
    shape = jax.ShapeDtypeStruct((2 * rows, width), F32)
    return pl.pallas_call(
        functools.partial(first_kernel, layout),
        grid=(heads,),
        in_specs=[by_head(a) for a in (queries, other_queries, *pieces)],
        out_specs=[by_head(shape)] * 2,
        out_shape=[shape] * 2,
        scratch_shapes=[pltpu.VMEM((keys, HD), BF16), pltpu.VMEM((keys, 2 * HD), BF16)],
        compiler_params=pltpu.CompilerParams(vmem_limit_bytes=VMEM_LIMIT),
        cost_estimate=estimate(2 * rows, keys, heads),
        name="attend_first",
    )(queries, other_queries, *pieces)


def attend_last(queries, other_queries, state, low, high, layout, pieces):
    width = queries.shape[1]
    heads = width // HD
    keys = piece_keys(layout)
    rows = high - low
    whole = queries.shape[0]
    part = jax.ShapeDtypeStruct((rows, width), BF16)
    logs = jax.ShapeDtypeStruct((rows, HD), F32)
    one = pl.BlockSpec((rows, HD), lambda head: (0, 0))
    return pl.pallas_call(
        functools.partial(last_kernel, layout, low, high),
        grid=(heads,),
        in_specs=[by_head(queries), by_head(other_queries)]
        + [by_head(a, place, whole) for place in range(2) for a in state]
        + [by_head(a) for a in pieces],
        out_specs=[by_head(part), one, by_head(part), one],
        out_shape=[part, logs, part, logs],
        scratch_shapes=[
            pltpu.VMEM((keys, HD), BF16),
            pltpu.VMEM((keys, 2 * HD), BF16),
            pltpu.VMEM((2 * rows, HD), BF16),
        ],
        compiler_params=pltpu.CompilerParams(vmem_limit_bytes=VMEM_LIMIT),
        cost_estimate=estimate(2 * rows, keys, heads),
        name="attend_last",
    )(queries, other_queries, *state, *state, *pieces)


def merge_heads(parts, logs, out_ref):
    for head in range(out_ref.shape[1] // HD):
        columns = slice(head * HD, (head + 1) * HD)
        first, second = (log[:, head : head + 1] for log in logs)
        top = jnp.maximum(first, second)
        first_factor = jnp.exp2(first - top)
        second_factor = jnp.exp2(second - top)
        scale = 1.0 / (first_factor + second_factor)
        out_ref[:, columns] = (
            parts[0][:, columns].astype(F32) * (first_factor * scale)
            + parts[1][:, columns].astype(F32) * (second_factor * scale)
        ).astype(BF16)


def send_kernel(steps, blocks_of, cols, own, own_log, got, got_log, weight, *out):
    outs, att = out[:-1], out[-1]
    step = pl.program_id(0)

    @pl.when(step == 0)
    def _():
        merge_heads((own, got), (own_log, got_log), att)

    result = jnp.dot(att[...], weight[...], preferred_element_type=F32).astype(BF16)
    for number, out_ref in enumerate(outs):

        @pl.when(step // blocks_of == number)
        def _():
            out_ref[...] = result


def project_send(cols, own, own_log, got, got_log, out_weight, n_outs):
    rows, width = own.shape
    blocks = cols.shape[0]
    blocks_of = blocks // n_outs

    def place(number):
        def index(step, cols):
            return (jnp.clip(step - number * blocks_of, 0, blocks_of - 1), 0)

        return index

    def whole(a):
        return pl.BlockSpec(a.shape, lambda step, cols: (0, 0))

    return pl.pallas_call(
        functools.partial(send_kernel, blocks, blocks_of),
        grid_spec=pltpu.PrefetchScalarGridSpec(
            num_scalar_prefetch=1,
            grid=(blocks,),
            in_specs=[whole(a) for a in (own, own_log, got, got_log)]
            + [pl.BlockSpec((width, width), lambda step, cols: (0, cols[step]))],
            out_specs=[pl.BlockSpec((rows, width), place(n)) for n in range(n_outs)]
            + [pl.BlockSpec((rows, width), lambda step, cols: (0, 0))],
        ),
        out_shape=[jax.ShapeDtypeStruct((blocks_of * rows, width), BF16)] * n_outs
        + [jax.ShapeDtypeStruct((rows, width), BF16)],
        compiler_params=pltpu.CompilerParams(vmem_limit_bytes=VMEM_LIMIT),
        cost_estimate=pl.CostEstimate(
            flops=2 * rows * width * width * blocks,
            bytes_accessed=2 * width * width * blocks,
            transcendentals=0,
        ),
        name="project_send",
    )(cols, own, own_log, got, got_log, out_weight)


def keep_kernel(cols, att, weight, out):
    out[...] = jnp.dot(att[...], weight[...], preferred_element_type=F32)


def project_keep(cols, att, out_weight):
    rows, width = att.shape
    blocks = cols.shape[0]
    return pl.pallas_call(
        keep_kernel,
        grid_spec=pltpu.PrefetchScalarGridSpec(
            num_scalar_prefetch=1,
            grid=(blocks,),
            in_specs=[
                pl.BlockSpec((rows, width), lambda step, cols: (0, 0)),
                pl.BlockSpec((width, width), lambda step, cols: (0, cols[step])),
            ],
            out_specs=pl.BlockSpec((rows, width), lambda step, cols: (step, 0)),
        ),
        out_shape=jax.ShapeDtypeStruct((blocks * rows, width), F32),
        compiler_params=pltpu.CompilerParams(vmem_limit_bytes=VMEM_LIMIT),
        cost_estimate=pl.CostEstimate(
            flops=2 * rows * width * width * blocks,
            bytes_accessed=2 * width * width * blocks,
            transcendentals=0,
        ),
        name="project_keep",
    )(cols, att, out_weight)


def added(kept, *got):
    total = kept
    for part in got:
        total = total + part.astype(F32)
    return total


def body(queries, keys, values, ref_keys, ref_values, out_weight):
    rows = queries.shape[0]
    half = ref_keys.shape[0]
    right_z, left_z, between = along_z(1), along_z(-1), between_frames()
    right_x, left_x = along_x(1), along_x(-1)
    odd = (lax.axis_index("seq") // 2) % 2 == 1

    own = jnp.concatenate([ref_keys, ref_values], axis=0)
    from_left = [lax.ppermute(own, "seq", right_z)]
    from_right = [lax.ppermute(own, "seq", left_z)]
    other_queries = swap(queries, "seq", 1)
    frame_keys = swap(keys, "seq", 2)
    frame_values = swap(values, "seq", 2)
    across = []
    for step in range(2):
        packed = [from_left[-1], from_right[-1]]
        if step == 0:
            packed = [own, *packed]
        from_left.append(lax.ppermute(from_left[-1], "seq", right_z))
        from_right.append(lax.ppermute(from_right[-1], "seq", left_z))
        across.append(swap(jnp.concatenate(packed, axis=0), "seq", 2 * Z))
    far = lax.ppermute(jnp.where(odd, from_left[-1], from_right[-1]), "seq", between)
    across.append(swap(jnp.concatenate([from_left[-1], from_right[-1]], axis=0), "seq", 2 * Z))
    across.append(swap(far, "seq", 2 * Z))

    first_layout = (("key", rows), ("value", rows))
    state = attend_first(queries, other_queries, first_layout, (keys, values))
    pieces = [frame_keys, frame_values]
    layout = [("key", rows), ("value", rows)]
    for piece in (own, *from_left, *from_right, far, *across):
        pieces.append(piece)
        layout.append(("both", half, piece.shape[0] // (2 * half)))
    layout = tuple(layout)

    cut = rows // 2
    place = lax.axis_index("head")
    mine, theirs = place % 2, 1 - place % 2
    ahead = [(place // 2 + step) % X * 2 for step in (2, 1, X - 1, 0)]

    def columns(*which):
        return jnp.stack([ahead[n] + side for n, side in which]).astype(jnp.int32)

    def finish(low, high):
        own_part, own_log, other_part, other_log = attend_last(
            queries, other_queries, state, low, high, layout, pieces
        )
        return own_part, own_log, swap(other_part, "seq", 1), swap(other_log, "seq", 1)

    n = cut
    done = finish(0, cut)
    go_right, go_left, att = project_send(
        columns((0, mine), (1, theirs), (0, theirs), (2, mine)), *done, out_weight, 2
    )
    got_left = lax.ppermute(go_right, "head", right_x)
    got_right = lax.ppermute(go_left, "head", left_x)

    m = rows - cut
    last_done = finish(cut, rows)
    go_across, last_att = project_send(
        columns(*((n, theirs) for n in range(4))), *last_done, out_weight, 1
    )
    got_across = swap(go_across, "head", 1)

    kept = project_keep(columns((1, mine), (2, theirs), (0 + 3, mine), (3, theirs)), att, out_weight)
    last_kept = project_keep(columns(*((n, mine) for n in range(4))), last_att, out_weight)

    on_right = lax.ppermute(added(kept[:n], got_left[:n]).astype(BF16), "head", right_x)
    on_left = lax.ppermute(added(kept[n : 2 * n], got_right[:n]).astype(BF16), "head", left_x)

    quarter = m // 2
    summed = [added(last_kept[k * m : (k + 1) * m], got_across[k * m : (k + 1) * m]) for k in range(4)]
    last_right = jnp.concatenate([summed[0][:quarter], summed[1][quarter:]], axis=0).astype(BF16)
    last_left = jnp.concatenate([summed[0][quarter:], summed[2][:quarter]], axis=0).astype(BF16)
    last_got_left = lax.ppermute(last_right, "head", right_x)
    last_got_right = lax.ppermute(last_left, "head", left_x)

    theirs_sum = added(kept[3 * n :], on_left, got_left[n:]).astype(BF16)
    mine_got = swap(theirs_sum, "head", 1)
    mine_sum = added(kept[2 * n : 3 * n], on_right, got_right[n:])

    last_on_right = lax.ppermute(
        added(summed[1][:quarter], last_got_left[:quarter]).astype(BF16), "head", right_x
    )
    last_on_left = lax.ppermute(
        added(summed[2][quarter:], last_got_right[:quarter]).astype(BF16), "head", left_x
    )
    return jnp.concatenate(
        [
            added(mine_sum, mine_got),
            added(summed[3][:quarter], last_on_right, last_got_right[quarter:]),
            added(summed[3][quarter:], last_on_left, last_got_left[quarter:]),
        ],
        axis=0,
    ).astype(BF16)


def solution(mesh):
    placed = (
        P("seq", "head"),
        P("seq", "head"),
        P("seq", "head"),
        P("seq", "head"),
        P("seq", "head"),
        P("head", None),
    )
    return jax.shard_map(
        body, mesh=mesh, in_specs=placed, out_specs=P("seq", "head"), check_vma=False
    )
```

time: 265 us -> 127 us (0.48)
  waiting for transfers between devices: 184 us -> 35.4 us
  Pallas kernels: 0 us -> 40.9 us
  starting transfers between devices: 2.7 us -> 35.6 us
  matrix products: 24.6 us -> 0 us
  local copies, waits for them, and re-layouts: 32.1 us -> 10.4 us
  between operations: 13.3 us -> 0.26 us
    unnamed x4 -> x0, waiting for transfers between devices: 89.4 us -> none
    all_gather x2 -> x0, waiting for transfers between devices: 50.4 us -> none  [the longest x1 49.3 us: body(): lax.all_gather(ref_values, 'seq', axis=0, tiled=True)]
    pallas_call x0 -> x7, Pallas kernels: none -> 40.9 us  [the longest x2 19 us: attend_last(): pl.pallas_call(functools.partial(last_kernel, layout, low, high), grid=(h...]
    ppermute x4 -> x28, starting transfers between devices: 2.62 us -> 35.6 us  [the longest x13 9.41 us: swap(): lax.ppermute(value, axis, [(i, i ^ bit) for i in range(lax.axis_size(axis...]
    dot_general x9 -> x0, matrix products: 24.6 us -> none  [the longest x4 10.9 us: attend(): jnp.einsum('hts,shd->htd', weights.astype(jnp.bfloat16), value_heads, pre...]
    unnamed x37 -> x39, local copies, waits for them, and re-layouts: 19.6 us -> 9.46 us
    ppermute x4 -> x28, waiting for transfers between devices: 44.4 us -> 35.4 us  [the longest x13 8.68 us: swap(): lax.ppermute(value, axis, [(i, i ^ bit) for i in range(lax.axis_size(axis...]
    all_gather x2 -> x0, local copies, waits for them, and re-layouts: 8.17 us -> none  [the longest x1 4.16 us: body(): lax.all_gather(ref_values, 'seq', axis=0, tiled=True)]
  transfers between devices with their start and end apart: 7 -> 28, of which waited for: 4 -> 13; matrix products, arithmetic and copies ran while one was open for 12% -> 3% of each run, Pallas kernels for 0% -> 25%
where the time goes in v1:
time: 127 us
  Pallas kernels  40.9 us (32%)
  starting transfers between devices  35.6 us (28%)
  waiting for transfers between devices  35.4 us (28%)
  local copies, waits for them, and re-layouts  10.4 us (8%)
  other arithmetic  4.15 us (3%)
    pallas_call x2, Pallas kernels, attend_last(): pl.pallas_call(functools.partial(last_kernel, layout, low, high), grid=(h...  19 us
    unnamed x39, local copies, waits for them, and re-layouts  9.46 us
    ppermute x13, starting transfers between devices, swap(): lax.ppermute(value, axis, [(i, i ^ bit) for i in range(lax.axis_size(axis...  9.41 us
    pallas_call x2, Pallas kernels, project_send(): pl.pallas_call(functools.partial(send_kernel, blocks, blocks_of), grid_sp...  9.16 us
    ppermute x13, waiting for transfers between devices, swap(): lax.ppermute(value, axis, [(i, i ^ bit) for i in range(lax.axis_size(axis...  8.68 us
    pallas_call x2, Pallas kernels, project_keep(): pl.pallas_call(keep_kernel, grid_spec=pltpu.PrefetchScalarGridSpec(num_sc...  8.23 us
    ppermute x2, starting transfers between devices, body(): from_right.append(lax.ppermute(from_right[-1], 'seq', left_z))  7.34 us
    ppermute x1, starting transfers between devices, body(): from_right = [lax.ppermute(own, 'seq', left_z)]  5.92 us
  transfers between devices with their start and end apart: 28, of which 13 were waited for; matrix products, arithmetic and copies ran while one was open for 3% of the time, Pallas kernels for 25%

profile of v1, /device:TPU:8, one launch (start us, length us, event | category | flops | bytes accessed | tf_op | source)
XLA Modules:
  0.0 126.7 jit_solution(13881043593077645801)
XLA Ops:
  0.0 0.9 constant_dynamic-update-slice_fusion.1
  0.9 0.8 constant_dynamic-update-slice_fusion.refs_8_
  1.7 5.9 %collective-permute-start.6 = (bf16[96,640]{1,0:T(8,128)(2,1)S(1)}, bf16[96,640]{1,0:T(8,128)(2,1)S(1)}, u32[]{:S(2)}, u32[]{:S(2)}) collective-permute-start(bf16[96,640]{1,0:T(8,128)(2,1)S(1)} %constant_dynamic-update-slice_fusion.refs_8_), channel_id=1, source_target_pairs={{0,112},{8,120},{16,0},{24,8},{32,16},{40,24},{48,32},{56,40},{64,... | collective-permute-start | bytes 368648 | tf_op jit(solution)/shard_map/ppermute | solution.py:292
  7.7 2.6 %collective-permute-done.6.refs_12_ = bf16[96,640]{1,0:T(8,128)(2,1)S(1)} collective-permute-done((bf16[96,640]{1,0:T(8,128)(2,1)S(1)}, bf16[96,640]{1,0:T(8,128)(2,1)S(1)}, u32[]{:S(2)}, u32[]{:S(2)}) %collective-permute-start.6) | collective-permute-done | bytes 122912 | tf_op jit(solution)/shard_map/ppermute | solution.py:292
  10.2 3.7 %collective-permute-start.7 = (bf16[96,640]{1,0:T(8,128)(2,1)S(1)}, bf16[96,640]{1,0:T(8,128)(2,1)S(1)}, u32[]{:S(2)}, u32[]{:S(2)}) collective-permute-start(bf16[96,640]{1,0:T(8,128)(2,1)S(1)} %collective-permute-done.6.refs_12_), channel_id=1, source_target_pairs={{0,112},{8,120},{16,0},{24,8},{32,16},{40,24},{48,32},{56,40},{64,... | collective-permute-start | bytes 368648 | tf_op jit(solution)/shard_map/ppermute | solution.py:302
  13.9 2.4 %collective-permute-done.7.refs_13_ = bf16[96,640]{1,0:T(8,128)(2,1)S(1)} collective-permute-done((bf16[96,640]{1,0:T(8,128)(2,1)S(1)}, bf16[96,640]{1,0:T(8,128)(2,1)S(1)}, u32[]{:S(2)}, u32[]{:S(2)}) %collective-permute-start.7) | collective-permute-done | bytes 122912 | tf_op jit(solution)/shard_map/ppermute | solution.py:302
  16.4 3.6 %collective-permute-start.8 = (bf16[96,640]{1,0:T(8,128)(2,1)S(1)}, bf16[96,640]{1,0:T(8,128)(2,1)S(1)}, u32[]{:S(2)}, u32[]{:S(2)}) collective-permute-start(bf16[96,640]{1,0:T(8,128)(2,1)S(1)} %collective-permute-done.7.refs_13_), channel_id=1, source_target_pairs={{0,112},{8,120},{16,0},{24,8},{32,16},{40,24},{48,32},{56,40},{64,... | collective-permute-start | bytes 368648 | tf_op jit(solution)/shard_map/ppermute | solution.py:302
  20.0 2.0 %collective-permute-start.2 = (bf16[384,640]{1,0:T(8,128)(2,1)}, bf16[384,640]{1,0:T(8,128)(2,1)S(1)}, u32[]{:S(2)}, u32[]{:S(2)}) collective-permute-start(bf16[384,640]{1,0:T(8,128)(2,1)} %refs_3_.1), channel_id=1, source_target_pairs={{0,16},{8,24},{16,0},{24,8},{32,48},{40,56},{48,32},{56,40},{64,80... | collective-permute-start | bytes 1474568 | tf_op jit(solution)/shard_map/ppermute | solution.py:46
  22.1 0.4 collective-permute-done.8.refs_14_
  22.5 3.6 %collective-permute-done.5.refs_11_ = bf16[96,640]{1,0:T(8,128)(2,1)S(1)} collective-permute-done((bf16[96,640]{1,0:T(8,128)(2,1)S(1)}, bf16[96,640]{1,0:T(8,128)(2,1)S(1)}, u32[]{:S(2)}, u32[]{:S(2)}) %collective-permute-start.5) | collective-permute-done | bytes 122912 | tf_op jit(solution)/shard_map/ppermute | solution.py:301
  26.1 0.2 collective-permute-start.9
  26.4 0.5 collective-permute-start.11
  26.9 0.9 pad_maximum_fusion.1
  27.8 4.5 %collective-permute-done.9.refs_15_ = bf16[96,640]{1,0:T(8,128)(2,1)S(1)} collective-permute-done((bf16[96,640]{1,0:T(8,128)(2,1)S(1)}, bf16[96,640]{1,0:T(8,128)(2,1)S(1)}, u32[]{:S(2)}, u32[]{:S(2)}) %collective-permute-start.9) | collective-permute-done | bytes 122912 | tf_op jit(solution)/shard_map/ppermute | solution.py:304
  32.3 0.4 collective-permute-start.10
  32.8 2.5 %collective-permute-done.11.refs_17_ = bf16[192,640]{1,0:T(8,128)(2,1)S(1)} collective-permute-done((bf16[192,640]{1,0:T(8,128)(2,1)S(1)}, bf16[192,640]{1,0:T(8,128)(2,1)S(1)}, u32[]{:S(2)}, u32[]{:S(2)}) %collective-permute-start.11) | collective-permute-done | bytes 245792 | tf_op jit(solution)/shard_map/ppermute | solution.py:46
  35.3 0.4 collective-permute-start.12
  35.8 1.6 %collective-permute-start.13 = (bf16[96,640]{1,0:T(8,128)(2,1)S(1)}, bf16[96,640]{1,0:T(8,128)(2,1)S(1)}, u32[]{:S(2)}, u32[]{:S(2)}) collective-permute-start(bf16[96,640]{1,0:T(8,128)(2,1)S(1)} %collective-permute-done.9.refs_15_), channel_id=1, source_target_pairs={{0,128},{8,136},{16,144},{24,152},{32,160},{40,168},{48,176},{56,1... | collective-permute-start | bytes 368648 | tf_op jit(solution)/shard_map/ppermute | solution.py:46
  37.4 4.5 %attend_first.1 = (f32[768,640]{1,0:T(8,128)S(1)}, f32[768,640]{1,0:T(8,128)S(1)}) custom-call(bf16[384,640]{1,0:T(8,128)(2,1)S(1)} %copy-done.2, bf16[384,640]{1,0:T(8,128)(2,1)S(1)} %collective-permute-done.refs_1_, bf16[384,640]{1,0:T(8,128)(2,1)S(1)} %copy-done.15, bf16[384,640]{1,0:T(8,128)(2,1)S(1)} %copy-done.16), custom_call_target="tpu_custom_call" | custom-call | flops 754974720 | bytes 2949120 | tf_op jit(solution)/shard_map/attend_first/pallas_call | solution.py:140
  41.9 1.3 %copy-done = f32[768,640]{1,0:T(8,128)} copy-done((f32[768,640]{1,0:T(8,128)}, f32[768,640]{1,0:T(8,128)S(1)}, u32[]{:S(2)}) %copy-start) | copy-done | bytes 1966104
  43.2 1.3 %copy-done.1 = f32[768,640]{1,0:T(8,128)} copy-done((f32[768,640]{1,0:T(8,128)}, f32[768,640]{1,0:T(8,128)S(1)}, u32[]{:S(2)}) %copy-start.1) | copy-done | bytes 1966104
  44.5 4.9 %collective-permute-done.13.refs_19_ = bf16[96,640]{1,0:T(8,128)(2,1)S(1)} collective-permute-done((bf16[96,640]{1,0:T(8,128)(2,1)S(1)}, bf16[96,640]{1,0:T(8,128)(2,1)S(1)}, u32[]{:S(2)}, u32[]{:S(2)}) %collective-permute-start.13) | collective-permute-done | bytes 122912 | tf_op jit(solution)/shard_map/ppermute | solution.py:46
  49.4 9.5 %attend_last.3 = (bf16[192,640]{1,0:T(8,128)(2,1)S(1)}, f32[192,128]{1,0:T(8,128)S(1)}, bf16[192,640]{1,0:T(8,128)(2,1)}, f32[192,128]{1,0:T(8,128)S(1)}) custom-call(bf16[384,640]{1,0:T(8,128)(2,1)S(1)} %copy-done.2, bf16[384,640]{1,0:T(8,128)(2,1)S(1)} %collective-permute-done.refs_1_, f32[768,640]{1,0:T(8,128)} %copy-done, f32[768,640]{1,0:T(8,128)} %copy-done.1, ...), custom_call_target="tpu_custom_call" | custom-call | flops 1132462080 | bytes 3932160 | tf_op jit(solution)/shard_map/attend_last/pallas_call | solution.py:162
  58.9 0.7 copy-done.9
  59.7 0.6 copy-done.17
  60.3 0.5 collective-permute-start.22
  60.8 0.9 copy-done.4
  61.8 0.9 copy-done.6
  62.7 0.9 copy-done.8
  63.6 9.5 %attend_last.2 = (bf16[192,640]{1,0:T(8,128)(2,1)S(1)}, f32[192,128]{1,0:T(8,128)S(1)}, bf16[192,640]{1,0:T(8,128)(2,1)}, f32[192,128]{1,0:T(8,128)S(1)}) custom-call(bf16[384,640]{1,0:T(8,128)(2,1)S(1)} %copy-done.2, bf16[384,640]{1,0:T(8,128)(2,1)S(1)} %collective-permute-done.refs_1_, f32[768,640]{1,0:T(8,128)} %copy-done, f32[768,640]{1,0:T(8,128)} %copy-done.1, ...), custom_call_target="tpu_custom_call" | custom-call | flops 1132462080 | bytes 3932160 | tf_op jit(solution)/shard_map/attend_last/pallas_call | solution.py:162
  73.1 0.1 collective-permute-start.14
  73.2 0.1 add_add_fusion.1.cols
  73.3 4.6 %project_send.3 = (bf16[768,640]{1,0:T(8,128)(2,1)S(1)}, bf16[192,640]{1,0:T(8,128)(2,1)S(1)}) custom-call(s32[4]{0:T(128)S(1)} %add_add_fusion.1.cols, bf16[192,640]{1,0:T(8,128)(2,1)S(1)} %copy-done.10, f32[192,128]{1,0:T(8,128)S(1)} %get-tuple-element.30.own_log, bf16[192,640]{1,0:T(8,128)(2,1)} %collective-permute-done.21.got, ...), custom_call_target="tpu_custom_call" | custom-call | flops 629145600 | bytes 3276800 | tf_op jit(solution)/shard_map/project_send/pallas_call | solution.py:225
  77.9 2.4 %collective-permute-start.23 = (bf16[768,640]{1,0:T(8,128)(2,1)S(1)}, bf16[768,640]{1,0:T(8,128)(2,1)}, u32[]{:S(2)}, u32[]{:S(2)}) collective-permute-start(bf16[768,640]{1,0:T(8,128)(2,1)S(1)} %get-tuple-element.34), channel_id=1, source_target_pairs={{0,1},{1,0},{2,3},{3,2},{4,5},{5,4},{6,7},{7,6},{8,9},{9,8},{10,11... | collective-permute-start | bytes 2949128 | tf_op jit(solution)/shard_map/ppermute | solution.py:46
  80.3 0.2 collective-permute-start.15
  80.5 0.1 pad_add_fusion.cols
  80.6 1.2 collective-permute-done.15.got_log
  81.8 0.9 copy-done.12
  82.7 0.9 copy-done.14
  83.6 4.6 %project_send.2 = (bf16[384,640]{1,0:T(8,128)(2,1)S(1)}, bf16[384,640]{1,0:T(8,128)(2,1)S(1)}, bf16[192,640]{1,0:T(8,128)(2,1)S(1)}) custom-call(s32[4]{0:T(128)S(1)} %pad_add_fusion.cols, bf16[192,640]{1,0:T(8,128)(2,1)S(1)} %copy-done.12, f32[192,128]{1,0:T(8,128)S(1)} %copy-done.14, bf16[192,640]{1,0:T(8,128)(2,1)S(1)} %collective-permute-done.14.got, ...), custom_call_target="tpu_custom_call" | custom-call | flops 629145600 | bytes 3276800 | tf_op jit(solution)/shard_map/project_send/pallas_call | solution.py:225
  88.2 2.8 %collective-permute-start.18 = (bf16[384,640]{1,0:T(8,128)(2,1)S(1)}, bf16[384,640]{1,0:T(8,128)(2,1)S(1)}, u32[]{:S(2)}, u32[]{:S(2)}) collective-permute-start(bf16[384,640]{1,0:T(8,128)(2,1)S(1)} %get-tuple-element.28), channel_id=1, source_target_pairs={{0,6},{1,7},{2,0},{3,1},{4,2},{5,3},{6,4},{7,5},{8,14},{9,15},{10,... | collective-permute-start | bytes 1474568 | tf_op jit(solution)/shard_map/ppermute | solution.py:337
  91.0 0.1 pad_add_fusion.1.cols
  91.1 0.1 add_add_fusion.cols
  91.2 0.0 collective-permute-start.16
  91.2 4.1 %project_keep.2 = f32[768,640]{1,0:T(8,128)S(1)} custom-call(s32[4]{0:T(128)S(1)} %add_add_fusion.cols, bf16[192,640]{1,0:T(8,128)(2,1)S(1)} %get-tuple-element.26.att, bf16[640,5120]{1,0:T(8,128)(2,1)} %weight.7), custom_call_target="tpu_custom_call" | custom-call | flops 629145600 | bytes 3276800 | tf_op jit(solution)/shard_map/project_keep/pallas_call | solution.py:254
  95.3 4.1 %project_keep.3 = f32[768,640]{1,0:T(8,128)S(1)} custom-call(s32[4]{0:T(128)S(1)} %pad_add_fusion.1.cols, bf16[192,640]{1,0:T(8,128)(2,1)S(1)} %get-tuple-element.33.att, bf16[640,5120]{1,0:T(8,128)(2,1)} %weight.7), custom_call_target="tpu_custom_call" | custom-call | flops 629145600 | bytes 3276800 | tf_op jit(solution)/shard_map/project_keep/pallas_call | solution.py:254
  99.5 2.4 %collective-permute-done.18 = bf16[384,640]{1,0:T(8,128)(2,1)S(1)} collective-permute-done((bf16[384,640]{1,0:T(8,128)(2,1)S(1)}, bf16[384,640]{1,0:T(8,128)(2,1)S(1)}, u32[]{:S(2)}, u32[]{:S(2)}) %collective-permute-start.18) | collective-permute-done | bytes 491552 | tf_op jit(solution)/shard_map/ppermute | solution.py:337
  101.9 0.1 fusion.1
  101.9 3.8 %collective-permute-start.19 = (bf16[192,640]{1,0:T(8,128)(2,1)S(1)}, bf16[192,640]{1,0:T(8,128)(2,1)S(1)}, u32[]{:S(2)}, u32[]{:S(2)}) collective-permute-start(bf16[192,640]{1,0:T(8,128)(2,1)S(1)} %fusion.1), channel_id=1, source_target_pairs={{0,6},{1,7},{2,0},{3,1},{4,2},{5,3},{6,4},{7,5},{8,14},{9,15},{10,... | collective-permute-start | bytes 737288 | tf_op jit(solution)/shard_map/ppermute | solution.py:350
  105.7 1.6 %slice_add_fusion.2 = (f32[192,640]{1,0:T(8,128)S(1)}, f32[192,640]{1,0:T(8,128)S(1)}, bf16[192,640]{1,0:T(8,128)(2,1)S(1)}, f32[192,640]{1,0:T(8,128)S(1)}) fusion(f32[768,640]{1,0:T(8,128)S(1)} %project_keep.3, bf16[768,640]{1,0:T(8,128)(2,1)} %collective-permute-done.23), kind=kLoop, calls=%fused_computation.3 | loop fusion | flops 1105920 | bytes 4669440 | tf_op jit(solution)/shard_map/add | solution.py:279
  107.4 0.9 collective-permute-start.26
  108.3 1.3 %collective-permute-start.24 = (bf16[192,640]{1,0:T(8,128)(2,1)S(1)}, bf16[192,640]{1,0:T(8,128)(2,1)S(1)}, u32[]{:S(2)}, u32[]{:S(2)}) collective-permute-start(bf16[192,640]{1,0:T(8,128)(2,1)S(1)} %pad_maximum_fusion.4), channel_id=1, source_target_pairs={{0,2},{1,3},{2,4},{3,5},{4,6},{5,7},{6,0},{7,1},{8,10},{9,11},{10,... | collective-permute-start | bytes 737288 | tf_op jit(solution)/shard_map/ppermute | solution.py:356
  109.6 2.5 %collective-permute-done.19 = bf16[192,640]{1,0:T(8,128)(2,1)S(1)} collective-permute-done((bf16[192,640]{1,0:T(8,128)(2,1)S(1)}, bf16[192,640]{1,0:T(8,128)(2,1)S(1)}, u32[]{:S(2)}, u32[]{:S(2)}) %collective-permute-start.19) | collective-permute-done | bytes 245792 | tf_op jit(solution)/shard_map/ppermute | solution.py:350
  112.1 0.1 fusion.4
  112.3 0.1 collective-permute-start.17
  112.4 1.2 collective-permute-start.20
  113.5 2.2 %collective-permute-done.26 = bf16[192,640]{1,0:T(8,128)(2,1)S(1)} collective-permute-done((bf16[192,640]{1,0:T(8,128)(2,1)S(1)}, bf16[192,640]{1,0:T(8,128)(2,1)S(1)}, u32[]{:S(2)}, u32[]{:S(2)}) %collective-permute-start.26) | collective-permute-done | bytes 245792 | tf_op jit(solution)/shard_map/ppermute | solution.py:357
  115.8 3.8 %collective-permute-start.27 = (bf16[96,640]{1,0:T(8,128)(2,1)S(1)}, bf16[96,640]{1,0:T(8,128)(2,1)S(1)}, u32[]{:S(2)}, u32[]{:S(2)}) collective-permute-start(bf16[96,640]{1,0:T(8,128)(2,1)S(1)} %fusion.8), channel_id=1, source_target_pairs={{0,6},{1,7},{2,0},{3,1},{4,2},{5,3},{6,4},{7,5},{8,14},{9,15},{10,... | collective-permute-start | bytes 368648 | tf_op jit(solution)/shard_map/ppermute | solution.py:366
  119.6 0.1 collective-permute-start.25
  119.7 2.8 %collective-permute-done.17 = bf16[192,640]{1,0:T(8,128)(2,1)S(1)} collective-permute-done((bf16[192,640]{1,0:T(8,128)(2,1)S(1)}, bf16[192,640]{1,0:T(8,128)(2,1)S(1)}, u32[]{:S(2)}, u32[]{:S(2)}) %collective-permute-start.17) | collective-permute-done | bytes 245792 | tf_op jit(solution)/shard_map/ppermute | solution.py:349
  122.5 0.1 fusion.7
  122.7 3.1 %collective-permute-done.25 = bf16[96,640]{1,0:T(8,128)(2,1)S(1)} collective-permute-done((bf16[96,640]{1,0:T(8,128)(2,1)S(1)}, bf16[96,640]{1,0:T(8,128)(2,1)S(1)}, u32[]{:S(2)}, u32[]{:S(2)}) %collective-permute-start.25) | collective-permute-done | bytes 122912 | tf_op jit(solution)/shard_map/ppermute | solution.py:363
  125.8 0.1 fusion.13
  125.9 0.8 pad_maximum_fusion
  (60 shorter events, 0.3 us)
Async XLA Ops:
  0.0 37.4 %copy-start.2 = (bf16[384,640]{1,0:T(8,128)(2,1)S(1)}, bf16[384,640]{1,0:T(8,128)(2,1)}, u32[]{:S(2)}) copy-start(bf16[384,640]{1,0:T(8,128)(2,1)} %refs_0_.5) | copy-start | bytes 1474564
  1.7 8.5 %collective-permute-start.6 = (bf16[96,640]{1,0:T(8,128)(2,1)S(1)}, bf16[96,640]{1,0:T(8,128)(2,1)S(1)}, u32[]{:S(2)}, u32[]{:S(2)}) collective-permute-start(bf16[96,640]{1,0:T(8,128)(2,1)S(1)} %constant_dynamic-update-slice_fusion.refs_8_), channel_id=1, source_target_pairs={{0,112},{8,120},{16,0},{24,8},{32,16},{40,24},{48,32},{56,40},{64,... | collective-permute-start | bytes 368648 | tf_op jit(solution)/shard_map/ppermute | solution.py:292
  7.7 6.3 %collective-permute-start.3 = (bf16[96,640]{1,0:T(8,128)(2,1)S(1)}, bf16[96,640]{1,0:T(8,128)(2,1)S(1)}, u32[]{:S(2)}, u32[]{:S(2)}) collective-permute-start(bf16[96,640]{1,0:T(8,128)(2,1)S(1)} %constant_dynamic-update-slice_fusion.refs_8_), channel_id=1, source_target_pairs={{0,16},{8,24},{16,32},{24,40},{32,48},{40,56},{48,64},{56,72},{64,... | collective-permute-start | bytes 368648 | tf_op jit(solution)/shard_map/ppermute | solution.py:291
  10.2 6.1 %collective-permute-start.7 = (bf16[96,640]{1,0:T(8,128)(2,1)S(1)}, bf16[96,640]{1,0:T(8,128)(2,1)S(1)}, u32[]{:S(2)}, u32[]{:S(2)}) collective-permute-start(bf16[96,640]{1,0:T(8,128)(2,1)S(1)} %collective-permute-done.6.refs_12_), channel_id=1, source_target_pairs={{0,112},{8,120},{16,0},{24,8},{32,16},{40,24},{48,32},{56,40},{64,... | collective-permute-start | bytes 368648 | tf_op jit(solution)/shard_map/ppermute | solution.py:302
  13.9 6.1 %collective-permute-start.4 = (bf16[96,640]{1,0:T(8,128)(2,1)S(1)}, bf16[96,640]{1,0:T(8,128)(2,1)S(1)}, u32[]{:S(2)}, u32[]{:S(2)}) collective-permute-start(bf16[96,640]{1,0:T(8,128)(2,1)S(1)} %collective-permute-done.3.refs_9_), channel_id=1, source_target_pairs={{0,16},{8,24},{16,32},{24,40},{32,48},{40,56},{48,64},{56,72},{64,... | collective-permute-start | bytes 368648 | tf_op jit(solution)/shard_map/ppermute | solution.py:301
  16.4 6.1 %collective-permute-start.8 = (bf16[96,640]{1,0:T(8,128)(2,1)S(1)}, bf16[96,640]{1,0:T(8,128)(2,1)S(1)}, u32[]{:S(2)}, u32[]{:S(2)}) collective-permute-start(bf16[96,640]{1,0:T(8,128)(2,1)S(1)} %collective-permute-done.7.refs_13_), channel_id=1, source_target_pairs={{0,112},{8,120},{16,0},{24,8},{32,16},{40,24},{48,32},{56,40},{64,... | collective-permute-start | bytes 368648 | tf_op jit(solution)/shard_map/ppermute | solution.py:302
  20.0 6.1 %collective-permute-start.5 = (bf16[96,640]{1,0:T(8,128)(2,1)S(1)}, bf16[96,640]{1,0:T(8,128)(2,1)S(1)}, u32[]{:S(2)}, u32[]{:S(2)}) collective-permute-start(bf16[96,640]{1,0:T(8,128)(2,1)S(1)} %collective-permute-done.4.refs_10_), channel_id=1, source_target_pairs={{0,16},{8,24},{16,32},{24,40},{32,48},{40,56},{48,64},{56,72},{64,... | collective-permute-start | bytes 368648 | tf_op jit(solution)/shard_map/ppermute | solution.py:301
  20.0 24.5 %collective-permute-start.1 = (bf16[384,640]{1,0:T(8,128)(2,1)}, bf16[384,640]{1,0:T(8,128)(2,1)S(1)}, u32[]{:S(2)}, u32[]{:S(2)}) collective-permute-start(bf16[384,640]{1,0:T(8,128)(2,1)} %refs_2_.1), channel_id=1, source_target_pairs={{0,16},{8,24},{16,0},{24,8},{32,48},{40,56},{48,32},{56,40},{64,80... | collective-permute-start | bytes 1474568 | tf_op jit(solution)/shard_map/ppermute | solution.py:46
  20.0 24.5 %collective-permute-start.2 = (bf16[384,640]{1,0:T(8,128)(2,1)}, bf16[384,640]{1,0:T(8,128)(2,1)S(1)}, u32[]{:S(2)}, u32[]{:S(2)}) collective-permute-start(bf16[384,640]{1,0:T(8,128)(2,1)} %refs_3_.1), channel_id=1, source_target_pairs={{0,16},{8,24},{16,0},{24,8},{32,48},{40,56},{48,32},{56,40},{64,80... | collective-permute-start | bytes 1474568 | tf_op jit(solution)/shard_map/ppermute | solution.py:46
  22.1 13.7 %collective-permute-start = (bf16[384,640]{1,0:T(8,128)(2,1)}, bf16[384,640]{1,0:T(8,128)(2,1)S(1)}, u32[]{:S(2)}, u32[]{:S(2)}) collective-permute-start(bf16[384,640]{1,0:T(8,128)(2,1)} %refs_0_.5), channel_id=1, source_target_pairs={{0,8},{8,0},{16,24},{24,16},{32,40},{40,32},{48,56},{56,48},{64,72... | collective-permute-start | bytes 1474568 | tf_op jit(solution)/shard_map/ppermute | solution.py:46
  22.1 15.3 %copy-start.15 = (bf16[384,640]{1,0:T(8,128)(2,1)S(1)}, bf16[384,640]{1,0:T(8,128)(2,1)}, u32[]{:S(2)}) copy-start(bf16[384,640]{1,0:T(8,128)(2,1)} %refs_2_.1) | copy-start | bytes 1474564
  22.1 15.3 %copy-start.16 = (bf16[384,640]{1,0:T(8,128)(2,1)S(1)}, bf16[384,640]{1,0:T(8,128)(2,1)}, u32[]{:S(2)}) copy-start(bf16[384,640]{1,0:T(8,128)(2,1)} %refs_3_.1) | copy-start | bytes 1474564
  26.1 6.2 %collective-permute-start.9 = (bf16[96,640]{1,0:T(8,128)(2,1)S(1)}, bf16[96,640]{1,0:T(8,128)(2,1)S(1)}, u32[]{:S(2)}, u32[]{:S(2)}) collective-permute-start(bf16[96,640]{1,0:T(8,128)(2,1)S(1)} %broadcast_select_fusion), channel_id=1, source_target_pairs={{0,112},{8,120},{16,32},{24,40},{32,16},{40,24},{48,64},{56,72},{6... | collective-permute-start | bytes 368648 | tf_op jit(solution)/shard_map/ppermute | solution.py:304
  26.4 9.0 %collective-permute-start.11 = (bf16[192,640]{1,0:T(8,128)(2,1)S(1)}, bf16[192,640]{1,0:T(8,128)(2,1)S(1)}, u32[]{:S(2)}, u32[]{:S(2)}) collective-permute-start(bf16[192,640]{1,0:T(8,128)(2,1)S(1)} %pad_maximum_fusion.2), channel_id=1, source_target_pairs={{0,128},{8,136},{16,144},{24,152},{32,160},{40,168},{48,176},{56,1... | collective-permute-start | bytes 737288 | tf_op jit(solution)/shard_map/ppermute | solution.py:46
  32.3 26.6 %copy-start.5 = (bf16[96,640]{1,0:T(8,128)(2,1)}, bf16[96,640]{1,0:T(8,128)(2,1)S(1)}, u32[]{:S(2)}) copy-start(bf16[96,640]{1,0:T(8,128)(2,1)S(1)} %collective-permute-done.9.refs_15_) | copy-start | bytes 368644
  32.3 12.2 %collective-permute-start.10 = (bf16[288,640]{1,0:T(8,128)(2,1)S(1)}, bf16[288,640]{1,0:T(8,128)(2,1)S(1)}, u32[]{:S(2)}, u32[]{:S(2)}) collective-permute-start(bf16[288,640]{1,0:T(8,128)(2,1)S(1)} %pad_maximum_fusion.1), channel_id=1, source_target_pairs={{0,128},{8,136},{16,144},{24,152},{32,160},{40,168},{48,176},{56,1... | collective-permute-start | bytes 1105928 | tf_op jit(solution)/shard_map/ppermute | solution.py:46
  35.3 14.1 %collective-permute-start.12 = (bf16[192,640]{1,0:T(8,128)(2,1)S(1)}, bf16[192,640]{1,0:T(8,128)(2,1)S(1)}, u32[]{:S(2)}, u32[]{:S(2)}) collective-permute-start(bf16[192,640]{1,0:T(8,128)(2,1)S(1)} %pad_maximum_fusion.3), channel_id=1, source_target_pairs={{0,128},{8,136},{16,144},{24,152},{32,160},{40,168},{48,176},{56,1... | collective-permute-start | bytes 737288 | tf_op jit(solution)/shard_map/ppermute | solution.py:46
  35.8 13.6 %collective-permute-start.13 = (bf16[96,640]{1,0:T(8,128)(2,1)S(1)}, bf16[96,640]{1,0:T(8,128)(2,1)S(1)}, u32[]{:S(2)}, u32[]{:S(2)}) collective-permute-start(bf16[96,640]{1,0:T(8,128)(2,1)S(1)} %collective-permute-done.9.refs_15_), channel_id=1, source_target_pairs={{0,128},{8,136},{16,144},{24,152},{32,160},{40,168},{48,176},{56,1... | collective-permute-start | bytes 368648 | tf_op jit(solution)/shard_map/ppermute | solution.py:46
  41.9 1.3 %copy-start = (f32[768,640]{1,0:T(8,128)}, f32[768,640]{1,0:T(8,128)S(1)}, u32[]{:S(2)}) copy-start(f32[768,640]{1,0:T(8,128)S(1)} %get-tuple-element.20.refs_2_.refs_4_) | copy-start | bytes 5898244
  43.2 1.3 %copy-start.1 = (f32[768,640]{1,0:T(8,128)}, f32[768,640]{1,0:T(8,128)S(1)}, u32[]{:S(2)}) copy-start(f32[768,640]{1,0:T(8,128)S(1)} %get-tuple-element.21.refs_3_.refs_5_) | copy-start | bytes 5898244
  49.4 9.5 %copy-start.7 = (bf16[96,640]{1,0:T(8,128)(2,1)}, bf16[96,640]{1,0:T(8,128)(2,1)S(1)}, u32[]{:S(2)}) copy-start(bf16[96,640]{1,0:T(8,128)(2,1)S(1)} %collective-permute-done.13.refs_19_) | copy-start | bytes 368644
  49.4 9.5 %copy-start.3 = (bf16[192,640]{1,0:T(8,128)(2,1)}, bf16[192,640]{1,0:T(8,128)(2,1)S(1)}, u32[]{:S(2)}) copy-start(bf16[192,640]{1,0:T(8,128)(2,1)S(1)} %collective-permute-done.12.refs_18_) | copy-start | bytes 737284
  58.9 0.7 copy-start.9
  59.7 0.7 copy-start.17
  60.3 12.9 %collective-permute-start.21 = (bf16[192,640]{1,0:T(8,128)(2,1)}, bf16[192,640]{1,0:T(8,128)(2,1)}, u32[]{:S(2)}, u32[]{:S(2)}) collective-permute-start(bf16[192,640]{1,0:T(8,128)(2,1)} %get-tuple-element.31), channel_id=1, source_target_pairs={{0,8},{8,0},{16,24},{24,16},{32,40},{40,32},{48,56},{56,48},{64,72... | collective-permute-start | bytes 737288 | tf_op jit(solution)/shard_map/ppermute | solution.py:46
  60.3 12.9 %collective-permute-start.22 = (f32[192,128]{1,0:T(8,128)}, f32[192,128]{1,0:T(8,128)S(1)}, u32[]{:S(2)}, u32[]{:S(2)}) collective-permute-start(f32[192,128]{1,0:T(8,128)} %copy-done.17), channel_id=1, source_target_pairs={{0,8},{8,0},{16,24},{24,16},{32,40},{40,32},{48,56},{56,48},{64,72... | collective-permute-start | bytes 294920 | tf_op jit(solution)/shard_map/ppermute | solution.py:46
  60.8 0.9 copy-start.4
  61.8 0.9 copy-start.6
  62.7 0.9 copy-start.8
  63.6 9.7 %copy-start.10 = (bf16[192,640]{1,0:T(8,128)(2,1)S(1)}, bf16[192,640]{1,0:T(8,128)(2,1)}, u32[]{:S(2)}) copy-start(bf16[192,640]{1,0:T(8,128)(2,1)} %copy-done.9) | copy-start | bytes 737284
  73.1 4.8 %copy-start.11 = (bf16[192,640]{1,0:T(8,128)(2,1)}, bf16[192,640]{1,0:T(8,128)(2,1)S(1)}, u32[]{:S(2)}) copy-start(bf16[192,640]{1,0:T(8,128)(2,1)S(1)} %get-tuple-element.22.own) | copy-start | bytes 737284
  73.1 4.8 %copy-start.13 = (f32[192,128]{1,0:T(8,128)}, f32[192,128]{1,0:T(8,128)S(1)}, u32[]{:S(2)}) copy-start(f32[192,128]{1,0:T(8,128)S(1)} %get-tuple-element.23.own_log) | copy-start | bytes 294916
  73.1 4.8 %copy-start.18 = (f32[192,128]{1,0:T(8,128)}, f32[192,128]{1,0:T(8,128)S(1)}, u32[]{:S(2)}) copy-start(f32[192,128]{1,0:T(8,128)S(1)} %get-tuple-element.25) | copy-start | bytes 294916
  73.1 8.7 %collective-permute-start.14 = (bf16[192,640]{1,0:T(8,128)(2,1)}, bf16[192,640]{1,0:T(8,128)(2,1)S(1)}, u32[]{:S(2)}, u32[]{:S(2)}) collective-permute-start(bf16[192,640]{1,0:T(8,128)(2,1)} %get-tuple-element.24), channel_id=1, source_target_pairs={{0,8},{8,0},{16,24},{24,16},{32,40},{40,32},{48,56},{56,48},{64,72... | collective-permute-start | bytes 737288 | tf_op jit(solution)/shard_map/ppermute | solution.py:46
  77.9 27.8 %collective-permute-start.23 = (bf16[768,640]{1,0:T(8,128)(2,1)S(1)}, bf16[768,640]{1,0:T(8,128)(2,1)}, u32[]{:S(2)}, u32[]{:S(2)}) collective-permute-start(bf16[768,640]{1,0:T(8,128)(2,1)S(1)} %get-tuple-element.34), channel_id=1, source_target_pairs={{0,1},{1,0},{2,3},{3,2},{4,5},{5,4},{6,7},{7,6},{8,9},{9,8},{10,11... | collective-permute-start | bytes 2949128 | tf_op jit(solution)/shard_map/ppermute | solution.py:46
  80.3 1.5 %collective-permute-start.15 = (f32[192,128]{1,0:T(8,128)}, f32[192,128]{1,0:T(8,128)S(1)}, u32[]{:S(2)}, u32[]{:S(2)}) collective-permute-start(f32[192,128]{1,0:T(8,128)} %copy-done.18), channel_id=1, source_target_pairs={{0,8},{8,0},{16,24},{24,16},{32,40},{40,32},{48,56},{56,48},{64,72... | collective-permute-start | bytes 294920 | tf_op jit(solution)/shard_map/ppermute | solution.py:46
  81.8 0.9 copy-start.12
  82.7 0.9 copy-start.14
  88.2 13.7 %collective-permute-start.18 = (bf16[384,640]{1,0:T(8,128)(2,1)S(1)}, bf16[384,640]{1,0:T(8,128)(2,1)S(1)}, u32[]{:S(2)}, u32[]{:S(2)}) collective-permute-start(bf16[384,640]{1,0:T(8,128)(2,1)S(1)} %get-tuple-element.28), channel_id=1, source_target_pairs={{0,6},{1,7},{2,0},{3,1},{4,2},{5,3},{6,4},{7,5},{8,14},{9,15},{10,... | collective-permute-start | bytes 1474568 | tf_op jit(solution)/shard_map/ppermute | solution.py:337
  91.2 18.4 %collective-permute-start.16 = (bf16[384,640]{1,0:T(8,128)(2,1)S(1)}, bf16[384,640]{1,0:T(8,128)(2,1)S(1)}, u32[]{:S(2)}, u32[]{:S(2)}) collective-permute-start(bf16[384,640]{1,0:T(8,128)(2,1)S(1)} %get-tuple-element.27), channel_id=1, source_target_pairs={{0,2},{1,3},{2,4},{3,5},{4,6},{5,7},{6,0},{7,1},{8,10},{9,11},{10,... | collective-permute-start | bytes 1474568 | tf_op jit(solution)/shard_map/ppermute | solution.py:336
  101.9 10.2 %collective-permute-start.19 = (bf16[192,640]{1,0:T(8,128)(2,1)S(1)}, bf16[192,640]{1,0:T(8,128)(2,1)S(1)}, u32[]{:S(2)}, u32[]{:S(2)}) collective-permute-start(bf16[192,640]{1,0:T(8,128)(2,1)S(1)} %fusion.1), channel_id=1, source_target_pairs={{0,6},{1,7},{2,0},{3,1},{4,2},{5,3},{6,4},{7,5},{8,14},{9,15},{10,... | collective-permute-start | bytes 737288 | tf_op jit(solution)/shard_map/ppermute | solution.py:350
  107.4 8.4 %collective-permute-start.26 = (bf16[192,640]{1,0:T(8,128)(2,1)S(1)}, bf16[192,640]{1,0:T(8,128)(2,1)S(1)}, u32[]{:S(2)}, u32[]{:S(2)}) collective-permute-start(bf16[192,640]{1,0:T(8,128)(2,1)S(1)} %pad_maximum_fusion.5), channel_id=1, source_target_pairs={{0,6},{1,7},{2,0},{3,1},{4,2},{5,3},{6,4},{7,5},{8,14},{9,15},{10,... | collective-permute-start | bytes 737288 | tf_op jit(solution)/shard_map/ppermute | solution.py:357
  108.3 11.3 %collective-permute-start.24 = (bf16[192,640]{1,0:T(8,128)(2,1)S(1)}, bf16[192,640]{1,0:T(8,128)(2,1)S(1)}, u32[]{:S(2)}, u32[]{:S(2)}) collective-permute-start(bf16[192,640]{1,0:T(8,128)(2,1)S(1)} %pad_maximum_fusion.4), channel_id=1, source_target_pairs={{0,2},{1,3},{2,4},{3,5},{4,6},{5,7},{6,0},{7,1},{8,10},{9,11},{10,... | collective-permute-start | bytes 737288 | tf_op jit(solution)/shard_map/ppermute | solution.py:356
  112.3 10.2 %collective-permute-start.17 = (bf16[192,640]{1,0:T(8,128)(2,1)S(1)}, bf16[192,640]{1,0:T(8,128)(2,1)S(1)}, u32[]{:S(2)}, u32[]{:S(2)}) collective-permute-start(bf16[192,640]{1,0:T(8,128)(2,1)S(1)} %get-tuple-element.39), channel_id=1, source_target_pairs={{0,2},{1,3},{2,4},{3,5},{4,6},{5,7},{6,0},{7,1},{8,10},{9,11},{10,... | collective-permute-start | bytes 737288 | tf_op jit(solution)/shard_map/ppermute | solution.py:349
  112.4 10.1 %collective-permute-start.20 = (bf16[192,640]{1,0:T(8,128)(2,1)S(1)}, bf16[192,640]{1,0:T(8,128)(2,1)S(1)}, u32[]{:S(2)}, u32[]{:S(2)}) collective-permute-start(bf16[192,640]{1,0:T(8,128)(2,1)S(1)} %get-tuple-element.40), channel_id=1, source_target_pairs={{0,1},{1,0},{2,3},{3,2},{4,5},{5,4},{6,7},{7,6},{8,9},{9,8},{10,11... | collective-permute-start | bytes 737288 | tf_op jit(solution)/shard_map/ppermute | solution.py:46
  115.8 6.9 %collective-permute-start.27 = (bf16[96,640]{1,0:T(8,128)(2,1)S(1)}, bf16[96,640]{1,0:T(8,128)(2,1)S(1)}, u32[]{:S(2)}, u32[]{:S(2)}) collective-permute-start(bf16[96,640]{1,0:T(8,128)(2,1)S(1)} %fusion.8), channel_id=1, source_target_pairs={{0,6},{1,7},{2,0},{3,1},{4,2},{5,3},{6,4},{7,5},{8,14},{9,15},{10,... | collective-permute-start | bytes 368648 | tf_op jit(solution)/shard_map/ppermute | solution.py:366
  119.6 6.2 %collective-permute-start.25 = (bf16[96,640]{1,0:T(8,128)(2,1)S(1)}, bf16[96,640]{1,0:T(8,128)(2,1)S(1)}, u32[]{:S(2)}, u32[]{:S(2)}) collective-permute-start(bf16[96,640]{1,0:T(8,128)(2,1)S(1)} %fusion.11), channel_id=1, source_target_pairs={{0,2},{1,3},{2,4},{3,5},{4,6},{5,7},{6,0},{7,1},{8,10},{9,11},{10,... | collective-permute-start | bytes 368648 | tf_op jit(solution)/shard_map/ppermute | solution.py:363

commit v2 on v0

v2 whole, which is shorter than its diff:
```python
import functools
import math

import jax
import jax.numpy as jnp
from jax import lax
from jax.experimental import pallas as pl
from jax.experimental.pallas import tpu as pltpu
from jax.sharding import PartitionSpec as P

HD = 128
Z = 8
X = 4
BASE2 = math.log2(math.e) / math.sqrt(HD)
F32 = jnp.float32
BF16 = jnp.bfloat16
VMEM_LIMIT = 20 << 20
IN_VMEM = pl.BlockSpec(memory_space=pltpu.VMEM)
CUT = 224
CHUNKS = 4
LITTLE = pl.CostEstimate(flops=1, bytes_accessed=1, transcendentals=0)


def seq_place(i):
    return i // (2 * Z), (i // 2) % Z, i % 2


def between_frames():
    pairs = []
    for i in range(4 * Z):
        y, z, core = seq_place(i)
        other = (z + 1) % Z if z % 2 else (z - 1) % Z
        pairs.append((i, (y * Z + other) * 2 + core))
    return pairs


def along_x(step):
    return [(i, (i // 2 + step) % X * 2 + i % 2) for i in range(2 * X)]


def swap(value, axis, bit):
    return lax.ppermute(value, axis, [(i, i ^ bit) for i in range(lax.axis_size(axis))])


def held(array):
    return pltpu.with_memory_space_constraint(array, pltpu.VMEM)


def local(kernel, outs, *ins, scalars=(), scratch=(), name="local"):
    return pl.pallas_call(
        kernel,
        in_specs=[pl.BlockSpec(memory_space=pltpu.SMEM)] * len(scalars) + [IN_VMEM] * len(ins),
        out_specs=[IN_VMEM] * len(outs),
        out_shape=[pltpu.VMEM(shape, dtype) for shape, dtype in outs],
        scratch_shapes=list(scratch),
        compiler_params=pltpu.CompilerParams(vmem_limit_bytes=VMEM_LIMIT),
        cost_estimate=LITTLE,
        name=name,
    )(*scalars, *(held(a) for a in ins))


def stack_kernel(parts, *refs):
    ins, out, sems = refs[:-2], refs[-2], refs[-1]
    copies = []
    at = 0
    for number, (place, low, high) in enumerate(parts):
        rows = high - low
        copies.append(
            pltpu.make_async_copy(
                ins[place].at[low:high, :], out.at[at : at + rows, :], sems.at[number]
            )
        )
        at += rows
    for copy in copies:
        copy.start()
    for copy in copies:
        copy.wait()


def stacked(*arrays, parts=None):
    parts = parts or tuple((n, 0, a.shape[0]) for n, a in enumerate(arrays))
    rows = sum(high - low for _, low, high in parts)
    return pl.pallas_call(
        functools.partial(stack_kernel, parts),
        in_specs=[pl.BlockSpec(memory_space=pl.ANY)] * len(arrays),
        out_specs=IN_VMEM,
        out_shape=pltpu.VMEM((rows, arrays[0].shape[1]), arrays[0].dtype),
        scratch_shapes=[pltpu.SemaphoreType.DMA((len(parts),))],
        compiler_params=pltpu.CompilerParams(vmem_limit_bytes=VMEM_LIMIT),
        cost_estimate=LITTLE,
        name="stacked",
    )(*arrays)


def scores_of(rows, keys):
    return lax.dot_general(rows, keys, (((1,), (1,)), ((), ())), preferred_element_type=F32)


def fill_keys(key_ref, value_ref, halves, pieces, columns):
    at = 0
    for half, piece in zip(halves, pieces):
        for low in range(0, piece.shape[0], 2 * half):
            key_ref[at : at + half, :] = piece[low : low + half, columns]
            value_ref[at : at + half, :HD] = piece[low + half : low + 2 * half, columns]
            at += half
    value_ref[:, HD:] = jnp.ones((at, HD), BF16)


def attend_kernel(halves, low, high, with_state, last, *refs):
    queries, refs = refs[:2], refs[2:]
    if with_state:
        (before, before_log), refs = refs[:2], refs[2:]
    pieces, refs = refs[: len(halves)], refs[len(halves) :]
    if last:
        (own_ref, own_log, other_ref, key_ref, value_ref, query_ref, log_ref) = refs
    else:
        (part_ref, log_ref, key_ref, value_ref, query_ref) = refs
    rows = high - low
    whole_rows = queries[0].shape[0]
    heads = queries[0].shape[1] // HD
    for head in range(heads):
        columns = slice(head * HD, (head + 1) * HD)
        slot = head % 2
        fill_keys(key_ref.at[slot], value_ref.at[slot], halves, pieces, columns)
        for place in range(2):
            query_ref[slot, place * rows : (place + 1) * rows, :] = queries[place][low:high, columns]
        scores = scores_of(query_ref[slot], key_ref[slot])
        peak = jnp.max(scores, axis=1, keepdims=True)
        weights = jnp.exp2((scores - peak) * BASE2).astype(BF16)
        both = jnp.dot(weights, value_ref[slot], preferred_element_type=F32)
        summed, total = both[:, :HD], both[:, HD:]
        peak = peak * BASE2
        for place in range(2):
            part = slice(place * rows, (place + 1) * rows)
            if with_state:
                held_rows = slice(place * whole_rows + low, place * whole_rows + high)
                log = before_log[held_rows, head : head + 1]
                top = jnp.maximum(log, peak[part])
                before_factor = jnp.exp2(log - top)
                factor = jnp.exp2(peak[part] - top)
                whole = before_factor + total[part] * factor
                result = (before[held_rows, columns] * before_factor + summed[part] * factor) / whole
            else:
                top = peak[part]
                whole = total[part]
                result = summed[part] / whole
            if last:
                (own_ref, other_ref)[place][:, columns] = result.astype(BF16)
            else:
                part_ref[part, columns] = result
            log_ref[part, head : head + 1] = (top + jnp.log2(whole))[:, :1]
    if last:
        lane = lax.broadcasted_iota(jnp.int32, (rows, HD), 1)
        own_log[...] = log_ref[:rows, :]
        logs = log_ref[rows:, :]
        high_part = logs.astype(BF16).astype(F32)
        rest = logs - high_part
        middle = rest.astype(BF16).astype(F32)
        packed = jnp.where(
            lane < 8,
            high_part,
            jnp.where(lane < 16, pltpu.roll(middle, 8, 1), pltpu.roll(rest - middle, 16, 1)),
        )
        other_ref[:, heads * HD :] = jnp.where(lane < 24, packed, 0.0).astype(BF16)


def attend(queries, other_queries, low, high, halves, pieces, state=None, last=False):
    whole_rows, width = queries.shape
    heads = width // HD
    rows = high - low
    keys = sum(piece.shape[0] for piece in pieces) // 2
    if last:
        outs = [((rows, width), BF16), ((rows, HD), F32), ((rows, width + HD), BF16)]
    else:
        outs = [((2 * rows, width), F32), ((2 * rows, HD), F32)]
    return local(
        functools.partial(attend_kernel, halves, low, high, state is not None, last),
        outs,
        queries,
        other_queries,
        *(state or ()),
        *pieces,
        scratch=[
            pltpu.VMEM((2, keys, HD), BF16),
            pltpu.VMEM((2, keys, 2 * HD), BF16),
            pltpu.VMEM((2, 2 * rows, HD), BF16),
        ]
        + [pltpu.VMEM((2 * rows, HD), F32)] * last,
        name="attend_last" if last else "attend_part",
    )


def merge_heads(own, own_log, got, att):
    width = own.shape[1]
    logs = got[:, width:].astype(F32)
    got_log = logs + pltpu.roll(logs, HD - 8, 1) + pltpu.roll(logs, HD - 16, 1)
    for head in range(width // HD):
        columns = slice(head * HD, (head + 1) * HD)
        first, second = own_log[:, head : head + 1], got_log[:, head : head + 1]
        top = jnp.maximum(first, second)
        first_factor = jnp.exp2(first - top)
        second_factor = jnp.exp2(second - top)
        scale = 1.0 / (first_factor + second_factor)
        att[:, columns] = (
            own[:, columns].astype(F32) * (first_factor * scale)
            + got[:, columns].astype(F32) * (second_factor * scale)
        ).astype(BF16)


def products(blocks, place, att, weight, outs):
    rows, width = att.shape
    number = 0
    x, side = place[0] // 2, place[0] % 2
    for out in outs:
        for low in range(0, out.shape[0], rows):
            step, flip = blocks[number]
            block = lax.rem(x + step, X) * 2 + (1 - side if flip else side)
            at = pl.multiple_of(block * width, HD)
            result = jnp.dot(att[...], weight[:, pl.ds(at, width)], preferred_element_type=F32)
            out[low : low + rows, :] = result.astype(out.dtype)
            number += 1


def send_kernel(blocks, place, own, own_log, got, weight, *outs):
    merge_heads(own, own_log, got, outs[-1])
    products(blocks, place, outs[-1], weight, outs[:-1])


def project_send(blocks, place, own, own_log, got, weight, n_outs):
    rows, width = own.shape
    count = len(blocks)
    outs = [((count // n_outs * rows, width), BF16)] * n_outs + [((rows, width), BF16)]
    return local(
        functools.partial(send_kernel, blocks),
        outs,
        own,
        own_log,
        got,
        weight,
        scalars=(place,),
        name="project_send",
    )


def keep_kernel(blocks, place, att, weight, out):
    products(blocks, place, att, weight, (out,))


def project_keep(blocks, place, att, weight):
    rows, width = att.shape
    count = len(blocks)
    return local(
        functools.partial(keep_kernel, blocks),
        [((count * rows, width), F32)],
        att,
        weight,
        scalars=(place,),
        name="project_keep",
    )[0]


def relay_kernel(kept, got_left, got_right, to_right, to_left):
    n = to_right.shape[0]
    to_right[...] = (kept[:n, :] + got_left[:n, :].astype(F32)).astype(BF16)
    to_left[...] = (kept[n : 2 * n, :] + got_right[:n, :].astype(F32)).astype(BF16)


def turn_kernel(kept, got_left, on_left, out):
    n = out.shape[0]
    out[...] = (
        kept[3 * n :, :] + on_left[...].astype(F32) + got_left[n:, :].astype(F32)
    ).astype(BF16)


def spread_kernel(kept, got, to_right, to_left, rest):
    m = to_right.shape[0]
    q = m // 2

    def total(block, low, high):
        rows = slice(block * m + low, block * m + high)
        return kept[rows, :] + got[rows, :].astype(F32)

    to_right[:q, :] = total(0, 0, q).astype(BF16)
    to_right[q:, :] = total(1, q, m).astype(BF16)
    to_left[:q, :] = total(0, q, m).astype(BF16)
    to_left[q:, :] = total(2, 0, q).astype(BF16)
    rest[:q, :] = total(1, 0, q)
    rest[q:m, :] = total(2, q, m)
    rest[m:, :] = total(3, 0, m)


def last_kernel(kept, on_right, got_right, mine, rest, on_right2, on_left2, left2, right2, out):
    n = on_right.shape[0]
    m = left2.shape[0]
    q = m // 2
    out[:n, :] = (
        kept[2 * n : 3 * n, :]
        + on_right[...].astype(F32)
        + got_right[n:, :].astype(F32)
        + mine[...].astype(F32)
    ).astype(BF16)
    out[n : n + q, :] = (
        rest[m : m + q, :] + on_right2[...].astype(F32) + right2[q:, :].astype(F32)
    ).astype(BF16)
    out[n + q :, :] = (
        rest[m + q :, :] + on_left2[...].astype(F32) + left2[q:, :].astype(F32)
    ).astype(BF16)


def body(queries, keys, values, ref_keys, ref_values, out_weight):
    rows, width = queries.shape
    half = ref_keys.shape[0]
    between = between_frames()
    right_x, left_x = along_x(1), along_x(-1)
    place = lax.axis_index("head").reshape(1)
    place, ref_keys = lax.optimization_barrier((place, ref_keys))

    own = stacked(ref_keys, ref_values)
    inner = [swap(own, "seq", 2)]
    outer = [lax.ppermute(own, "seq", between)]
    other_queries = swap(queries, "seq", 1)
    frame, other_frame, across = [], [], []

    def exchange_chunk(number, after):
        part = rows // CHUNKS
        low, high = number * part, (number + 1) * part
        held_back, _ = lax.optimization_barrier(((keys, values), after))
        chunk = stacked(*held_back, parts=((0, low, high), (1, low, high)))
        frame.append(chunk)
        other_frame.append(swap(chunk, "seq", 2))

    exchange_chunk(0, other_queries)
    for step in range(3):
        came_inner, came_outer = inner[-1], outer[-1]
        if step < 2:
            inner.append(swap(came_outer, "seq", 2))
        outer.append(lax.ppermute(came_inner, "seq", between))
        packed = stacked(*([own] * (step == 0)), came_inner, came_outer)
        exchange_chunk(step + 1, packed)
        across.append(swap(packed, "seq", 2 * Z))
    far, frame, other_frame = lax.optimization_barrier((outer[-1], frame, other_frame))
    across.append(swap(far, "seq", 2 * Z))
    state = attend(
        queries, other_queries, 0, rows, (rows // CHUNKS,) * (2 * CHUNKS), (*frame, *other_frame)
    )
    pieces = (own, *inner, *outer[:-1], far, *across)
    halves = (half,) * len(pieces)

    def finish(low, high):
        own_part, own_log, other_part = attend(
            queries, other_queries, low, high, halves, pieces, state, True
        )
        return own_part, own_log, swap(other_part, "seq", 1)

    done = finish(0, CUT)
    go_right, go_left, att = project_send(
        ((2, 0), (1, 1), (2, 1), (3, 0)), place, *done, out_weight, 2
    )
    got_left = lax.ppermute(go_right, "head", right_x)
    got_right = lax.ppermute(go_left, "head", left_x)

    last_done = finish(CUT, rows)
    go_across, last_att = project_send(
        ((2, 1), (1, 1), (3, 1), (0, 1)), place, *last_done, out_weight, 1
    )
    got_across = swap(go_across, "head", 1)

    kept = project_keep(((1, 0), (3, 1), (0, 0), (0, 1)), place, att, out_weight)
    last_kept = project_keep(((2, 0), (1, 0), (3, 0), (0, 0)), place, last_att, out_weight)

    one = ((CUT, width), BF16)
    to_right, to_left = local(relay_kernel, [one, one], kept, got_left, got_right, name="relay")
    on_right = lax.ppermute(to_right, "head", right_x)
    on_left = lax.ppermute(to_left, "head", left_x)

    m = rows - CUT
    two = ((m, width), BF16)
    last_right, last_left, rest = local(
        spread_kernel, [two, two, ((2 * m, width), F32)], last_kept, got_across, name="spread"
    )
    left2 = lax.ppermute(last_right, "head", right_x)
    right2 = lax.ppermute(last_left, "head", left_x)

    (turned,) = local(turn_kernel, [one], kept, got_left, on_left, name="turn")
    mine_got = swap(turned, "head", 1)

    small = ((m // 2, width), BF16)
    to_right2, to_left2 = local(relay_kernel, [small, small], rest, left2, right2, name="relay")
    on_right2 = lax.ppermute(to_right2, "head", right_x)
    on_left2 = lax.ppermute(to_left2, "head", left_x)
    return local_out(
        last_kernel,
        ((rows, width), BF16),
        kept,
        on_right,
        got_right,
        mine_got,
        rest,
        on_right2,
        on_left2,
        left2,
        right2,
    )


def local_out(kernel, out, *ins):
    return pl.pallas_call(
        kernel,
        in_specs=[IN_VMEM] * len(ins),
        out_specs=IN_VMEM,
        out_shape=jax.ShapeDtypeStruct(*out),
        compiler_params=pltpu.CompilerParams(vmem_limit_bytes=VMEM_LIMIT),
        cost_estimate=LITTLE,
        name="last",
    )(*(held(a) for a in ins))


def solution(mesh):
    placed = (
        P("seq", "head"),
        P("seq", "head"),
        P("seq", "head"),
        P("seq", "head"),
        P("seq", "head"),
        P("head", None),
    )
    return jax.shard_map(
        body, mesh=mesh, in_specs=placed, out_specs=P("seq", "head"), check_vma=False
    )
```

time: 265 us -> 106 us (0.40)
  waiting for transfers between devices: 184 us -> 42.7 us
  starting transfers between devices: 2.7 us -> 37.5 us
  local copies, waits for them, and re-layouts: 32.1 us -> 3.78 us
  matrix products: 24.6 us -> 0 us
  Pallas kernels: 0 us -> 21.1 us
  between operations: 13.3 us -> 0.21 us
  other arithmetic: 6.6 us -> 0.01 us
    unnamed x4 -> x0, waiting for transfers between devices: 89.4 us -> none
    all_gather x2 -> x0, waiting for transfers between devices: 50.4 us -> none  [the longest x1 49.3 us: body(): lax.all_gather(ref_values, 'seq', axis=0, tiled=True)]
    ppermute x4 -> x28, starting transfers between devices: 2.62 us -> 37.5 us  [the longest x16 11.2 us: swap(): lax.ppermute(value, axis, [(i, i ^ bit) for i in range(lax.axis_size(axis...]
    dot_general x9 -> x0, matrix products: 24.6 us -> none  [the longest x4 10.9 us: attend(): jnp.einsum('hts,shd->htd', weights.astype(jnp.bfloat16), value_heads, pre...]
    pallas_call x0 -> x20, Pallas kernels: none -> 21.1 us  [the longest x11 17.5 us: local(): pl.pallas_call(kernel, in_specs=[pl.BlockSpec(memory_space=pltpu.SMEM)] *...]
    unnamed x37 -> x16, local copies, waits for them, and re-layouts: 19.6 us -> 3.78 us
    all_gather x2 -> x0, local copies, waits for them, and re-layouts: 8.17 us -> none  [the longest x1 4.16 us: body(): lax.all_gather(ref_values, 'seq', axis=0, tiled=True)]
    reduce_sum x3 -> x0, other arithmetic: 4.31 us -> none  [attend(): totals = jnp.sum(weights, axis=2)]
  transfers between devices with their start and end apart: 7 -> 28, of which waited for: 4 -> 15; matrix products, arithmetic and copies ran while one was open for 12% -> 0% of each run, Pallas kernels for 0% -> 15%
where the time goes in v2:
time: 106 us; the launch traced here: 105 us
  waiting for transfers between devices  42.7 us (40%)
  starting transfers between devices  37.5 us (35%)
  Pallas kernels  21.1 us (20%)
  local copies, waits for them, and re-layouts  3.78 us (4%)
    ppermute x16, waiting for transfers between devices, swap(): lax.ppermute(value, axis, [(i, i ^ bit) for i in range(lax.axis_size(axis...  22 us
    pallas_call x11, Pallas kernels, local(): pl.pallas_call(kernel, in_specs=[pl.BlockSpec(memory_space=pltpu.SMEM)] *...  17.5 us
    ppermute x16, starting transfers between devices, swap(): lax.ppermute(value, axis, [(i, i ^ bit) for i in range(lax.axis_size(axis...  11.2 us
    ppermute x1, waiting for transfers between devices, body(): got_left = lax.ppermute(go_right, 'head', right_x)  7.96 us
    ppermute x3, starting transfers between devices, body(): outer.append(lax.ppermute(came_inner, 'seq', between))  7.41 us
    ppermute x1, starting transfers between devices, body(): outer = [lax.ppermute(own, 'seq', between)]  5.94 us
    ppermute x1, waiting for transfers between devices, body(): outer = [lax.ppermute(own, 'seq', between)]  3.93 us
    unnamed x16, local copies, waits for them, and re-layouts  3.78 us
  transfers between devices with their start and end apart: 28, of which 15 were waited for; matrix products, arithmetic and copies ran while one was open for 0% of the time, Pallas kernels for 15%

profile of v2, /device:TPU:8, one launch (start us, length us, event | category | flops | bytes accessed | tf_op | source)
XLA Modules:
  0.0 105.3 jit_solution(18250534601864144296)
XLA Ops:
  0.0 0.9 copy-done.4
  0.9 0.8 copy-done.5
  1.7 0.1 stacked.8.refs_0_.refs_4_
  1.9 5.9 %collective-permute-start.5 = (bf16[96,640]{1,0:T(8,128)(2,1)S(1)}, bf16[96,640]{1,0:T(8,128)(2,1)S(1)}, u32[]{:S(2)}, u32[]{:S(2)}) collective-permute-start(bf16[96,640]{1,0:T(8,128)(2,1)S(1)} %stacked.8.refs_0_.refs_4_), channel_id=1, source_target_pairs={{0,112},{8,120},{16,32},{24,40},{32,16},{40,24},{48,64},{56,72},{6... | collective-permute-start | bytes 368648 | tf_op jit(solution)/shard_map/ppermute | solution.py:320
  7.8 3.9 %collective-permute-done.5.refs_2_.refs_8_ = bf16[96,640]{1,0:T(8,128)(2,1)S(1)} collective-permute-done((bf16[96,640]{1,0:T(8,128)(2,1)S(1)}, bf16[96,640]{1,0:T(8,128)(2,1)S(1)}, u32[]{:S(2)}, u32[]{:S(2)}) %collective-permute-start.5) | collective-permute-done | bytes 122912 | tf_op jit(solution)/shard_map/ppermute | solution.py:320
  11.8 1.5 %collective-permute-done.1.refs_1_.refs_5_ = bf16[96,640]{1,0:T(8,128)(2,1)S(1)} collective-permute-done((bf16[96,640]{1,0:T(8,128)(2,1)S(1)}, bf16[96,640]{1,0:T(8,128)(2,1)S(1)}, u32[]{:S(2)}, u32[]{:S(2)}) %collective-permute-start.1) | collective-permute-done | bytes 122912 | tf_op jit(solution)/shard_map/ppermute | solution.py:42
  13.2 1.5 %collective-permute-start.2 = (bf16[96,640]{1,0:T(8,128)(2,1)S(1)}, bf16[96,640]{1,0:T(8,128)(2,1)S(1)}, u32[]{:S(2)}, u32[]{:S(2)}) collective-permute-start(bf16[96,640]{1,0:T(8,128)(2,1)S(1)} %collective-permute-done.1.refs_1_.refs_5_), channel_id=1, source_target_pairs={{0,112},{8,120},{16,32},{24,40},{32,16},{40,24},{48,64},{56,72},{6... | collective-permute-start | bytes 368648 | tf_op jit(solution)/shard_map/ppermute | solution.py:337
  14.7 0.5 stacked.10
  15.2 0.0 copy-start
  15.2 1.0 copy-done
  16.2 1.0 copy-done.2
  17.3 0.3 stacked.11.refs_3_
  17.6 0.0 copy-start.3
  17.6 0.2 collective-permute-start.9
  17.7 2.9 %collective-permute-start.7 = (bf16[96,640]{1,0:T(8,128)(2,1)S(1)}, bf16[96,640]{1,0:T(8,128)(2,1)S(1)}, u32[]{:S(2)}, u32[]{:S(2)}) collective-permute-start(bf16[96,640]{1,0:T(8,128)(2,1)S(1)} %collective-permute-done.6.refs_0_.refs_6_), channel_id=1, source_target_pairs={{0,112},{8,120},{16,32},{24,40},{32,16},{40,24},{48,64},{56,72},{6... | collective-permute-start | bytes 368648 | tf_op jit(solution)/shard_map/ppermute | solution.py:337
  20.7 0.0 collective-permute-start.3
  20.7 0.3 stacked.12
  21.0 0.3 stacked.13.refs_4_
  21.4 2.1 %collective-permute-start.10 = (bf16[192,640]{1,0:T(8,128)(2,1)S(1)}, bf16[192,640]{1,0:T(8,128)(2,1)S(1)}, u32[]{:S(2)}, u32[]{:S(2)}) collective-permute-start(bf16[192,640]{1,0:T(8,128)(2,1)S(1)} %stacked.13.refs_4_), channel_id=1, source_target_pairs={{0,16},{8,24},{16,0},{24,8},{32,48},{40,56},{48,32},{56,40},{64,80... | collective-permute-start | bytes 737288 | tf_op jit(solution)/shard_map/ppermute | solution.py:42
  23.5 0.4 collective-permute-done.7.refs_1_.refs_10_
  23.9 5.3 %collective-permute-done.3.refs_0_.refs_7_ = bf16[96,640]{1,0:T(8,128)(2,1)S(1)} collective-permute-done((bf16[96,640]{1,0:T(8,128)(2,1)S(1)}, bf16[96,640]{1,0:T(8,128)(2,1)S(1)}, u32[]{:S(2)}, u32[]{:S(2)}) %collective-permute-start.3) | collective-permute-done | bytes 122912 | tf_op jit(solution)/shard_map/ppermute | solution.py:42
  29.2 0.3 stacked.14
  29.5 0.3 stacked.15.refs_5_
  29.9 0.1 collective-permute-start.11
  30.0 3.0 %collective-permute-start.4 = (bf16[96,640]{1,0:T(8,128)(2,1)S(1)}, bf16[96,640]{1,0:T(8,128)(2,1)S(1)}, u32[]{:S(2)}, u32[]{:S(2)}) collective-permute-start(bf16[96,640]{1,0:T(8,128)(2,1)S(1)} %collective-permute-done.3.refs_0_.refs_7_), channel_id=1, source_target_pairs={{0,112},{8,120},{16,32},{24,40},{32,16},{40,24},{48,64},{56,72},{6... | collective-permute-start | bytes 368648 | tf_op jit(solution)/shard_map/ppermute | solution.py:337
  33.0 0.3 stacked.9.refs_2_
  33.3 0.1 collective-permute-start.8
  33.4 0.5 collective-permute-start.12
  33.9 2.2 %collective-permute-done.4.refs_11_ = bf16[96,640]{1,0:T(8,128)(2,1)S(1)} collective-permute-done((bf16[96,640]{1,0:T(8,128)(2,1)S(1)}, bf16[96,640]{1,0:T(8,128)(2,1)S(1)}, u32[]{:S(2)}, u32[]{:S(2)}) %collective-permute-start.4) | collective-permute-done | bytes 122912 | tf_op jit(solution)/shard_map/ppermute | solution.py:337
  36.1 0.4 collective-permute-start.13
  36.6 1.6 %collective-permute-start.14 = (bf16[192,640]{1,0:T(8,128)(2,1)S(1)}, bf16[192,640]{1,0:T(8,128)(2,1)S(1)}, u32[]{:S(2)}, u32[]{:S(2)}) collective-permute-start(bf16[192,640]{1,0:T(8,128)(2,1)S(1)} %stacked.14), channel_id=1, source_target_pairs={{0,128},{8,136},{16,144},{24,152},{32,160},{40,168},{48,176},{56,1... | collective-permute-start | bytes 737288 | tf_op jit(solution)/shard_map/ppermute | solution.py:42
  38.2 1.6 %collective-permute-done.11.refs_9_ = bf16[192,640]{1,0:T(8,128)(2,1)S(1)} collective-permute-done((bf16[192,640]{1,0:T(8,128)(2,1)S(1)}, bf16[192,640]{1,0:T(8,128)(2,1)S(1)}, u32[]{:S(2)}, u32[]{:S(2)}) %collective-permute-start.11) | collective-permute-done | bytes 245792 | tf_op jit(solution)/shard_map/ppermute | solution.py:42
  39.7 3.6 %collective-permute-done.8.refs_6_ = bf16[192,640]{1,0:T(8,128)(2,1)S(1)} collective-permute-done((bf16[192,640]{1,0:T(8,128)(2,1)S(1)}, bf16[192,640]{1,0:T(8,128)(2,1)S(1)}, u32[]{:S(2)}, u32[]{:S(2)}) %collective-permute-start.8) | collective-permute-done | bytes 245792 | tf_op jit(solution)/shard_map/ppermute | solution.py:42
  43.3 0.5 collective-permute-start.15
  43.8 4.7 %attend_part.1 = (f32[768,640]{1,0:T(8,128)S(1)}, f32[768,128]{1,0:T(8,128)S(1)}) custom-call(bf16[384,640]{1,0:T(8,128)(2,1)S(1)} %copy-done.3, bf16[384,640]{1,0:T(8,128)(2,1)S(1)} %collective-permute-done.refs_1_, bf16[192,640]{1,0:T(8,128)(2,1)S(1)} %stacked.9.refs_2_, bf16[192,640]{1,0:T(8,128)(2,1)S(1)} %stacked.11.refs_3_, ...), custom_call_target="tpu_custom_call" | custom-call | flops 1 | bytes 1 | tf_op jit(solution)/shard_map/attend_part/pallas_call | solution.py:50
  48.5 0.5 collective-permute-done.13.refs_13_
  49.1 2.6 %collective-permute-done.14.refs_14_ = bf16[192,640]{1,0:T(8,128)(2,1)S(1)} collective-permute-done((bf16[192,640]{1,0:T(8,128)(2,1)S(1)}, bf16[192,640]{1,0:T(8,128)(2,1)S(1)}, u32[]{:S(2)}, u32[]{:S(2)}) %collective-permute-start.14) | collective-permute-done | bytes 245792 | tf_op jit(solution)/shard_map/ppermute | solution.py:42
  51.7 1.3 %collective-permute-done.15.refs_15_ = bf16[96,640]{1,0:T(8,128)(2,1)S(1)} collective-permute-done((bf16[96,640]{1,0:T(8,128)(2,1)S(1)}, bf16[96,640]{1,0:T(8,128)(2,1)S(1)}, u32[]{:S(2)}, u32[]{:S(2)}) %collective-permute-start.15) | collective-permute-done | bytes 122912 | tf_op jit(solution)/shard_map/ppermute | solution.py:42
  53.0 4.3 %attend_last.2 = (bf16[224,640]{1,0:T(8,128)(2,1)S(1)}, f32[224,128]{1,0:T(8,128)S(1)}, bf16[224,768]{1,0:T(8,128)(2,1)S(1)}) custom-call(bf16[384,640]{1,0:T(8,128)(2,1)S(1)} %copy-done.3, bf16[384,640]{1,0:T(8,128)(2,1)S(1)} %collective-permute-done.refs_1_, f32[768,640]{1,0:T(8,128)S(1)} %get-tuple-element.62.refs_2_, ...), custom_call_target="tpu_custom_call" | custom-call | flops 1 | bytes 1 | tf_op jit(solution)/shard_map/attend_last/pallas_call | solution.py:50
  57.4 0.1 collective-permute-start.16
  57.5 2.9 %attend_last.3 = (bf16[160,640]{1,0:T(8,128)(2,1)S(1)}, f32[160,128]{1,0:T(8,128)S(1)}, bf16[160,768]{1,0:T(8,128)(2,1)S(1)}) custom-call(bf16[384,640]{1,0:T(8,128)(2,1)S(1)} %copy-done.3, bf16[384,640]{1,0:T(8,128)(2,1)S(1)} %collective-permute-done.refs_1_, f32[768,640]{1,0:T(8,128)S(1)} %get-tuple-element.62.refs_2_, ...), custom_call_target="tpu_custom_call" | custom-call | flops 1 | bytes 1 | tf_op jit(solution)/shard_map/attend_last/pallas_call | solution.py:50
  60.4 0.8 collective-permute-start.22
  61.2 1.6 %project_send.2 = (bf16[448,640]{1,0:T(8,128)(2,1)S(1)}, bf16[448,640]{1,0:T(8,128)(2,1)S(1)}, bf16[224,640]{1,0:T(8,128)(2,1)S(1)}) custom-call(s32[1]{0:T(128)} %bitcast.place, bf16[224,640]{1,0:T(8,128)(2,1)S(1)} %get-tuple-element.65.own, f32[224,128]{1,0:T(8,128)S(1)} %get-tuple-element.66.own_log, bf16[224,768]{1,0:T(8,128)(2,1)S(1)} %collective-permute-done.16.got, ...), custom_call_target="tpu_custom_call" | custom-call | flops 1 | bytes 1 | tf_op jit(solution)/shard_map/project_send/pallas_call | solution.py:50
  62.9 1.6 %collective-permute-start.17 = (bf16[448,640]{1,0:T(8,128)(2,1)S(1)}, bf16[448,640]{1,0:T(8,128)(2,1)S(1)}, u32[]{:S(2)}, u32[]{:S(2)}) collective-permute-start(bf16[448,640]{1,0:T(8,128)(2,1)S(1)} %get-tuple-element.69), channel_id=1, source_target_pairs={{0,2},{1,3},{2,4},{3,5},{4,6},{5,7},{6,0},{7,1},{8,10},{9,11},{10,... | collective-permute-start | bytes 1720328 | tf_op jit(solution)/shard_map/ppermute | solution.py:359
  64.4 1.7 %collective-permute-start.18 = (bf16[448,640]{1,0:T(8,128)(2,1)S(1)}, bf16[448,640]{1,0:T(8,128)(2,1)S(1)}, u32[]{:S(2)}, u32[]{:S(2)}) collective-permute-start(bf16[448,640]{1,0:T(8,128)(2,1)S(1)} %get-tuple-element.70), channel_id=1, source_target_pairs={{0,6},{1,7},{2,0},{3,1},{4,2},{5,3},{6,4},{7,5},{8,14},{9,15},{10,... | collective-permute-start | bytes 1720328 | tf_op jit(solution)/shard_map/ppermute | solution.py:360
  66.2 1.3 %project_send.3 = (bf16[640,640]{1,0:T(8,128)(2,1)S(1)}, bf16[160,640]{1,0:T(8,128)(2,1)S(1)}) custom-call(s32[1]{0:T(128)} %bitcast.place, bf16[160,640]{1,0:T(8,128)(2,1)S(1)} %get-tuple-element.73.own, f32[160,128]{1,0:T(8,128)S(1)} %get-tuple-element.74.own_log, bf16[160,768]{1,0:T(8,128)(2,1)S(1)} %collective-permute-done.22.got, ...), custom_call_target="tpu_custom_call" | custom-call | flops 1 | bytes 1 | tf_op jit(solution)/shard_map/project_send/pallas_call | solution.py:50
  67.5 2.4 %collective-permute-start.23 = (bf16[640,640]{1,0:T(8,128)(2,1)S(1)}, bf16[640,640]{1,0:T(8,128)(2,1)S(1)}, u32[]{:S(2)}, u32[]{:S(2)}) collective-permute-start(bf16[640,640]{1,0:T(8,128)(2,1)S(1)} %get-tuple-element.77), channel_id=1, source_target_pairs={{0,1},{1,0},{2,3},{3,2},{4,5},{5,4},{6,7},{7,6},{8,9},{9,8},{10,11... | collective-permute-start | bytes 2457608 | tf_op jit(solution)/shard_map/ppermute | solution.py:42
  69.9 1.2 %project_keep.2.kept = f32[896,640]{1,0:T(8,128)S(1)} custom-call(s32[1]{0:T(128)} %bitcast.place, bf16[224,640]{1,0:T(8,128)(2,1)S(1)} %get-tuple-element.68.att, bf16[640,5120]{1,0:T(8,128)(2,1)S(1)} %bitcast.2), custom_call_target="tpu_custom_call" | custom-call | flops 1 | bytes 1 | tf_op jit(solution)/shard_map/project_keep/pallas_call | solution.py:50
  71.1 8.0 %collective-permute-done.17.got_left = bf16[448,640]{1,0:T(8,128)(2,1)S(1)} collective-permute-done((bf16[448,640]{1,0:T(8,128)(2,1)S(1)}, bf16[448,640]{1,0:T(8,128)(2,1)S(1)}, u32[]{:S(2)}, u32[]{:S(2)}) %collective-permute-start.17) | collective-permute-done | bytes 573472 | tf_op jit(solution)/shard_map/ppermute | solution.py:359
  79.1 0.1 relay.2
  79.2 3.0 %collective-permute-start.20 = (bf16[224,640]{1,0:T(8,128)(2,1)S(1)}, bf16[224,640]{1,0:T(8,128)(2,1)S(1)}, u32[]{:S(2)}, u32[]{:S(2)}) collective-permute-start(bf16[224,640]{1,0:T(8,128)(2,1)S(1)} %get-tuple-element.72), channel_id=1, source_target_pairs={{0,6},{1,7},{2,0},{3,1},{4,2},{5,3},{6,4},{7,5},{8,14},{9,15},{10,... | collective-permute-start | bytes 860168 | tf_op jit(solution)/shard_map/ppermute | solution.py:374
  82.2 1.0 project_keep.3.kept
  83.2 5.5 %collective-permute-done.23.got = bf16[640,640]{1,0:T(8,128)(2,1)S(1)} collective-permute-done((bf16[640,640]{1,0:T(8,128)(2,1)S(1)}, bf16[640,640]{1,0:T(8,128)(2,1)S(1)}, u32[]{:S(2)}, u32[]{:S(2)}) %collective-permute-start.23) | collective-permute-done | bytes 819232 | tf_op jit(solution)/shard_map/ppermute | solution.py:42
  88.7 0.2 spread.1
  88.9 0.4 collective-permute-start.24
  89.2 2.9 %collective-permute-start.25 = (bf16[160,640]{1,0:T(8,128)(2,1)S(1)}, bf16[160,640]{1,0:T(8,128)(2,1)S(1)}, u32[]{:S(2)}, u32[]{:S(2)}) collective-permute-start(bf16[160,640]{1,0:T(8,128)(2,1)S(1)} %get-tuple-element.80), channel_id=1, source_target_pairs={{0,6},{1,7},{2,0},{3,1},{4,2},{5,3},{6,4},{7,5},{8,14},{9,15},{10,... | collective-permute-start | bytes 614408 | tf_op jit(solution)/shard_map/ppermute | solution.py:382
  92.2 0.1 turn.1
  92.3 2.4 %collective-permute-start.21 = (bf16[224,640]{1,0:T(8,128)(2,1)S(1)}, bf16[224,640]{1,0:T(8,128)(2,1)S(1)}, u32[]{:S(2)}, u32[]{:S(2)}) collective-permute-start(bf16[224,640]{1,0:T(8,128)(2,1)S(1)} %turn.1), channel_id=1, source_target_pairs={{0,1},{1,0},{2,3},{3,2},{4,5},{5,4},{6,7},{7,6},{8,9},{9,8},{10,11... | collective-permute-start | bytes 860168 | tf_op jit(solution)/shard_map/ppermute | solution.py:42
  94.7 3.1 %collective-permute-done.24.got_left.left2 = bf16[160,640]{1,0:T(8,128)(2,1)S(1)} collective-permute-done((bf16[160,640]{1,0:T(8,128)(2,1)S(1)}, bf16[160,640]{1,0:T(8,128)(2,1)S(1)}, u32[]{:S(2)}, u32[]{:S(2)}) %collective-permute-start.24) | collective-permute-done | bytes 204832 | tf_op jit(solution)/shard_map/ppermute | solution.py:381
  97.9 0.1 collective-permute-start.26
  98.0 3.2 %collective-permute-start.27 = (bf16[80,640]{1,0:T(8,128)(2,1)S(1)}, bf16[80,640]{1,0:T(8,128)(2,1)S(1)}, u32[]{:S(2)}, u32[]{:S(2)}) collective-permute-start(bf16[80,640]{1,0:T(8,128)(2,1)S(1)} %get-tuple-element.82), channel_id=1, source_target_pairs={{0,6},{1,7},{2,0},{3,1},{4,2},{5,3},{6,4},{7,5},{8,14},{9,15},{10,... | collective-permute-start | bytes 307208 | tf_op jit(solution)/shard_map/ppermute | solution.py:390
  101.2 1.9 %collective-permute-done.19.on_right = bf16[224,640]{1,0:T(8,128)(2,1)S(1)} collective-permute-done((bf16[224,640]{1,0:T(8,128)(2,1)S(1)}, bf16[224,640]{1,0:T(8,128)(2,1)S(1)}, u32[]{:S(2)}, u32[]{:S(2)}) %collective-permute-start.19) | collective-permute-done | bytes 286752 | tf_op jit(solution)/shard_map/ppermute | solution.py:373
  103.2 1.1 %collective-permute-done.26.on_right2 = bf16[80,640]{1,0:T(8,128)(2,1)S(1)} collective-permute-done((bf16[80,640]{1,0:T(8,128)(2,1)S(1)}, bf16[80,640]{1,0:T(8,128)(2,1)S(1)}, u32[]{:S(2)}, u32[]{:S(2)}) %collective-permute-start.26) | collective-permute-done | bytes 102432 | tf_op jit(solution)/shard_map/ppermute | solution.py:389
  104.3 1.0 last.1
  (29 shorter events, 0.1 us)
Async XLA Ops:
  0.0 21.0 %copy-start.1 = (bf16[384,640]{1,0:T(8,128)(2,1)S(1)}, bf16[384,640]{1,0:T(8,128)(2,1)}, u32[]{:S(2)}) copy-start(bf16[384,640]{1,0:T(8,128)(2,1)} %refs_0_.7) | copy-start | bytes 1474564
  0.0 33.0 %collective-permute-start = (bf16[384,640]{1,0:T(8,128)(2,1)}, bf16[384,640]{1,0:T(8,128)(2,1)S(1)}, u32[]{:S(2)}, u32[]{:S(2)}) collective-permute-start(bf16[384,640]{1,0:T(8,128)(2,1)} %refs_0_.10), channel_id=1, source_target_pairs={{0,8},{8,0},{16,24},{24,16},{32,40},{40,32},{48,56},{56,48},{64,72... | collective-permute-start | bytes 1474568 | tf_op jit(solution)/shard_map/ppermute | solution.py:42
  0.0 0.9 copy-start.4
  0.9 0.8 copy-start.5
  1.9 9.9 %collective-permute-start.5 = (bf16[96,640]{1,0:T(8,128)(2,1)S(1)}, bf16[96,640]{1,0:T(8,128)(2,1)S(1)}, u32[]{:S(2)}, u32[]{:S(2)}) collective-permute-start(bf16[96,640]{1,0:T(8,128)(2,1)S(1)} %stacked.8.refs_0_.refs_4_), channel_id=1, source_target_pairs={{0,112},{8,120},{16,32},{24,40},{32,16},{40,24},{48,64},{56,72},{6... | collective-permute-start | bytes 368648 | tf_op jit(solution)/shard_map/ppermute | solution.py:320
  7.8 5.4 %collective-permute-start.1 = (bf16[96,640]{1,0:T(8,128)(2,1)S(1)}, bf16[96,640]{1,0:T(8,128)(2,1)S(1)}, u32[]{:S(2)}, u32[]{:S(2)}) collective-permute-start(bf16[96,640]{1,0:T(8,128)(2,1)S(1)} %stacked.8.refs_0_.refs_4_), channel_id=1, source_target_pairs={{0,16},{8,24},{16,0},{24,8},{32,48},{40,56},{48,32},{56,40},{64,80... | collective-permute-start | bytes 368648 | tf_op jit(solution)/shard_map/ppermute | solution.py:42
  11.8 6.0 %collective-permute-start.6 = (bf16[96,640]{1,0:T(8,128)(2,1)S(1)}, bf16[96,640]{1,0:T(8,128)(2,1)S(1)}, u32[]{:S(2)}, u32[]{:S(2)}) collective-permute-start(bf16[96,640]{1,0:T(8,128)(2,1)S(1)} %collective-permute-done.5.refs_2_.refs_8_), channel_id=1, source_target_pairs={{0,16},{8,24},{16,0},{24,8},{32,48},{40,56},{48,32},{56,40},{64,80... | collective-permute-start | bytes 368648 | tf_op jit(solution)/shard_map/ppermute | solution.py:42
  13.2 7.5 %collective-permute-start.2 = (bf16[96,640]{1,0:T(8,128)(2,1)S(1)}, bf16[96,640]{1,0:T(8,128)(2,1)S(1)}, u32[]{:S(2)}, u32[]{:S(2)}) collective-permute-start(bf16[96,640]{1,0:T(8,128)(2,1)S(1)} %collective-permute-done.1.refs_1_.refs_5_), channel_id=1, source_target_pairs={{0,112},{8,120},{16,32},{24,40},{32,16},{40,24},{48,64},{56,72},{6... | collective-permute-start | bytes 368648 | tf_op jit(solution)/shard_map/ppermute | solution.py:337
  15.2 1.0 copy-start
  16.2 1.0 copy-start.2
  17.6 26.2 %copy-start.3 = (bf16[384,640]{1,0:T(8,128)(2,1)S(1)}, bf16[384,640]{1,0:T(8,128)(2,1)}, u32[]{:S(2)}) copy-start(bf16[384,640]{1,0:T(8,128)(2,1)} %refs_0_.10) | copy-start | bytes 1474564
  17.6 15.8 %collective-permute-start.9 = (bf16[192,640]{1,0:T(8,128)(2,1)S(1)}, bf16[192,640]{1,0:T(8,128)(2,1)S(1)}, u32[]{:S(2)}, u32[]{:S(2)}) collective-permute-start(bf16[192,640]{1,0:T(8,128)(2,1)S(1)} %stacked.11.refs_3_), channel_id=1, source_target_pairs={{0,16},{8,24},{16,0},{24,8},{32,48},{40,56},{48,32},{56,40},{64,80... | collective-permute-start | bytes 737288 | tf_op jit(solution)/shard_map/ppermute | solution.py:42
  17.7 6.1 %collective-permute-start.7 = (bf16[96,640]{1,0:T(8,128)(2,1)S(1)}, bf16[96,640]{1,0:T(8,128)(2,1)S(1)}, u32[]{:S(2)}, u32[]{:S(2)}) collective-permute-start(bf16[96,640]{1,0:T(8,128)(2,1)S(1)} %collective-permute-done.6.refs_0_.refs_6_), channel_id=1, source_target_pairs={{0,112},{8,120},{16,32},{24,40},{32,16},{40,24},{48,64},{56,72},{6... | collective-permute-start | bytes 368648 | tf_op jit(solution)/shard_map/ppermute | solution.py:337
  20.7 8.5 %collective-permute-start.3 = (bf16[96,640]{1,0:T(8,128)(2,1)S(1)}, bf16[96,640]{1,0:T(8,128)(2,1)S(1)}, u32[]{:S(2)}, u32[]{:S(2)}) collective-permute-start(bf16[96,640]{1,0:T(8,128)(2,1)S(1)} %collective-permute-done.2.refs_1_.refs_9_), channel_id=1, source_target_pairs={{0,16},{8,24},{16,0},{24,8},{32,48},{40,56},{48,32},{56,40},{64,80... | collective-permute-start | bytes 368648 | tf_op jit(solution)/shard_map/ppermute | solution.py:42
  21.4 15.2 %collective-permute-start.10 = (bf16[192,640]{1,0:T(8,128)(2,1)S(1)}, bf16[192,640]{1,0:T(8,128)(2,1)S(1)}, u32[]{:S(2)}, u32[]{:S(2)}) collective-permute-start(bf16[192,640]{1,0:T(8,128)(2,1)S(1)} %stacked.13.refs_4_), channel_id=1, source_target_pairs={{0,16},{8,24},{16,0},{24,8},{32,48},{40,56},{48,32},{56,40},{64,80... | collective-permute-start | bytes 737288 | tf_op jit(solution)/shard_map/ppermute | solution.py:42
  29.9 9.9 %collective-permute-start.11 = (bf16[192,640]{1,0:T(8,128)(2,1)S(1)}, bf16[192,640]{1,0:T(8,128)(2,1)S(1)}, u32[]{:S(2)}, u32[]{:S(2)}) collective-permute-start(bf16[192,640]{1,0:T(8,128)(2,1)S(1)} %stacked.15.refs_5_), channel_id=1, source_target_pairs={{0,16},{8,24},{16,0},{24,8},{32,48},{40,56},{48,32},{56,40},{64,80... | collective-permute-start | bytes 737288 | tf_op jit(solution)/shard_map/ppermute | solution.py:42
  30.0 6.1 %collective-permute-start.4 = (bf16[96,640]{1,0:T(8,128)(2,1)S(1)}, bf16[96,640]{1,0:T(8,128)(2,1)S(1)}, u32[]{:S(2)}, u32[]{:S(2)}) collective-permute-start(bf16[96,640]{1,0:T(8,128)(2,1)S(1)} %collective-permute-done.3.refs_0_.refs_7_), channel_id=1, source_target_pairs={{0,112},{8,120},{16,32},{24,40},{32,16},{40,24},{48,64},{56,72},{6... | collective-permute-start | bytes 368648 | tf_op jit(solution)/shard_map/ppermute | solution.py:337
  33.3 10.1 %collective-permute-start.8 = (bf16[192,640]{1,0:T(8,128)(2,1)S(1)}, bf16[192,640]{1,0:T(8,128)(2,1)S(1)}, u32[]{:S(2)}, u32[]{:S(2)}) collective-permute-start(bf16[192,640]{1,0:T(8,128)(2,1)S(1)} %stacked.9.refs_2_), channel_id=1, source_target_pairs={{0,16},{8,24},{16,0},{24,8},{32,48},{40,56},{48,32},{56,40},{64,80... | collective-permute-start | bytes 737288 | tf_op jit(solution)/shard_map/ppermute | solution.py:42
  33.4 15.7 %collective-permute-start.12 = (bf16[288,640]{1,0:T(8,128)(2,1)S(1)}, bf16[288,640]{1,0:T(8,128)(2,1)S(1)}, u32[]{:S(2)}, u32[]{:S(2)}) collective-permute-start(bf16[288,640]{1,0:T(8,128)(2,1)S(1)} %stacked.10), channel_id=1, source_target_pairs={{0,128},{8,136},{16,144},{24,152},{32,160},{40,168},{48,176},{56,1... | collective-permute-start | bytes 1105928 | tf_op jit(solution)/shard_map/ppermute | solution.py:42
  36.1 12.9 %collective-permute-start.13 = (bf16[192,640]{1,0:T(8,128)(2,1)S(1)}, bf16[192,640]{1,0:T(8,128)(2,1)S(1)}, u32[]{:S(2)}, u32[]{:S(2)}) collective-permute-start(bf16[192,640]{1,0:T(8,128)(2,1)S(1)} %stacked.12), channel_id=1, source_target_pairs={{0,128},{8,136},{16,144},{24,152},{32,160},{40,168},{48,176},{56,1... | collective-permute-start | bytes 737288 | tf_op jit(solution)/shard_map/ppermute | solution.py:42
  36.6 15.1 %collective-permute-start.14 = (bf16[192,640]{1,0:T(8,128)(2,1)S(1)}, bf16[192,640]{1,0:T(8,128)(2,1)S(1)}, u32[]{:S(2)}, u32[]{:S(2)}) collective-permute-start(bf16[192,640]{1,0:T(8,128)(2,1)S(1)} %stacked.14), channel_id=1, source_target_pairs={{0,128},{8,136},{16,144},{24,152},{32,160},{40,168},{48,176},{56,1... | collective-permute-start | bytes 737288 | tf_op jit(solution)/shard_map/ppermute | solution.py:42
  43.3 9.7 %collective-permute-start.15 = (bf16[96,640]{1,0:T(8,128)(2,1)S(1)}, bf16[96,640]{1,0:T(8,128)(2,1)S(1)}, u32[]{:S(2)}, u32[]{:S(2)}) collective-permute-start(bf16[96,640]{1,0:T(8,128)(2,1)S(1)} %collective-permute-done.4.refs_11_), channel_id=1, source_target_pairs={{0,128},{8,136},{16,144},{24,152},{32,160},{40,168},{48,176},{56,1... | collective-permute-start | bytes 368648 | tf_op jit(solution)/shard_map/ppermute | solution.py:42
  43.8 17.4 %slice-start = ((s8[6553600]{0:T(1024)(128)(4,1)}), s8[4194304]{0:T(1024)(128)(4,1)S(1)}, s32[]{:S(2)}) async-start(s8[6553600]{0:T(1024)(128)(4,1)} %bitcast.1), calls=%async_computation | async-start | bytes 8388608
  53.0 8.2 %slice-start.1 = ((s8[6553600]{0:T(1024)(128)(4,1)}), s8[2359296]{0:T(1024)(128)(4,1)S(1)}, s32[]{:S(2)}) async-start(s8[6553600]{0:T(1024)(128)(4,1)} %bitcast.1), calls=%async_computation.1 | async-start | bytes 4718592
  57.4 3.8 %collective-permute-start.16 = (bf16[224,768]{1,0:T(8,128)(2,1)S(1)}, bf16[224,768]{1,0:T(8,128)(2,1)S(1)}, u32[]{:S(2)}, u32[]{:S(2)}) collective-permute-start(bf16[224,768]{1,0:T(8,128)(2,1)S(1)} %get-tuple-element.67), channel_id=1, source_target_pairs={{0,8},{8,0},{16,24},{24,16},{32,40},{40,32},{48,56},{56,48},{64,72... | collective-permute-start | bytes 1032200 | tf_op jit(solution)/shard_map/ppermute | solution.py:42
  60.4 5.8 %collective-permute-start.22 = (bf16[160,768]{1,0:T(8,128)(2,1)S(1)}, bf16[160,768]{1,0:T(8,128)(2,1)S(1)}, u32[]{:S(2)}, u32[]{:S(2)}) collective-permute-start(bf16[160,768]{1,0:T(8,128)(2,1)S(1)} %get-tuple-element.75), channel_id=1, source_target_pairs={{0,8},{8,0},{16,24},{24,16},{32,40},{40,32},{48,56},{56,48},{64,72... | collective-permute-start | bytes 737288 | tf_op jit(solution)/shard_map/ppermute | solution.py:42
  62.9 16.2 %collective-permute-start.17 = (bf16[448,640]{1,0:T(8,128)(2,1)S(1)}, bf16[448,640]{1,0:T(8,128)(2,1)S(1)}, u32[]{:S(2)}, u32[]{:S(2)}) collective-permute-start(bf16[448,640]{1,0:T(8,128)(2,1)S(1)} %get-tuple-element.69), channel_id=1, source_target_pairs={{0,2},{1,3},{2,4},{3,5},{4,6},{5,7},{6,0},{7,1},{8,10},{9,11},{10,... | collective-permute-start | bytes 1720328 | tf_op jit(solution)/shard_map/ppermute | solution.py:359
  64.4 14.6 %collective-permute-start.18 = (bf16[448,640]{1,0:T(8,128)(2,1)S(1)}, bf16[448,640]{1,0:T(8,128)(2,1)S(1)}, u32[]{:S(2)}, u32[]{:S(2)}) collective-permute-start(bf16[448,640]{1,0:T(8,128)(2,1)S(1)} %get-tuple-element.70), channel_id=1, source_target_pairs={{0,6},{1,7},{2,0},{3,1},{4,2},{5,3},{6,4},{7,5},{8,14},{9,15},{10,... | collective-permute-start | bytes 1720328 | tf_op jit(solution)/shard_map/ppermute | solution.py:360
  67.5 21.2 %collective-permute-start.23 = (bf16[640,640]{1,0:T(8,128)(2,1)S(1)}, bf16[640,640]{1,0:T(8,128)(2,1)S(1)}, u32[]{:S(2)}, u32[]{:S(2)}) collective-permute-start(bf16[640,640]{1,0:T(8,128)(2,1)S(1)} %get-tuple-element.77), channel_id=1, source_target_pairs={{0,1},{1,0},{2,3},{3,2},{4,5},{5,4},{6,7},{7,6},{8,9},{9,8},{10,11... | collective-permute-start | bytes 2457608 | tf_op jit(solution)/shard_map/ppermute | solution.py:42
  79.2 13.0 %collective-permute-start.20 = (bf16[224,640]{1,0:T(8,128)(2,1)S(1)}, bf16[224,640]{1,0:T(8,128)(2,1)S(1)}, u32[]{:S(2)}, u32[]{:S(2)}) collective-permute-start(bf16[224,640]{1,0:T(8,128)(2,1)S(1)} %get-tuple-element.72), channel_id=1, source_target_pairs={{0,6},{1,7},{2,0},{3,1},{4,2},{5,3},{6,4},{7,5},{8,14},{9,15},{10,... | collective-permute-start | bytes 860168 | tf_op jit(solution)/shard_map/ppermute | solution.py:374
  88.9 9.0 %collective-permute-start.24 = (bf16[160,640]{1,0:T(8,128)(2,1)S(1)}, bf16[160,640]{1,0:T(8,128)(2,1)S(1)}, u32[]{:S(2)}, u32[]{:S(2)}) collective-permute-start(bf16[160,640]{1,0:T(8,128)(2,1)S(1)} %get-tuple-element.79), channel_id=1, source_target_pairs={{0,2},{1,3},{2,4},{3,5},{4,6},{5,7},{6,0},{7,1},{8,10},{9,11},{10,... | collective-permute-start | bytes 614408 | tf_op jit(solution)/shard_map/ppermute | solution.py:381
  89.2 8.6 %collective-permute-start.25 = (bf16[160,640]{1,0:T(8,128)(2,1)S(1)}, bf16[160,640]{1,0:T(8,128)(2,1)S(1)}, u32[]{:S(2)}, u32[]{:S(2)}) collective-permute-start(bf16[160,640]{1,0:T(8,128)(2,1)S(1)} %get-tuple-element.80), channel_id=1, source_target_pairs={{0,6},{1,7},{2,0},{3,1},{4,2},{5,3},{6,4},{7,5},{8,14},{9,15},{10,... | collective-permute-start | bytes 614408 | tf_op jit(solution)/shard_map/ppermute | solution.py:382
  92.2 11.0 %collective-permute-start.19 = (bf16[224,640]{1,0:T(8,128)(2,1)S(1)}, bf16[224,640]{1,0:T(8,128)(2,1)S(1)}, u32[]{:S(2)}, u32[]{:S(2)}) collective-permute-start(bf16[224,640]{1,0:T(8,128)(2,1)S(1)} %get-tuple-element.71), channel_id=1, source_target_pairs={{0,2},{1,3},{2,4},{3,5},{4,6},{5,7},{6,0},{7,1},{8,10},{9,11},{10,... | collective-permute-start | bytes 860168 | tf_op jit(solution)/shard_map/ppermute | solution.py:373
  92.3 12.0 %collective-permute-start.21 = (bf16[224,640]{1,0:T(8,128)(2,1)S(1)}, bf16[224,640]{1,0:T(8,128)(2,1)S(1)}, u32[]{:S(2)}, u32[]{:S(2)}) collective-permute-start(bf16[224,640]{1,0:T(8,128)(2,1)S(1)} %turn.1), channel_id=1, source_target_pairs={{0,1},{1,0},{2,3},{3,2},{4,5},{5,4},{6,7},{7,6},{8,9},{9,8},{10,11... | collective-permute-start | bytes 860168 | tf_op jit(solution)/shard_map/ppermute | solution.py:42
  97.9 6.3 %collective-permute-start.26 = (bf16[80,640]{1,0:T(8,128)(2,1)S(1)}, bf16[80,640]{1,0:T(8,128)(2,1)S(1)}, u32[]{:S(2)}, u32[]{:S(2)}) collective-permute-start(bf16[80,640]{1,0:T(8,128)(2,1)S(1)} %get-tuple-element.81), channel_id=1, source_target_pairs={{0,2},{1,3},{2,4},{3,5},{4,6},{5,7},{6,0},{7,1},{8,10},{9,11},{10,... | collective-permute-start | bytes 307208 | tf_op jit(solution)/shard_map/ppermute | solution.py:389
  98.0 6.3 %collective-permute-start.27 = (bf16[80,640]{1,0:T(8,128)(2,1)S(1)}, bf16[80,640]{1,0:T(8,128)(2,1)S(1)}, u32[]{:S(2)}, u32[]{:S(2)}) collective-permute-start(bf16[80,640]{1,0:T(8,128)(2,1)S(1)} %get-tuple-element.82), channel_id=1, source_target_pairs={{0,6},{1,7},{2,0},{3,1},{4,2},{5,3},{6,4},{7,5},{8,14},{9,15},{10,... | collective-permute-start | bytes 307208 | tf_op jit(solution)/shard_map/ppermute | solution.py:390

commit v3 on v2

--- a/solution.py
+++ b/solution.py
@@ -17,8 +17,8 @@
 VMEM_LIMIT = 20 << 20
 IN_VMEM = pl.BlockSpec(memory_space=pltpu.VMEM)
 CUT = 224
-CHUNKS = 4
 LITTLE = pl.CostEstimate(flops=1, bytes_accessed=1, transcendentals=0)
+AFTER_STARTS = pl.CostEstimate(flops=20_000_000_000, bytes_accessed=1, transcendentals=0)
 
 
 def seq_place(i):
@@ -34,6 +34,10 @@
     return pairs
 
 
+def between_frames_across():
+    return [(i, to ^ 2 * Z) for i, to in between_frames()]
+
+
 def along_x(step):
     return [(i, (i // 2 + step) % X * 2 + i % 2) for i in range(2 * X)]
 
@@ -46,7 +50,7 @@
     return pltpu.with_memory_space_constraint(array, pltpu.VMEM)
 
 
-def local(kernel, outs, *ins, scalars=(), scratch=(), name="local"):
+def local(kernel, outs, *ins, scalars=(), scratch=(), cost=LITTLE, name="local"):
     return pl.pallas_call(
         kernel,
         in_specs=[pl.BlockSpec(memory_space=pltpu.SMEM)] * len(scalars) + [IN_VMEM] * len(ins),
@@ -54,40 +58,38 @@
         out_shape=[pltpu.VMEM(shape, dtype) for shape, dtype in outs],
         scratch_shapes=list(scratch),
         compiler_params=pltpu.CompilerParams(vmem_limit_bytes=VMEM_LIMIT),
-        cost_estimate=LITTLE,
+        cost_estimate=cost,
         name=name,
     )(*scalars, *(held(a) for a in ins))
 
 
-def stack_kernel(parts, *refs):
-    ins, out, sems = refs[:-2], refs[-2], refs[-1]
+def stack_kernel(parts, n_ins, *refs):
+    ins, outs, sems = refs[:n_ins], refs[n_ins:-1], refs[-1]
     copies = []
-    at = 0
-    for number, (place, low, high) in enumerate(parts):
-        rows = high - low
-        copies.append(
-            pltpu.make_async_copy(
-                ins[place].at[low:high, :], out.at[at : at + rows, :], sems.at[number]
-            )
-        )
-        at += rows
+    for out, out_parts in zip(outs, parts):
+        at = 0
+        for place, low, high in out_parts:
+            to = out.at[at : at + high - low, :]
+            sem = sems.at[len(copies)]
+            copies.append(pltpu.make_async_copy(ins[place].at[low:high, :], to, sem))
+            at += high - low
     for copy in copies:
         copy.start()
     for copy in copies:
         copy.wait()
 
 
-def stacked(*arrays, parts=None):
-    parts = parts or tuple((n, 0, a.shape[0]) for n, a in enumerate(arrays))
-    rows = sum(high - low for _, low, high in parts)
+def stacked(arrays, parts=None, cost=LITTLE):
+    parts = parts or (tuple((n, 0, a.shape[0]) for n, a in enumerate(arrays)),)
+    width, dtype = arrays[0].shape[1], arrays[0].dtype
     return pl.pallas_call(
-        functools.partial(stack_kernel, parts),
+        functools.partial(stack_kernel, parts, len(arrays)),
         in_specs=[pl.BlockSpec(memory_space=pl.ANY)] * len(arrays),
-        out_specs=IN_VMEM,
-        out_shape=pltpu.VMEM((rows, arrays[0].shape[1]), arrays[0].dtype),
-        scratch_shapes=[pltpu.SemaphoreType.DMA((len(parts),))],
+        out_specs=[IN_VMEM] * len(parts),
+        out_shape=[pltpu.VMEM((sum(h - l for _, l, h in part), width), dtype) for part in parts],
+        scratch_shapes=[pltpu.SemaphoreType.DMA((sum(len(part) for part in parts),))],
         compiler_params=pltpu.CompilerParams(vmem_limit_bytes=VMEM_LIMIT),
-        cost_estimate=LITTLE,
+        cost_estimate=cost,
         name="stacked",
     )(*arrays)
 
@@ -116,7 +118,6 @@
     else:
         (part_ref, log_ref, key_ref, value_ref, query_ref) = refs
     rows = high - low
-    whole_rows = queries[0].shape[0]
     heads = queries[0].shape[1] // HD
     for head in range(heads):
         columns = slice(head * HD, (head + 1) * HD)
@@ -133,13 +134,12 @@
         for place in range(2):
             part = slice(place * rows, (place + 1) * rows)
             if with_state:
-                held_rows = slice(place * whole_rows + low, place * whole_rows + high)
-                log = before_log[held_rows, head : head + 1]
+                log = before_log[part, head : head + 1]
                 top = jnp.maximum(log, peak[part])
                 before_factor = jnp.exp2(log - top)
                 factor = jnp.exp2(peak[part] - top)
                 whole = before_factor + total[part] * factor
-                result = (before[held_rows, columns] * before_factor + summed[part] * factor) / whole
+                result = (before[part, columns] * before_factor + summed[part] * factor) / whole
             else:
                 top = peak[part]
                 whole = total[part]
@@ -186,6 +186,7 @@
             pltpu.VMEM((2, 2 * rows, HD), BF16),
         ]
         + [pltpu.VMEM((2 * rows, HD), F32)] * last,
+        cost=LITTLE if last else AFTER_STARTS,
         name="attend_last" if last else "attend_part",
     )
 
@@ -226,7 +227,7 @@
     products(blocks, place, outs[-1], weight, outs[:-1])
 
 
-def project_send(blocks, place, own, own_log, got, weight, n_outs):
+def project_send(blocks, place, own, own_log, got, weight, n_outs, cost=LITTLE):
     rows, width = own.shape
     count = len(blocks)
     outs = [((count // n_outs * rows, width), BF16)] * n_outs + [((rows, width), BF16)]
@@ -238,6 +239,7 @@
         got,
         weight,
         scalars=(place,),
+        cost=cost,
         name="project_send",
     )
 
@@ -260,51 +262,43 @@
 
 
 def relay_kernel(kept, got_left, got_right, to_right, to_left):
-    n = to_right.shape[0]
-    to_right[...] = (kept[:n, :] + got_left[:n, :].astype(F32)).astype(BF16)
-    to_left[...] = (kept[n : 2 * n, :] + got_right[:n, :].astype(F32)).astype(BF16)
-
-
-def turn_kernel(kept, got_left, on_left, out):
+    n = got_left.shape[0]
+    to_right[:n, :] = (kept[:n, :] + got_left[...].astype(F32)).astype(BF16)
+    to_right[n:, :] = kept[n : 2 * n, :].astype(BF16)
+    to_left[:n, :] = (kept[2 * n : 3 * n, :] + got_right[...].astype(F32)).astype(BF16)
+    to_left[n:, :] = kept[3 * n : 4 * n, :].astype(BF16)
+
+
+def turn_kernel(kept, on_right, on_left, out):
     n = out.shape[0]
     out[...] = (
-        kept[3 * n :, :] + on_left[...].astype(F32) + got_left[n:, :].astype(F32)
+        kept[5 * n :, :] + on_left[:n, :].astype(F32) + on_right[n:, :].astype(F32)
     ).astype(BF16)
 
 
-def spread_kernel(kept, got, to_right, to_left, rest):
-    m = to_right.shape[0]
-    q = m // 2
-
-    def total(block, low, high):
-        rows = slice(block * m + low, block * m + high)
-        return kept[rows, :] + got[rows, :].astype(F32)
-
-    to_right[:q, :] = total(0, 0, q).astype(BF16)
-    to_right[q:, :] = total(1, q, m).astype(BF16)
-    to_left[:q, :] = total(0, q, m).astype(BF16)
-    to_left[q:, :] = total(2, 0, q).astype(BF16)
-    rest[:q, :] = total(1, 0, q)
-    rest[q:m, :] = total(2, q, m)
-    rest[m:, :] = total(3, 0, m)
-
-
-def last_kernel(kept, on_right, got_right, mine, rest, on_right2, on_left2, left2, right2, out):
-    n = on_right.shape[0]
-    m = left2.shape[0]
-    q = m // 2
+def spread_kernel(kept, got, *outs):
+    m = outs[0].shape[0]
+    for number, out in enumerate(outs):
+        rows = slice(number * m, (number + 1) * m)
+        out[...] = (kept[rows, :] + got[rows, :].astype(F32)).astype(out.dtype)
+
+
+def total_kernel(first, *refs):
+    total = first[...]
+    for other in refs[:-1]:
+        total = total + other[...].astype(F32)
+    refs[-1][...] = total.astype(BF16)
+
+
+def last_kernel(kept, on_right, on_left, mine, above, out):
+    n = mine.shape[0]
     out[:n, :] = (
-        kept[2 * n : 3 * n, :]
-        + on_right[...].astype(F32)
-        + got_right[n:, :].astype(F32)
+        kept[4 * n : 5 * n, :]
+        + on_right[:n, :].astype(F32)
+        + on_left[n:, :].astype(F32)
         + mine[...].astype(F32)
     ).astype(BF16)
-    out[n : n + q, :] = (
-        rest[m : m + q, :] + on_right2[...].astype(F32) + right2[q:, :].astype(F32)
-    ).astype(BF16)
-    out[n + q :, :] = (
-        rest[m + q :, :] + on_left2[...].astype(F32) + left2[q:, :].astype(F32)
-    ).astype(BF16)
+    out[n:, :] = above[...]
 
 
 def body(queries, keys, values, ref_keys, ref_values, out_weight):
@@ -314,92 +308,103 @@
     right_x, left_x = along_x(1), along_x(-1)
     place = lax.axis_index("head").reshape(1)
     place, ref_keys = lax.optimization_barrier((place, ref_keys))
-
-    own = stacked(ref_keys, ref_values)
+    keys, values, ref_keys, ref_values = (
+        pltpu.with_memory_space_constraint(a, pltpu.HBM) for a in (keys, values, ref_keys, ref_values)
+    )
+
+    (own,) = stacked((ref_keys, ref_values))
     inner = [swap(own, "seq", 2)]
     outer = [lax.ppermute(own, "seq", between)]
     other_queries = swap(queries, "seq", 1)
-    frame, other_frame, across = [], [], []
-
-    def exchange_chunk(number, after):
-        part = rows // CHUNKS
-        low, high = number * part, (number + 1) * part
-        held_back, _ = lax.optimization_barrier(((keys, values), after))
-        chunk = stacked(*held_back, parts=((0, low, high), (1, low, high)))
-        frame.append(chunk)
-        other_frame.append(swap(chunk, "seq", 2))
-
-    exchange_chunk(0, other_queries)
+    (keys, values), own = lax.optimization_barrier(((keys, values), own))
+    parts = (rows // 4, rows // 4, rows // 2)
+    lows = (0, rows // 4, rows // 2)
+    frame = list(stacked(
+        (keys, values),
+        tuple(
+            ((0, low, low + part), (1, low, low + part)) for low, part in zip(lows, parts)
+        ),
+    ))
+    other_frame, across = [swap(frame[0], "seq", 2)], []
     for step in range(3):
         came_inner, came_outer = inner[-1], outer[-1]
+        if step:
+            came_inner, came_outer, other_frame[step - 1], other_queries = lax.optimization_barrier(
+                (came_inner, came_outer, other_frame[step - 1], other_queries)
+            )
         if step < 2:
             inner.append(swap(came_outer, "seq", 2))
         outer.append(lax.ppermute(came_inner, "seq", between))
-        packed = stacked(*([own] * (step == 0)), came_inner, came_outer)
-        exchange_chunk(step + 1, packed)
+        if step == 2:
+            far_across = lax.ppermute(came_inner, "seq", between_frames_across())
+        (packed,) = stacked([own] * (step == 0) + [came_inner, came_outer], cost=AFTER_STARTS)
+        if step < 2:
+            packed, frame[step + 1] = lax.optimization_barrier((packed, frame[step + 1]))
+            other_frame.append(swap(frame[step + 1], "seq", 2))
         across.append(swap(packed, "seq", 2 * Z))
-    far, frame, other_frame = lax.optimization_barrier((outer[-1], frame, other_frame))
-    across.append(swap(far, "seq", 2 * Z))
-    state = attend(
-        queries, other_queries, 0, rows, (rows // CHUNKS,) * (2 * CHUNKS), (*frame, *other_frame)
-    )
-    pieces = (own, *inner, *outer[:-1], far, *across)
-    halves = (half,) * len(pieces)
-
-    def finish(low, high):
+
+    early = (own, *inner[:2], *outer[:2], across[0])
+
+    def attend_early(low, high):
+        return attend(
+            queries,
+            other_queries,
+            low,
+            high,
+            parts + parts[:2] + (half,) * len(early),
+            (*frame, *other_frame[:2], *early),
+        )
+
+    state = attend_early(0, CUT)
+    last_state = attend_early(CUT, rows)
+    state, last_state = lax.optimization_barrier((state, last_state))
+    pieces = (inner[2], *outer[2:], far_across, *across[1:], *other_frame[2:])
+    halves = (half,) * (len(pieces) - 1) + parts[2:]
+
+    def finish(low, high, state):
         own_part, own_log, other_part = attend(
             queries, other_queries, low, high, halves, pieces, state, True
         )
         return own_part, own_log, swap(other_part, "seq", 1)
 
-    done = finish(0, CUT)
-    go_right, go_left, att = project_send(
-        ((2, 0), (1, 1), (2, 1), (3, 0)), place, *done, out_weight, 2
-    )
+    done = finish(0, CUT, state)
+    go_right, go_left, att = project_send(((2, 0), (2, 1)), place, *done, out_weight, 2)
+
+    last_done = finish(CUT, rows, last_state)
+    last_done, go_right, go_left = lax.optimization_barrier((last_done, go_right, go_left))
     got_left = lax.ppermute(go_right, "head", right_x)
     got_right = lax.ppermute(go_left, "head", left_x)
-
-    last_done = finish(CUT, rows)
     go_across, last_att = project_send(
-        ((2, 1), (1, 1), (3, 1), (0, 1)), place, *last_done, out_weight, 1
+        ((2, 1), (1, 1), (3, 1), (0, 1)), place, *last_done, out_weight, 1, AFTER_STARTS
     )
     got_across = swap(go_across, "head", 1)
 
-    kept = project_keep(((1, 0), (3, 1), (0, 0), (0, 1)), place, att, out_weight)
-    last_kept = project_keep(((2, 0), (1, 0), (3, 0), (0, 0)), place, last_att, out_weight)
-
-    one = ((CUT, width), BF16)
-    to_right, to_left = local(relay_kernel, [one, one], kept, got_left, got_right, name="relay")
+    att, last_att = lax.optimization_barrier((att, last_att))
+    kept = project_keep(
+        ((1, 0), (1, 1), (3, 1), (3, 0), (0, 0), (0, 1)), place, att, out_weight
+    )
+    last_kept = project_keep(
+        ((2, 0), (1, 0), (3, 0), (0, 0)), place, last_att, out_weight
+    )
+
+    two = ((2 * CUT, width), BF16)
+    to_right, to_left = local(relay_kernel, [two, two], kept, got_left, got_right, name="relay")
     on_right = lax.ppermute(to_right, "head", right_x)
     on_left = lax.ppermute(to_left, "head", left_x)
 
-    m = rows - CUT
-    two = ((m, width), BF16)
-    last_right, last_left, rest = local(
-        spread_kernel, [two, two, ((2 * m, width), F32)], last_kept, got_across, name="spread"
-    )
-    left2 = lax.ppermute(last_right, "head", right_x)
-    right2 = lax.ppermute(last_left, "head", left_x)
-
-    (turned,) = local(turn_kernel, [one], kept, got_left, on_left, name="turn")
+    part = (rows - CUT, width)
+    *spread, rest = local(
+        spread_kernel, [(part, BF16)] * 3 + [(part, F32)], last_kept, got_across, name="spread"
+    )
+    on_left, on_right, spread, rest = lax.optimization_barrier((on_left, on_right, spread, rest))
+    others = [lax.ppermute(a, "head", along_x(step)) for a, step in zip(spread, (2, 1, X - 1))]
+    (turned,) = local(
+        turn_kernel, [((CUT, width), BF16)], kept, on_right, on_left, cost=AFTER_STARTS, name="turn"
+    )
     mine_got = swap(turned, "head", 1)
-
-    small = ((m // 2, width), BF16)
-    to_right2, to_left2 = local(relay_kernel, [small, small], rest, left2, right2, name="relay")
-    on_right2 = lax.ppermute(to_right2, "head", right_x)
-    on_left2 = lax.ppermute(to_left2, "head", left_x)
+    (above,) = local(total_kernel, [(part, BF16)], rest, *others, cost=AFTER_STARTS, name="total")
     return local_out(
-        last_kernel,
-        ((rows, width), BF16),
-        kept,
-        on_right,
-        got_right,
-        mine_got,
-        rest,
-        on_right2,
-        on_left2,
-        left2,
-        right2,
+        last_kernel, ((rows, width), BF16), kept, on_right, on_left, mine_got, above
     )
 
 

time: 106 us -> 91.3 us (0.86)
  waiting for transfers between devices: 42.7 us -> 34 us
  starting transfers between devices: 37.5 us -> 33.1 us
  local copies, waits for them, and re-layouts: 3.78 us -> 0.02 us
  Pallas kernels: 21.1 us -> 23.9 us
    ppermute x1, waiting for transfers between devices: 7.96 us -> 1.55 us  [body(): got_left = lax.ppermute(go_right, 'head', right_x)]
    ppermute x3, starting transfers between devices: 7.41 us -> 2.03 us  [body(): outer.append(lax.ppermute(came_inner, 'seq', between))]
    ppermute x1, waiting for transfers between devices: 3.93 us -> 0.01 us  [body(): outer = [lax.ppermute(own, 'seq', between)]]
    unnamed x16 -> x6, local copies, waits for them, and re-layouts: 3.78 us -> 0.02 us
    ppermute x16 -> x14, waiting for transfers between devices: 22 us -> 25.1 us  [swap(): lax.ppermute(value, axis, [(i, i ^ bit) for i in range(lax.axis_size(axis...]
    ppermute x3, waiting for transfers between devices: 2.59 us -> 0.01 us  [body(): outer.append(lax.ppermute(came_inner, 'seq', between))]
    ppermute x16 -> x14, starting transfers between devices: 11.2 us -> 13.4 us  [swap(): lax.ppermute(value, axis, [(i, i ^ bit) for i in range(lax.axis_size(axis...]
    pallas_call x11 -> x12, Pallas kernels: 17.5 us -> 19.6 us  [local(): pl.pallas_call(kernel, in_specs=[pl.BlockSpec(memory_space=pltpu.SMEM)] *...]
  transfers between devices with their start and end apart: 28 -> 26, of which waited for: 15 -> 11; matrix products, arithmetic and copies ran while one was open for 0% -> 0% of each run, Pallas kernels for 15% -> 20%
where the time goes in v3:
time: 91.3 us; the launch traced here: 91.1 us
  waiting for transfers between devices  34 us (37%)
  starting transfers between devices  33.1 us (36%)
  Pallas kernels  23.9 us (26%)
    ppermute x14, waiting for transfers between devices, swap(): lax.ppermute(value, axis, [(i, i ^ bit) for i in range(lax.axis_size(axis...  25.1 us
    pallas_call x12, Pallas kernels, local(): pl.pallas_call(kernel, in_specs=[pl.BlockSpec(memory_space=pltpu.SMEM)] *...  19.6 us
    ppermute x14, starting transfers between devices, swap(): lax.ppermute(value, axis, [(i, i ^ bit) for i in range(lax.axis_size(axis...  13.4 us
    ppermute x1, starting transfers between devices, body(): outer = [lax.ppermute(own, 'seq', between)]  5.94 us
    ppermute x3, waiting for transfers between devices, body(): lax.ppermute(a, 'head', along_x(step))  5.09 us
    pallas_call x5, Pallas kernels, stacked(): pl.pallas_call(functools.partial(stack_kernel, parts, len(arrays)), in_sp...  3.31 us
    ppermute x3, starting transfers between devices, body(): lax.ppermute(a, 'head', along_x(step))  3.24 us
    ppermute x1, starting transfers between devices, body(): on_left = lax.ppermute(to_left, 'head', left_x)  3.03 us
  transfers between devices with their start and end apart: 26, of which 11 were waited for; matrix products, arithmetic and copies ran while one was open for 0% of the time, Pallas kernels for 20%

profile of v3, /device:TPU:8, one launch (start us, length us, event | category | flops | bytes accessed | tf_op | source)
XLA Modules:
  0.0 91.1 jit_solution(4820461638107965629)
XLA Ops:
  0.0 0.9 stacked.5.refs_0_.refs_7_
  0.9 5.9 %collective-permute-start = (bf16[96,640]{1,0:T(8,128)(2,1)S(1)}, bf16[96,640]{1,0:T(8,128)(2,1)S(1)}, u32[]{:S(2)}, u32[]{:S(2)}) collective-permute-start(bf16[96,640]{1,0:T(8,128)(2,1)S(1)} %stacked.5.refs_0_.refs_7_), channel_id=1, source_target_pairs={{0,112},{8,120},{16,32},{24,40},{32,16},{40,24},{48,64},{56,72},{6... | collective-permute-start | bytes 368648 | tf_op jit(solution)/shard_map/ppermute | solution.py:317
  6.8 0.0 collective-permute-start.2
  6.8 1.4 %stacked.6 = (bf16[192,640]{1,0:T(8,128)(2,1)S(1)}, bf16[192,640]{1,0:T(8,128)(2,1)S(1)}, bf16[384,640]{1,0:T(8,128)(2,1)S(1)}) custom-call(bf16[384,640]{1,0:T(8,128)(2,1)} %refs_0_.5, bf16[384,640]{1,0:T(8,128)(2,1)} %refs_1_.2), custom_call_target="tpu_custom_call" | custom-call | flops 1 | bytes 1 | tf_op jit(solution)/shard_map/stacked/pallas_call | solution.py:85
  8.2 2.1 %collective-permute-start.4 = (bf16[192,640]{1,0:T(8,128)(2,1)S(1)}, bf16[192,640]{1,0:T(8,128)(2,1)S(1)}, u32[]{:S(2)}, u32[]{:S(2)}) collective-permute-start(bf16[192,640]{1,0:T(8,128)(2,1)S(1)} %get-tuple-element.67.refs_2_), channel_id=1, source_target_pairs={{0,16},{8,24},{16,0},{24,8},{32,48},{40,56},{48,32},{56,40},{64,80... | collective-permute-start | bytes 737288 | tf_op jit(solution)/shard_map/ppermute | solution.py:46
  10.3 0.0 collective-permute-start.5
  10.3 0.0 collective-permute-done.refs_2_.refs_10_
  10.3 0.2 collective-permute-start.1
  10.5 2.5 %collective-permute-done.2.refs_1_.refs_8_ = bf16[96,640]{1,0:T(8,128)(2,1)S(1)} collective-permute-done((bf16[96,640]{1,0:T(8,128)(2,1)S(1)}, bf16[96,640]{1,0:T(8,128)(2,1)S(1)}, u32[]{:S(2)}, u32[]{:S(2)}) %collective-permute-start.2) | collective-permute-done | bytes 122912 | tf_op jit(solution)/shard_map/ppermute | solution.py:46
  13.0 0.1 collective-permute-start.3
  13.1 0.5 stacked.7
  13.6 0.5 collective-permute-start.8
  14.1 4.2 %collective-permute-done.4.refs_5_ = bf16[192,640]{1,0:T(8,128)(2,1)S(1)} collective-permute-done((bf16[192,640]{1,0:T(8,128)(2,1)S(1)}, bf16[192,640]{1,0:T(8,128)(2,1)S(1)}, u32[]{:S(2)}, u32[]{:S(2)}) %collective-permute-start.4) | collective-permute-done | bytes 245792 | tf_op jit(solution)/shard_map/ppermute | solution.py:46
  18.2 0.4 collective-permute-start.9
  18.7 2.2 %collective-permute-done.1.refs_0_.refs_9_ = bf16[96,640]{1,0:T(8,128)(2,1)S(1)} collective-permute-done((bf16[96,640]{1,0:T(8,128)(2,1)S(1)}, bf16[96,640]{1,0:T(8,128)(2,1)S(1)}, u32[]{:S(2)}, u32[]{:S(2)}) %collective-permute-start.1) | collective-permute-done | bytes 122912 | tf_op jit(solution)/shard_map/ppermute | solution.py:46
  20.9 0.0 collective-permute-done.3.refs_1_.refs_11_
  20.9 0.0 collective-permute-done.5.refs_1_
  20.9 1.0 %collective-permute-start.6 = (bf16[96,640]{1,0:T(8,128)(2,1)S(1)}, bf16[96,640]{1,0:T(8,128)(2,1)S(1)}, u32[]{:S(2)}, u32[]{:S(2)}) collective-permute-start(bf16[96,640]{1,0:T(8,128)(2,1)S(1)} %collective-permute-done.3.refs_1_.refs_11_), channel_id=1, source_target_pairs={{0,16},{8,24},{16,0},{24,8},{32,48},{40,56},{48,32},{56,40},{64,80... | collective-permute-start | bytes 368648 | tf_op jit(solution)/shard_map/ppermute | solution.py:46
  21.8 1.0 %collective-permute-start.7 = (bf16[96,640]{1,0:T(8,128)(2,1)S(1)}, bf16[96,640]{1,0:T(8,128)(2,1)S(1)}, u32[]{:S(2)}, u32[]{:S(2)}) collective-permute-start(bf16[96,640]{1,0:T(8,128)(2,1)S(1)} %collective-permute-done.1.refs_0_.refs_9_), channel_id=1, source_target_pairs={{0,112},{8,120},{16,32},{24,40},{32,16},{40,24},{48,64},{56,72},{6... | collective-permute-start | bytes 368648 | tf_op jit(solution)/shard_map/ppermute | solution.py:337
  22.8 0.3 stacked.8
  23.1 0.0 copy-start
  23.1 1.2 %collective-permute-start.14 = (bf16[384,640]{1,0:T(8,128)(2,1)S(1)}, bf16[384,640]{1,0:T(8,128)(2,1)S(1)}, u32[]{:S(2)}, u32[]{:S(2)}) collective-permute-start(bf16[384,640]{1,0:T(8,128)(2,1)S(1)} %get-tuple-element.76.refs_4_), channel_id=1, source_target_pairs={{0,16},{8,24},{16,0},{24,8},{32,48},{40,56},{48,32},{56,40},{64,80... | collective-permute-start | bytes 1474568 | tf_op jit(solution)/shard_map/ppermute | solution.py:46
  24.3 1.8 %collective-permute-done.8.refs_6_ = bf16[192,640]{1,0:T(8,128)(2,1)S(1)} collective-permute-done((bf16[192,640]{1,0:T(8,128)(2,1)S(1)}, bf16[192,640]{1,0:T(8,128)(2,1)S(1)}, u32[]{:S(2)}, u32[]{:S(2)}) %collective-permute-start.8) | collective-permute-done | bytes 245792 | tf_op jit(solution)/shard_map/ppermute | solution.py:46
  26.1 0.4 collective-permute-start.12
  26.6 2.2 %collective-permute-done.6.refs_0_.refs_4_ = bf16[96,640]{1,0:T(8,128)(2,1)S(1)} collective-permute-done((bf16[96,640]{1,0:T(8,128)(2,1)S(1)}, bf16[96,640]{1,0:T(8,128)(2,1)S(1)}, u32[]{:S(2)}, u32[]{:S(2)}) %collective-permute-start.6) | collective-permute-done | bytes 122912 | tf_op jit(solution)/shard_map/ppermute | solution.py:46
  28.8 0.0 collective-permute-done.7.refs_1_.refs_5_
  28.8 0.9 %collective-permute-start.10 = (bf16[96,640]{1,0:T(8,128)(2,1)S(1)}, bf16[96,640]{1,0:T(8,128)(2,1)S(1)}, u32[]{:S(2)}, u32[]{:S(2)}) collective-permute-start(bf16[96,640]{1,0:T(8,128)(2,1)S(1)} %collective-permute-done.6.refs_0_.refs_4_), channel_id=1, source_target_pairs={{0,112},{8,120},{16,32},{24,40},{32,16},{40,24},{48,64},{56,72},{6... | collective-permute-start | bytes 368648 | tf_op jit(solution)/shard_map/ppermute | solution.py:337
  29.7 2.2 %collective-permute-start.11 = (bf16[96,640]{1,0:T(8,128)(2,1)S(1)}, bf16[96,640]{1,0:T(8,128)(2,1)S(1)}, u32[]{:S(2)}, u32[]{:S(2)}) collective-permute-start(bf16[96,640]{1,0:T(8,128)(2,1)S(1)} %collective-permute-done.6.refs_0_.refs_4_), channel_id=1, source_target_pairs={{0,240},{8,248},{16,160},{24,168},{32,144},{40,152},{48,192},{56,2... | collective-permute-start | bytes 368648 | tf_op jit(solution)/shard_map/ppermute | solution.py:339
  31.9 0.3 stacked.9
  32.2 0.0 collective-permute-done.9.refs_12_
  32.2 1.8 %collective-permute-start.13 = (bf16[192,640]{1,0:T(8,128)(2,1)S(1)}, bf16[192,640]{1,0:T(8,128)(2,1)S(1)}, u32[]{:S(2)}, u32[]{:S(2)}) collective-permute-start(bf16[192,640]{1,0:T(8,128)(2,1)S(1)} %stacked.9), channel_id=1, source_target_pairs={{0,128},{8,136},{16,144},{24,152},{32,160},{40,168},{48,176},{56,1... | collective-permute-start | bytes 737288 | tf_op jit(solution)/shard_map/ppermute | solution.py:46
  34.1 3.1 %attend_part.3 = (f32[320,640]{1,0:T(8,128)S(1)}, f32[320,128]{1,0:T(8,128)S(1)}) custom-call(bf16[384,640]{1,0:T(8,128)(2,1)S(1)} %copy-done, bf16[384,640]{1,0:T(8,128)(2,1)S(1)} %collective-permute-done.5.refs_1_, bf16[192,640]{1,0:T(8,128)(2,1)S(1)} %get-tuple-element.67.refs_2_, bf16[192,640]{1,0:T(8,128)(2,1)S(1)} %get-tuple-element.72.refs_3_, ...), custom_call_target="tpu_custom_call" | custom-call | flops 20000000000 | bytes 1 | tf_op jit(solution)/shard_map/attend_part/pallas_call | solution.py:54
  37.2 0.0 slice-start.1
  37.2 4.0 %attend_part.2 = (f32[448,640]{1,0:T(8,128)S(1)}, f32[448,128]{1,0:T(8,128)S(1)}) custom-call(bf16[384,640]{1,0:T(8,128)(2,1)S(1)} %copy-done, bf16[384,640]{1,0:T(8,128)(2,1)S(1)} %collective-permute-done.5.refs_1_, bf16[192,640]{1,0:T(8,128)(2,1)S(1)} %get-tuple-element.67.refs_2_, bf16[192,640]{1,0:T(8,128)(2,1)S(1)} %get-tuple-element.72.refs_3_, ...), custom_call_target="tpu_custom_call" | custom-call | flops 20000000000 | bytes 1 | tf_op jit(solution)/shard_map/attend_part/pallas_call | solution.py:54
  41.2 0.0 collective-permute-done.12.refs_8_
  41.3 3.7 %attend_last.2 = (bf16[224,640]{1,0:T(8,128)(2,1)S(1)}, f32[224,128]{1,0:T(8,128)S(1)}, bf16[224,768]{1,0:T(8,128)(2,1)S(1)}) custom-call(bf16[384,640]{1,0:T(8,128)(2,1)S(1)} %copy-done, bf16[384,640]{1,0:T(8,128)(2,1)S(1)} %collective-permute-done.5.refs_1_, f32[448,640]{1,0:T(8,128)S(1)} %get-tuple-element.84.refs_2_, ...), custom_call_target="tpu_custom_call" | custom-call | flops 1 | bytes 1 | tf_op jit(solution)/shard_map/attend_last/pallas_call | solution.py:54
  45.0 0.3 collective-permute-start.15
  45.3 3.1 %attend_last.3 = (bf16[160,640]{1,0:T(8,128)(2,1)S(1)}, f32[160,128]{1,0:T(8,128)S(1)}, bf16[160,768]{1,0:T(8,128)(2,1)S(1)}) custom-call(bf16[384,640]{1,0:T(8,128)(2,1)S(1)} %copy-done, bf16[384,640]{1,0:T(8,128)(2,1)S(1)} %collective-permute-done.5.refs_1_, f32[320,640]{1,0:T(8,128)S(1)} %get-tuple-element.93.refs_2_, ...), custom_call_target="tpu_custom_call" | custom-call | flops 1 | bytes 1 | tf_op jit(solution)/shard_map/attend_last/pallas_call | solution.py:54
  48.4 0.6 collective-permute-start.16
  49.0 1.1 %project_send.2 = (bf16[224,640]{1,0:T(8,128)(2,1)S(1)}, bf16[224,640]{1,0:T(8,128)(2,1)S(1)}, bf16[224,640]{1,0:T(8,128)(2,1)S(1)}) custom-call(s32[1]{0:T(128)} %bitcast.place, bf16[224,640]{1,0:T(8,128)(2,1)S(1)} %get-tuple-element.89.own, f32[224,128]{1,0:T(8,128)S(1)} %get-tuple-element.90.own_log, bf16[224,768]{1,0:T(8,128)(2,1)S(1)} %collective-permute-done.15.got, ...), custom_call_target="tpu_custom_call" | custom-call | flops 1 | bytes 1 | tf_op jit(solution)/shard_map/project_send/pallas_call | solution.py:54
  50.1 1.6 %collective-permute-start.17 = (bf16[224,640]{1,0:T(8,128)(2,1)S(1)}, bf16[224,640]{1,0:T(8,128)(2,1)S(1)}, u32[]{:S(2)}, u32[]{:S(2)}) collective-permute-start(bf16[224,640]{1,0:T(8,128)(2,1)S(1)} %get-tuple-element.105), channel_id=1, source_target_pairs={{0,2},{1,3},{2,4},{3,5},{4,6},{5,7},{6,0},{7,1},{8,10},{9,11},{10,... | collective-permute-start | bytes 860168 | tf_op jit(solution)/shard_map/ppermute | solution.py:375
  51.7 1.8 %collective-permute-start.18 = (bf16[224,640]{1,0:T(8,128)(2,1)S(1)}, bf16[224,640]{1,0:T(8,128)(2,1)S(1)}, u32[]{:S(2)}, u32[]{:S(2)}) collective-permute-start(bf16[224,640]{1,0:T(8,128)(2,1)S(1)} %get-tuple-element.106), channel_id=1, source_target_pairs={{0,6},{1,7},{2,0},{3,1},{4,2},{5,3},{6,4},{7,5},{8,14},{9,15},{10,... | collective-permute-start | bytes 860168 | tf_op jit(solution)/shard_map/ppermute | solution.py:376
  53.5 1.3 %project_send.3 = (bf16[640,640]{1,0:T(8,128)(2,1)S(1)}, bf16[160,640]{1,0:T(8,128)(2,1)S(1)}) custom-call(s32[1]{0:T(128)} %bitcast.place, bf16[160,640]{1,0:T(8,128)(2,1)S(1)} %get-tuple-element.100.own, f32[160,128]{1,0:T(8,128)S(1)} %get-tuple-element.101.own_log, bf16[160,768]{1,0:T(8,128)(2,1)S(1)} %collective-permute-done.16.got, ...), custom_call_target="tpu_custom_call" | custom-call | flops 20000000000 | bytes 1 | tf_op jit(solution)/shard_map/project_send/pallas_call | solution.py:54
  54.8 2.4 %collective-permute-start.21 = (bf16[640,640]{1,0:T(8,128)(2,1)S(1)}, bf16[640,640]{1,0:T(8,128)(2,1)S(1)}, u32[]{:S(2)}, u32[]{:S(2)}) collective-permute-start(bf16[640,640]{1,0:T(8,128)(2,1)S(1)} %get-tuple-element.110), channel_id=1, source_target_pairs={{0,1},{1,0},{2,3},{3,2},{4,5},{5,4},{6,7},{7,6},{8,9},{9,8},{10,11... | collective-permute-start | bytes 2457608 | tf_op jit(solution)/shard_map/ppermute | solution.py:46
  57.1 1.7 %project_keep.2.kept = f32[1344,640]{1,0:T(8,128)S(1)} custom-call(s32[1]{0:T(128)} %bitcast.place, bf16[224,640]{1,0:T(8,128)(2,1)S(1)} %get-tuple-element.104.att, bf16[640,5120]{1,0:T(8,128)(2,1)S(1)} %bitcast.2), custom_call_target="tpu_custom_call" | custom-call | flops 1 | bytes 1 | tf_op jit(solution)/shard_map/project_keep/pallas_call | solution.py:54
  58.9 1.6 %collective-permute-done.17.got_left = bf16[224,640]{1,0:T(8,128)(2,1)S(1)} collective-permute-done((bf16[224,640]{1,0:T(8,128)(2,1)S(1)}, bf16[224,640]{1,0:T(8,128)(2,1)S(1)}, u32[]{:S(2)}, u32[]{:S(2)}) %collective-permute-start.17) | collective-permute-done | bytes 286752 | tf_op jit(solution)/shard_map/ppermute | solution.py:375
  60.4 0.2 relay.1
  60.6 3.0 %collective-permute-start.19 = (bf16[448,640]{1,0:T(8,128)(2,1)S(1)}, bf16[448,640]{1,0:T(8,128)(2,1)S(1)}, u32[]{:S(2)}, u32[]{:S(2)}) collective-permute-start(bf16[448,640]{1,0:T(8,128)(2,1)S(1)} %get-tuple-element.107), channel_id=1, source_target_pairs={{0,6},{1,7},{2,0},{3,1},{4,2},{5,3},{6,4},{7,5},{8,14},{9,15},{10,... | collective-permute-start | bytes 1720328 | tf_op jit(solution)/shard_map/ppermute | solution.py:393
  63.7 0.0 collective-permute-start.20
  63.7 1.0 %project_keep.3.kept = f32[640,640]{1,0:T(8,128)S(1)} custom-call(s32[1]{0:T(128)} %bitcast.place, bf16[160,640]{1,0:T(8,128)(2,1)S(1)} %get-tuple-element.109.att, bf16[640,5120]{1,0:T(8,128)(2,1)S(1)} %bitcast.2), custom_call_target="tpu_custom_call" | custom-call | flops 1 | bytes 1 | tf_op jit(solution)/shard_map/project_keep/pallas_call | solution.py:54
  64.6 11.6 %collective-permute-done.21.got = bf16[640,640]{1,0:T(8,128)(2,1)S(1)} collective-permute-done((bf16[640,640]{1,0:T(8,128)(2,1)S(1)}, bf16[640,640]{1,0:T(8,128)(2,1)S(1)}, u32[]{:S(2)}, u32[]{:S(2)}) %collective-permute-start.21) | collective-permute-done | bytes 819232 | tf_op jit(solution)/shard_map/ppermute | solution.py:46
  76.2 0.2 spread.1
  76.4 0.0 collective-permute-done.19.on_left
  76.4 2.2 %collective-permute-done.20.on_right = bf16[448,640]{1,0:T(8,128)(2,1)S(1)} collective-permute-done((bf16[448,640]{1,0:T(8,128)(2,1)S(1)}, bf16[448,640]{1,0:T(8,128)(2,1)S(1)}, u32[]{:S(2)}, u32[]{:S(2)}) %collective-permute-start.20) | collective-permute-done | bytes 573472 | tf_op jit(solution)/shard_map/ppermute | solution.py:392
  78.6 1.1 %collective-permute-start.24 = (bf16[160,640]{1,0:T(8,128)(2,1)S(1)}, bf16[160,640]{1,0:T(8,128)(2,1)S(1)}, u32[]{:S(2)}, u32[]{:S(2)}) collective-permute-start(bf16[160,640]{1,0:T(8,128)(2,1)S(1)} %get-tuple-element.119), channel_id=1, source_target_pairs={{0,2},{1,3},{2,4},{3,5},{4,6},{5,7},{6,0},{7,1},{8,10},{9,11},{10,... | collective-permute-start | bytes 614408 | tf_op jit(solution)/shard_map/ppermute | solution.py:400
  79.8 2.1 %collective-permute-start.25 = (bf16[160,640]{1,0:T(8,128)(2,1)S(1)}, bf16[160,640]{1,0:T(8,128)(2,1)S(1)}, u32[]{:S(2)}, u32[]{:S(2)}) collective-permute-start(bf16[160,640]{1,0:T(8,128)(2,1)S(1)} %get-tuple-element.120), channel_id=1, source_target_pairs={{0,6},{1,7},{2,0},{3,1},{4,2},{5,3},{6,4},{7,5},{8,14},{9,15},{10,... | collective-permute-start | bytes 614408 | tf_op jit(solution)/shard_map/ppermute | solution.py:400
  81.9 0.1 turn.1
  82.0 2.4 %collective-permute-start.22 = (bf16[224,640]{1,0:T(8,128)(2,1)S(1)}, bf16[224,640]{1,0:T(8,128)(2,1)S(1)}, u32[]{:S(2)}, u32[]{:S(2)}) collective-permute-start(bf16[224,640]{1,0:T(8,128)(2,1)S(1)} %turn.1), channel_id=1, source_target_pairs={{0,1},{1,0},{2,3},{3,2},{4,5},{5,4},{6,7},{7,6},{8,9},{9,8},{10,11... | collective-permute-start | bytes 860168 | tf_op jit(solution)/shard_map/ppermute | solution.py:46
  84.4 3.0 %collective-permute-done.23.refs_0_ = bf16[160,640]{1,0:T(8,128)(2,1)S(1)} collective-permute-done((bf16[160,640]{1,0:T(8,128)(2,1)S(1)}, bf16[160,640]{1,0:T(8,128)(2,1)S(1)}, u32[]{:S(2)}, u32[]{:S(2)}) %collective-permute-start.23) | collective-permute-done | bytes 204832 | tf_op jit(solution)/shard_map/ppermute | solution.py:400
  87.4 2.1 %collective-permute-done.24.refs_1_ = bf16[160,640]{1,0:T(8,128)(2,1)S(1)} collective-permute-done((bf16[160,640]{1,0:T(8,128)(2,1)S(1)}, bf16[160,640]{1,0:T(8,128)(2,1)S(1)}, u32[]{:S(2)}, u32[]{:S(2)}) %collective-permute-start.24) | collective-permute-done | bytes 204832 | tf_op jit(solution)/shard_map/ppermute | solution.py:400
  89.4 0.0 collective-permute-done.25.refs_2_
  89.4 0.1 total.1.above
  89.5 0.7 collective-permute-done.22.mine
  90.2 0.9 %last.1 = bf16[384,640]{1,0:T(8,128)(2,1)} custom-call(f32[1344,640]{1,0:T(8,128)S(1)} %project_keep.2.kept, bf16[448,640]{1,0:T(8,128)(2,1)S(1)} %collective-permute-done.20.on_right, bf16[448,640]{1,0:T(8,128)(2,1)S(1)} %collective-permute-done.19.on_left, bf16[224,640]{1,0:T(8,128)(2,1)S(1)} %collective-permute-done.22.mine, bf16[160,640]{1,0:T(8,128)(2,1)S(1)} %total.1.above), custom_call_target="tpu_custom_call" | custom-call | flops 1 | bytes 1 | tf_op jit(solution)/shard_map/last/pallas_call | solution.py:412
  (13 shorter events, 0.0 us)
Async XLA Ops:
  0.9 9.4 %collective-permute-start = (bf16[96,640]{1,0:T(8,128)(2,1)S(1)}, bf16[96,640]{1,0:T(8,128)(2,1)S(1)}, u32[]{:S(2)}, u32[]{:S(2)}) collective-permute-start(bf16[96,640]{1,0:T(8,128)(2,1)S(1)} %stacked.5.refs_0_.refs_7_), channel_id=1, source_target_pairs={{0,112},{8,120},{16,32},{24,40},{32,16},{40,24},{48,64},{56,72},{6... | collective-permute-start | bytes 368648 | tf_op jit(solution)/shard_map/ppermute | solution.py:317
  6.8 6.2 %collective-permute-start.2 = (bf16[96,640]{1,0:T(8,128)(2,1)S(1)}, bf16[96,640]{1,0:T(8,128)(2,1)S(1)}, u32[]{:S(2)}, u32[]{:S(2)}) collective-permute-start(bf16[96,640]{1,0:T(8,128)(2,1)S(1)} %stacked.5.refs_0_.refs_7_), channel_id=1, source_target_pairs={{0,16},{8,24},{16,0},{24,8},{32,48},{40,56},{48,32},{56,40},{64,80... | collective-permute-start | bytes 368648 | tf_op jit(solution)/shard_map/ppermute | solution.py:46
  8.2 10.1 %collective-permute-start.4 = (bf16[192,640]{1,0:T(8,128)(2,1)S(1)}, bf16[192,640]{1,0:T(8,128)(2,1)S(1)}, u32[]{:S(2)}, u32[]{:S(2)}) collective-permute-start(bf16[192,640]{1,0:T(8,128)(2,1)S(1)} %get-tuple-element.67.refs_2_), channel_id=1, source_target_pairs={{0,16},{8,24},{16,0},{24,8},{32,48},{40,56},{48,32},{56,40},{64,80... | collective-permute-start | bytes 737288 | tf_op jit(solution)/shard_map/ppermute | solution.py:46
  10.3 10.6 %collective-permute-start.5 = (bf16[384,640]{1,0:T(8,128)(2,1)}, bf16[384,640]{1,0:T(8,128)(2,1)S(1)}, u32[]{:S(2)}, u32[]{:S(2)}) collective-permute-start(bf16[384,640]{1,0:T(8,128)(2,1)} %refs_0_.9), channel_id=1, source_target_pairs={{0,8},{8,0},{16,24},{24,16},{32,40},{40,32},{48,56},{56,48},{64,72... | collective-permute-start | bytes 1474568 | tf_op jit(solution)/shard_map/ppermute | solution.py:46
  10.3 10.6 %collective-permute-start.1 = (bf16[96,640]{1,0:T(8,128)(2,1)S(1)}, bf16[96,640]{1,0:T(8,128)(2,1)S(1)}, u32[]{:S(2)}, u32[]{:S(2)}) collective-permute-start(bf16[96,640]{1,0:T(8,128)(2,1)S(1)} %collective-permute-done.refs_2_.refs_10_), channel_id=1, source_target_pairs={{0,16},{8,24},{16,0},{24,8},{32,48},{40,56},{48,32},{56,40},{64,80... | collective-permute-start | bytes 368648 | tf_op jit(solution)/shard_map/ppermute | solution.py:46
  13.0 7.9 %collective-permute-start.3 = (bf16[96,640]{1,0:T(8,128)(2,1)S(1)}, bf16[96,640]{1,0:T(8,128)(2,1)S(1)}, u32[]{:S(2)}, u32[]{:S(2)}) collective-permute-start(bf16[96,640]{1,0:T(8,128)(2,1)S(1)} %collective-permute-done.2.refs_1_.refs_8_), channel_id=1, source_target_pairs={{0,112},{8,120},{16,32},{24,40},{32,16},{40,24},{48,64},{56,72},{6... | collective-permute-start | bytes 368648 | tf_op jit(solution)/shard_map/ppermute | solution.py:337
  13.6 12.6 %collective-permute-start.8 = (bf16[192,640]{1,0:T(8,128)(2,1)S(1)}, bf16[192,640]{1,0:T(8,128)(2,1)S(1)}, u32[]{:S(2)}, u32[]{:S(2)}) collective-permute-start(bf16[192,640]{1,0:T(8,128)(2,1)S(1)} %get-tuple-element.72.refs_3_), channel_id=1, source_target_pairs={{0,16},{8,24},{16,0},{24,8},{32,48},{40,56},{48,32},{56,40},{64,80... | collective-permute-start | bytes 737288 | tf_op jit(solution)/shard_map/ppermute | solution.py:46
  18.2 14.0 %collective-permute-start.9 = (bf16[288,640]{1,0:T(8,128)(2,1)S(1)}, bf16[288,640]{1,0:T(8,128)(2,1)S(1)}, u32[]{:S(2)}, u32[]{:S(2)}) collective-permute-start(bf16[288,640]{1,0:T(8,128)(2,1)S(1)} %stacked.7), channel_id=1, source_target_pairs={{0,128},{8,136},{16,144},{24,152},{32,160},{40,168},{48,176},{56,1... | collective-permute-start | bytes 1105928 | tf_op jit(solution)/shard_map/ppermute | solution.py:46
  20.9 7.9 %collective-permute-start.6 = (bf16[96,640]{1,0:T(8,128)(2,1)S(1)}, bf16[96,640]{1,0:T(8,128)(2,1)S(1)}, u32[]{:S(2)}, u32[]{:S(2)}) collective-permute-start(bf16[96,640]{1,0:T(8,128)(2,1)S(1)} %collective-permute-done.3.refs_1_.refs_11_), channel_id=1, source_target_pairs={{0,16},{8,24},{16,0},{24,8},{32,48},{40,56},{48,32},{56,40},{64,80... | collective-permute-start | bytes 368648 | tf_op jit(solution)/shard_map/ppermute | solution.py:46
  21.8 6.9 %collective-permute-start.7 = (bf16[96,640]{1,0:T(8,128)(2,1)S(1)}, bf16[96,640]{1,0:T(8,128)(2,1)S(1)}, u32[]{:S(2)}, u32[]{:S(2)}) collective-permute-start(bf16[96,640]{1,0:T(8,128)(2,1)S(1)} %collective-permute-done.1.refs_0_.refs_9_), channel_id=1, source_target_pairs={{0,112},{8,120},{16,32},{24,40},{32,16},{40,24},{48,64},{56,72},{6... | collective-permute-start | bytes 368648 | tf_op jit(solution)/shard_map/ppermute | solution.py:337
  23.1 11.0 %copy-start = (bf16[384,640]{1,0:T(8,128)(2,1)S(1)}, bf16[384,640]{1,0:T(8,128)(2,1)}, u32[]{:S(2)}) copy-start(bf16[384,640]{1,0:T(8,128)(2,1)} %refs_0_.9) | copy-start | bytes 1474564
  23.1 18.1 %collective-permute-start.14 = (bf16[384,640]{1,0:T(8,128)(2,1)S(1)}, bf16[384,640]{1,0:T(8,128)(2,1)S(1)}, u32[]{:S(2)}, u32[]{:S(2)}) collective-permute-start(bf16[384,640]{1,0:T(8,128)(2,1)S(1)} %get-tuple-element.76.refs_4_), channel_id=1, source_target_pairs={{0,16},{8,24},{16,0},{24,8},{32,48},{40,56},{48,32},{56,40},{64,80... | collective-permute-start | bytes 1474568 | tf_op jit(solution)/shard_map/ppermute | solution.py:46
  26.1 15.1 %collective-permute-start.12 = (bf16[192,640]{1,0:T(8,128)(2,1)S(1)}, bf16[192,640]{1,0:T(8,128)(2,1)S(1)}, u32[]{:S(2)}, u32[]{:S(2)}) collective-permute-start(bf16[192,640]{1,0:T(8,128)(2,1)S(1)} %stacked.8), channel_id=1, source_target_pairs={{0,128},{8,136},{16,144},{24,152},{32,160},{40,168},{48,176},{56,1... | collective-permute-start | bytes 737288 | tf_op jit(solution)/shard_map/ppermute | solution.py:46
  28.8 12.4 %collective-permute-start.10 = (bf16[96,640]{1,0:T(8,128)(2,1)S(1)}, bf16[96,640]{1,0:T(8,128)(2,1)S(1)}, u32[]{:S(2)}, u32[]{:S(2)}) collective-permute-start(bf16[96,640]{1,0:T(8,128)(2,1)S(1)} %collective-permute-done.6.refs_0_.refs_4_), channel_id=1, source_target_pairs={{0,112},{8,120},{16,32},{24,40},{32,16},{40,24},{48,64},{56,72},{6... | collective-permute-start | bytes 368648 | tf_op jit(solution)/shard_map/ppermute | solution.py:337
  29.7 11.5 %collective-permute-start.11 = (bf16[96,640]{1,0:T(8,128)(2,1)S(1)}, bf16[96,640]{1,0:T(8,128)(2,1)S(1)}, u32[]{:S(2)}, u32[]{:S(2)}) collective-permute-start(bf16[96,640]{1,0:T(8,128)(2,1)S(1)} %collective-permute-done.6.refs_0_.refs_4_), channel_id=1, source_target_pairs={{0,240},{8,248},{16,160},{24,168},{32,144},{40,152},{48,192},{56,2... | collective-permute-start | bytes 368648 | tf_op jit(solution)/shard_map/ppermute | solution.py:339
  32.2 9.0 %collective-permute-start.13 = (bf16[192,640]{1,0:T(8,128)(2,1)S(1)}, bf16[192,640]{1,0:T(8,128)(2,1)S(1)}, u32[]{:S(2)}, u32[]{:S(2)}) collective-permute-start(bf16[192,640]{1,0:T(8,128)(2,1)S(1)} %stacked.9), channel_id=1, source_target_pairs={{0,128},{8,136},{16,144},{24,152},{32,160},{40,168},{48,176},{56,1... | collective-permute-start | bytes 737288 | tf_op jit(solution)/shard_map/ppermute | solution.py:46
  34.1 14.9 %slice-start = ((s8[6553600]{0:T(1024)(128)(4,1)}), s8[4194304]{0:T(1024)(128)(4,1)S(1)}, s32[]{:S(2)}) async-start(s8[6553600]{0:T(1024)(128)(4,1)} %bitcast.1), calls=%async_computation | async-start | bytes 8388608
  37.2 11.8 %slice-start.1 = ((s8[6553600]{0:T(1024)(128)(4,1)}), s8[2359296]{0:T(1024)(128)(4,1)S(1)}, s32[]{:S(2)}) async-start(s8[6553600]{0:T(1024)(128)(4,1)} %bitcast.1), calls=%async_computation.1 | async-start | bytes 4718592
  45.0 4.0 %collective-permute-start.15 = (bf16[224,768]{1,0:T(8,128)(2,1)S(1)}, bf16[224,768]{1,0:T(8,128)(2,1)S(1)}, u32[]{:S(2)}, u32[]{:S(2)}) collective-permute-start(bf16[224,768]{1,0:T(8,128)(2,1)S(1)} %get-tuple-element.91), channel_id=1, source_target_pairs={{0,8},{8,0},{16,24},{24,16},{32,40},{40,32},{48,56},{56,48},{64,72... | collective-permute-start | bytes 1032200 | tf_op jit(solution)/shard_map/ppermute | solution.py:46
  48.4 1.7 %collective-permute-start.16 = (bf16[160,768]{1,0:T(8,128)(2,1)S(1)}, bf16[160,768]{1,0:T(8,128)(2,1)S(1)}, u32[]{:S(2)}, u32[]{:S(2)}) collective-permute-start(bf16[160,768]{1,0:T(8,128)(2,1)S(1)} %get-tuple-element.97), channel_id=1, source_target_pairs={{0,8},{8,0},{16,24},{24,16},{32,40},{40,32},{48,56},{56,48},{64,72... | collective-permute-start | bytes 737288 | tf_op jit(solution)/shard_map/ppermute | solution.py:46
  50.1 10.3 %collective-permute-start.17 = (bf16[224,640]{1,0:T(8,128)(2,1)S(1)}, bf16[224,640]{1,0:T(8,128)(2,1)S(1)}, u32[]{:S(2)}, u32[]{:S(2)}) collective-permute-start(bf16[224,640]{1,0:T(8,128)(2,1)S(1)} %get-tuple-element.105), channel_id=1, source_target_pairs={{0,2},{1,3},{2,4},{3,5},{4,6},{5,7},{6,0},{7,1},{8,10},{9,11},{10,... | collective-permute-start | bytes 860168 | tf_op jit(solution)/shard_map/ppermute | solution.py:375
  51.7 8.7 %collective-permute-start.18 = (bf16[224,640]{1,0:T(8,128)(2,1)S(1)}, bf16[224,640]{1,0:T(8,128)(2,1)S(1)}, u32[]{:S(2)}, u32[]{:S(2)}) collective-permute-start(bf16[224,640]{1,0:T(8,128)(2,1)S(1)} %get-tuple-element.106), channel_id=1, source_target_pairs={{0,6},{1,7},{2,0},{3,1},{4,2},{5,3},{6,4},{7,5},{8,14},{9,15},{10,... | collective-permute-start | bytes 860168 | tf_op jit(solution)/shard_map/ppermute | solution.py:376
  54.8 21.5 %collective-permute-start.21 = (bf16[640,640]{1,0:T(8,128)(2,1)S(1)}, bf16[640,640]{1,0:T(8,128)(2,1)S(1)}, u32[]{:S(2)}, u32[]{:S(2)}) collective-permute-start(bf16[640,640]{1,0:T(8,128)(2,1)S(1)} %get-tuple-element.110), channel_id=1, source_target_pairs={{0,1},{1,0},{2,3},{3,2},{4,5},{5,4},{6,7},{7,6},{8,9},{9,8},{10,11... | collective-permute-start | bytes 2457608 | tf_op jit(solution)/shard_map/ppermute | solution.py:46
  60.6 15.8 %collective-permute-start.19 = (bf16[448,640]{1,0:T(8,128)(2,1)S(1)}, bf16[448,640]{1,0:T(8,128)(2,1)S(1)}, u32[]{:S(2)}, u32[]{:S(2)}) collective-permute-start(bf16[448,640]{1,0:T(8,128)(2,1)S(1)} %get-tuple-element.107), channel_id=1, source_target_pairs={{0,6},{1,7},{2,0},{3,1},{4,2},{5,3},{6,4},{7,5},{8,14},{9,15},{10,... | collective-permute-start | bytes 1720328 | tf_op jit(solution)/shard_map/ppermute | solution.py:393
  63.7 15.0 %collective-permute-start.20 = (bf16[448,640]{1,0:T(8,128)(2,1)S(1)}, bf16[448,640]{1,0:T(8,128)(2,1)S(1)}, u32[]{:S(2)}, u32[]{:S(2)}) collective-permute-start(bf16[448,640]{1,0:T(8,128)(2,1)S(1)} %get-tuple-element.108), channel_id=1, source_target_pairs={{0,2},{1,3},{2,4},{3,5},{4,6},{5,7},{6,0},{7,1},{8,10},{9,11},{10,... | collective-permute-start | bytes 1720328 | tf_op jit(solution)/shard_map/ppermute | solution.py:392
  78.6 8.7 %collective-permute-start.23 = (bf16[160,640]{1,0:T(8,128)(2,1)S(1)}, bf16[160,640]{1,0:T(8,128)(2,1)S(1)}, u32[]{:S(2)}, u32[]{:S(2)}) collective-permute-start(bf16[160,640]{1,0:T(8,128)(2,1)S(1)} %get-tuple-element.118), channel_id=1, source_target_pairs={{0,4},{1,5},{2,6},{3,7},{4,0},{5,1},{6,2},{7,3},{8,12},{9,13},{10,... | collective-permute-start | bytes 614408 | tf_op jit(solution)/shard_map/ppermute | solution.py:400
  78.6 10.8 %collective-permute-start.24 = (bf16[160,640]{1,0:T(8,128)(2,1)S(1)}, bf16[160,640]{1,0:T(8,128)(2,1)S(1)}, u32[]{:S(2)}, u32[]{:S(2)}) collective-permute-start(bf16[160,640]{1,0:T(8,128)(2,1)S(1)} %get-tuple-element.119), channel_id=1, source_target_pairs={{0,2},{1,3},{2,4},{3,5},{4,6},{5,7},{6,0},{7,1},{8,10},{9,11},{10,... | collective-permute-start | bytes 614408 | tf_op jit(solution)/shard_map/ppermute | solution.py:400
  79.8 9.7 %collective-permute-start.25 = (bf16[160,640]{1,0:T(8,128)(2,1)S(1)}, bf16[160,640]{1,0:T(8,128)(2,1)S(1)}, u32[]{:S(2)}, u32[]{:S(2)}) collective-permute-start(bf16[160,640]{1,0:T(8,128)(2,1)S(1)} %get-tuple-element.120), channel_id=1, source_target_pairs={{0,6},{1,7},{2,0},{3,1},{4,2},{5,3},{6,4},{7,5},{8,14},{9,15},{10,... | collective-permute-start | bytes 614408 | tf_op jit(solution)/shard_map/ppermute | solution.py:400
  82.0 8.2 %collective-permute-start.22 = (bf16[224,640]{1,0:T(8,128)(2,1)S(1)}, bf16[224,640]{1,0:T(8,128)(2,1)S(1)}, u32[]{:S(2)}, u32[]{:S(2)}) collective-permute-start(bf16[224,640]{1,0:T(8,128)(2,1)S(1)} %turn.1), channel_id=1, source_target_pairs={{0,1},{1,0},{2,3},{3,2},{4,5},{5,4},{6,7},{7,6},{8,9},{9,8},{10,11... | collective-permute-start | bytes 860168 | tf_op jit(solution)/shard_map/ppermute | solution.py:46

commit v4 on v3

--- a/solution.py
+++ b/solution.py
@@ -16,7 +16,8 @@
 BF16 = jnp.bfloat16
 VMEM_LIMIT = 20 << 20
 IN_VMEM = pl.BlockSpec(memory_space=pltpu.VMEM)
-CUT = 224
+CUT = 256
+AHEAD_ROWS = 160
 LITTLE = pl.CostEstimate(flops=1, bytes_accessed=1, transcendentals=0)
 AFTER_STARTS = pl.CostEstimate(flops=20_000_000_000, bytes_accessed=1, transcendentals=0)
 
@@ -119,16 +120,28 @@
         (part_ref, log_ref, key_ref, value_ref, query_ref) = refs
     rows = high - low
     heads = queries[0].shape[1] // HD
-    for head in range(heads):
+
+    def scores_for(head):
         columns = slice(head * HD, (head + 1) * HD)
         slot = head % 2
         fill_keys(key_ref.at[slot], value_ref.at[slot], halves, pieces, columns)
         for place in range(2):
             query_ref[slot, place * rows : (place + 1) * rows, :] = queries[place][low:high, columns]
-        scores = scores_of(query_ref[slot], key_ref[slot])
+        return scores_of(query_ref[slot], key_ref[slot])
+
+    ahead = rows <= AHEAD_ROWS
+    next_scores = scores_for(0)
+    for head in range(heads):
+        columns = slice(head * HD, (head + 1) * HD)
+        slot = head % 2
+        scores = next_scores
+        if ahead and head + 1 < heads:
+            next_scores = scores_for(head + 1)
         peak = jnp.max(scores, axis=1, keepdims=True)
         weights = jnp.exp2((scores - peak) * BASE2).astype(BF16)
         both = jnp.dot(weights, value_ref[slot], preferred_element_type=F32)
+        if not ahead and head + 1 < heads:
+            next_scores = scores_for(head + 1)
         summed, total = both[:, :HD], both[:, HD:]
         peak = peak * BASE2
         for place in range(2):
@@ -244,35 +257,32 @@
     )
 
 
-def keep_kernel(blocks, place, att, weight, out):
-    products(blocks, place, att, weight, (out,))
-
-
-def project_keep(blocks, place, att, weight):
+def keep_kernel(blocks, place, att, weight, *outs):
+    products(blocks, place, att, weight, outs)
+
+
+def project_keep(blocks, place, att, weight, n_outs=1, dtype=F32):
     rows, width = att.shape
-    count = len(blocks)
     return local(
         functools.partial(keep_kernel, blocks),
-        [((count * rows, width), F32)],
+        [((len(blocks) // n_outs * rows, width), dtype)] * n_outs,
         att,
         weight,
         scalars=(place,),
         name="project_keep",
-    )[0]
+    )
 
 
 def relay_kernel(kept, got_left, got_right, to_right, to_left):
     n = got_left.shape[0]
-    to_right[:n, :] = (kept[:n, :] + got_left[...].astype(F32)).astype(BF16)
-    to_right[n:, :] = kept[n : 2 * n, :].astype(BF16)
-    to_left[:n, :] = (kept[2 * n : 3 * n, :] + got_right[...].astype(F32)).astype(BF16)
-    to_left[n:, :] = kept[3 * n : 4 * n, :].astype(BF16)
-
-
-def turn_kernel(kept, on_right, on_left, out):
+    to_right[...] = (kept[:n, :] + got_left[...].astype(F32)).astype(BF16)
+    to_left[...] = (kept[n : 2 * n, :] + got_right[...].astype(F32)).astype(BF16)
+
+
+def turn_kernel(kept, next_left, on_left, out):
     n = out.shape[0]
     out[...] = (
-        kept[5 * n :, :] + on_left[:n, :].astype(F32) + on_right[n:, :].astype(F32)
+        kept[3 * n :, :] + on_left[...].astype(F32) + next_left[...].astype(F32)
     ).astype(BF16)
 
 
@@ -283,22 +293,24 @@
         out[...] = (kept[rows, :] + got[rows, :].astype(F32)).astype(out.dtype)
 
 
-def total_kernel(first, *refs):
-    total = first[...]
-    for other in refs[:-1]:
-        total = total + other[...].astype(F32)
-    refs[-1][...] = total.astype(BF16)
-
-
-def last_kernel(kept, on_right, on_left, mine, above, out):
+def below_kernel(kept, on_right, next_right, mine, out):
     n = mine.shape[0]
-    out[:n, :] = (
-        kept[4 * n : 5 * n, :]
-        + on_right[:n, :].astype(F32)
-        + on_left[n:, :].astype(F32)
+    out[...] = (
+        kept[2 * n : 3 * n, :]
+        + on_right[...].astype(F32)
+        + next_right[...].astype(F32)
         + mine[...].astype(F32)
     ).astype(BF16)
-    out[n:, :] = above[...]
+
+
+def last_kernel(below, rest, *refs):
+    others, out = refs[:-1], refs[-1]
+    n = below.shape[0]
+    out[:n, :] = below[...]
+    total = rest[...]
+    for other in others:
+        total = total + other[...].astype(F32)
+    out[n:, :] = total.astype(BF16)
 
 
 def body(queries, keys, values, ref_keys, ref_values, out_weight):
@@ -372,40 +384,50 @@
 
     last_done = finish(CUT, rows, last_state)
     last_done, go_right, go_left = lax.optimization_barrier((last_done, go_right, go_left))
-    got_left = lax.ppermute(go_right, "head", right_x)
-    got_right = lax.ppermute(go_left, "head", left_x)
     go_across, last_att = project_send(
         ((2, 1), (1, 1), (3, 1), (0, 1)), place, *last_done, out_weight, 1, AFTER_STARTS
     )
     got_across = swap(go_across, "head", 1)
+    got_right = lax.ppermute(go_left, "head", left_x)
+    got_left = lax.ppermute(go_right, "head", right_x)
 
     att, last_att = lax.optimization_barrier((att, last_att))
-    kept = project_keep(
-        ((1, 0), (1, 1), (3, 1), (3, 0), (0, 0), (0, 1)), place, att, out_weight
-    )
-    last_kept = project_keep(
-        ((2, 0), (1, 0), (3, 0), (0, 0)), place, last_att, out_weight
-    )
-
-    two = ((2 * CUT, width), BF16)
-    to_right, to_left = local(relay_kernel, [two, two], kept, got_left, got_right, name="relay")
+    next_go_right, next_go_left = project_keep(((1, 1), (3, 0)), place, att, out_weight, 2, BF16)
+    next_left = lax.ppermute(next_go_right, "head", right_x)
+    next_right = lax.ppermute(next_go_left, "head", left_x)
+    att, next_go_right = lax.optimization_barrier((att, next_go_right))
+    (kept,) = project_keep(((1, 0), (3, 1), (0, 0), (0, 1)), place, att, out_weight)
+
+    one = ((CUT, width), BF16)
+    to_right, to_left = local(relay_kernel, [one, one], kept, got_left, got_right, name="relay")
     on_right = lax.ppermute(to_right, "head", right_x)
     on_left = lax.ppermute(to_left, "head", left_x)
 
+    last_att, next_left, next_right = lax.optimization_barrier((last_att, next_left, next_right))
+    (last_kept,) = project_keep(
+        ((2, 0), (1, 0), (3, 0), (0, 0)), place, last_att, out_weight
+    )
     part = (rows - CUT, width)
     *spread, rest = local(
         spread_kernel, [(part, BF16)] * 3 + [(part, F32)], last_kept, got_across, name="spread"
     )
-    on_left, on_right, spread, rest = lax.optimization_barrier((on_left, on_right, spread, rest))
     others = [lax.ppermute(a, "head", along_x(step)) for a, step in zip(spread, (2, 1, X - 1))]
+    kept, rest, on_left, on_right = lax.optimization_barrier((kept, rest, on_left, on_right))
     (turned,) = local(
-        turn_kernel, [((CUT, width), BF16)], kept, on_right, on_left, cost=AFTER_STARTS, name="turn"
+        turn_kernel, [((CUT, width), BF16)], kept, next_left, on_left, cost=AFTER_STARTS, name="turn"
     )
     mine_got = swap(turned, "head", 1)
-    (above,) = local(total_kernel, [(part, BF16)], rest, *others, cost=AFTER_STARTS, name="total")
-    return local_out(
-        last_kernel, ((rows, width), BF16), kept, on_right, on_left, mine_got, above
-    )
+    (below,) = local(
+        below_kernel,
+        [((CUT, width), BF16)],
+        kept,
+        on_right,
+        next_right,
+        mine_got,
+        cost=AFTER_STARTS,
+        name="below",
+    )
+    return local_out(last_kernel, ((rows, width), BF16), below, rest, *others)
 
 
 def local_out(kernel, out, *ins):

time: 91.3 us -> 89.9 us (0.985); the launches traced: 91.1 us -> 88.6 us
  waiting for transfers between devices: 34 us -> 26.5 us
  starting transfers between devices: 33.1 us -> 38.2 us
    ppermute x14, waiting for transfers between devices: 25.1 us -> 16.7 us  [swap(): lax.ppermute(value, axis, [(i, i ^ bit) for i in range(lax.axis_size(axis...]
    ppermute x0 -> x2, waiting for transfers between devices: none -> 4.8 us  [the longest x1 4.8 us: body(): next_left = lax.ppermute(next_go_right, 'head', right_x)]
    ppermute x0 -> x2, starting transfers between devices: none -> 3.31 us  [the longest x1 2.97 us: body(): next_right = lax.ppermute(next_go_left, 'head', left_x)]
    ppermute x3, waiting for transfers between devices: 5.09 us -> 2.22 us  [body(): lax.ppermute(a, 'head', along_x(step))]
    ppermute x1, waiting for transfers between devices: 0.01 us -> 2.74 us  [body(): on_left = lax.ppermute(to_left, 'head', left_x)]
    ppermute x3, starting transfers between devices: 3.24 us -> 5.97 us  [body(): lax.ppermute(a, 'head', along_x(step))]
    ppermute x1, waiting for transfers between devices: 2.23 us -> 0.01 us  [body(): on_right = lax.ppermute(to_right, 'head', right_x)]
    ppermute x1, waiting for transfers between devices: 1.55 us -> 0.01 us  [body(): got_left = lax.ppermute(go_right, 'head', right_x)]
  transfers between devices with their start and end apart: 26 -> 28, of which waited for: 11 -> 11; matrix products, arithmetic and copies ran while one was open for 0% -> 0% of each run, Pallas kernels for 20% -> 20%
where the time goes in v4:
time: 89.9 us; the launch traced here: 88.6 us
  starting transfers between devices  38.2 us (42%)
  waiting for transfers between devices  26.5 us (29%)
  Pallas kernels  23.7 us (26%)
    pallas_call x13, Pallas kernels, local(): pl.pallas_call(kernel, in_specs=[pl.BlockSpec(memory_space=pltpu.SMEM)] *...  19.5 us
    ppermute x14, waiting for transfers between devices, swap(): lax.ppermute(value, axis, [(i, i ^ bit) for i in range(lax.axis_size(axis...  16.7 us
    ppermute x14, starting transfers between devices, swap(): lax.ppermute(value, axis, [(i, i ^ bit) for i in range(lax.axis_size(axis...  13.4 us
    ppermute x3, starting transfers between devices, body(): lax.ppermute(a, 'head', along_x(step))  5.97 us
    ppermute x1, starting transfers between devices, body(): outer = [lax.ppermute(own, 'seq', between)]  5.94 us
    ppermute x1, waiting for transfers between devices, body(): next_left = lax.ppermute(next_go_right, 'head', right_x)  4.8 us
    pallas_call x5, Pallas kernels, stacked(): pl.pallas_call(functools.partial(stack_kernel, parts, len(arrays)), in_sp...  3.31 us
    ppermute x1, starting transfers between devices, body(): next_right = lax.ppermute(next_go_left, 'head', left_x)  2.97 us
  transfers between devices with their start and end apart: 28, of which 11 were waited for; matrix products, arithmetic and copies ran while one was open for 0% of the time, Pallas kernels for 20%

profile of v4, /device:TPU:8, one launch (start us, length us, event | category | flops | bytes accessed | tf_op | source)
XLA Modules:
  0.0 88.6 jit_solution(7707414659077969490)
XLA Ops:
  0.0 0.9 stacked.5.refs_0_.refs_7_
  0.9 5.9 %collective-permute-start = (bf16[96,640]{1,0:T(8,128)(2,1)S(1)}, bf16[96,640]{1,0:T(8,128)(2,1)S(1)}, u32[]{:S(2)}, u32[]{:S(2)}) collective-permute-start(bf16[96,640]{1,0:T(8,128)(2,1)S(1)} %stacked.5.refs_0_.refs_7_), channel_id=1, source_target_pairs={{0,112},{8,120},{16,32},{24,40},{32,16},{40,24},{48,64},{56,72},{6... | collective-permute-start | bytes 368648 | tf_op jit(solution)/shard_map/ppermute | solution.py:329
  6.8 1.4 %stacked.6 = (bf16[192,640]{1,0:T(8,128)(2,1)S(1)}, bf16[192,640]{1,0:T(8,128)(2,1)S(1)}, bf16[384,640]{1,0:T(8,128)(2,1)S(1)}) custom-call(bf16[384,640]{1,0:T(8,128)(2,1)} %refs_0_.5, bf16[384,640]{1,0:T(8,128)(2,1)} %refs_1_.2), custom_call_target="tpu_custom_call" | custom-call | flops 1 | bytes 1 | tf_op jit(solution)/shard_map/stacked/pallas_call | solution.py:86
  8.2 2.1 %collective-permute-start.4 = (bf16[192,640]{1,0:T(8,128)(2,1)S(1)}, bf16[192,640]{1,0:T(8,128)(2,1)S(1)}, u32[]{:S(2)}, u32[]{:S(2)}) collective-permute-start(bf16[192,640]{1,0:T(8,128)(2,1)S(1)} %get-tuple-element.71.refs_2_), channel_id=1, source_target_pairs={{0,16},{8,24},{16,0},{24,8},{32,48},{40,56},{48,32},{56,40},{64,80... | collective-permute-start | bytes 737288 | tf_op jit(solution)/shard_map/ppermute | solution.py:47
  10.3 0.0 collective-permute-done.refs_2_.refs_10_
  10.3 0.2 collective-permute-start.1
  10.5 2.5 %collective-permute-done.2.refs_1_.refs_8_ = bf16[96,640]{1,0:T(8,128)(2,1)S(1)} collective-permute-done((bf16[96,640]{1,0:T(8,128)(2,1)S(1)}, bf16[96,640]{1,0:T(8,128)(2,1)S(1)}, u32[]{:S(2)}, u32[]{:S(2)}) %collective-permute-start.2) | collective-permute-done | bytes 122912 | tf_op jit(solution)/shard_map/ppermute | solution.py:47
  13.0 0.1 collective-permute-start.3
  13.1 0.5 stacked.7
  13.6 0.5 collective-permute-start.8
  14.1 4.2 %collective-permute-done.4.refs_5_ = bf16[192,640]{1,0:T(8,128)(2,1)S(1)} collective-permute-done((bf16[192,640]{1,0:T(8,128)(2,1)S(1)}, bf16[192,640]{1,0:T(8,128)(2,1)S(1)}, u32[]{:S(2)}, u32[]{:S(2)}) %collective-permute-start.4) | collective-permute-done | bytes 245792 | tf_op jit(solution)/shard_map/ppermute | solution.py:47
  18.2 0.4 collective-permute-start.9
  18.7 2.2 %collective-permute-done.1.refs_0_.refs_9_ = bf16[96,640]{1,0:T(8,128)(2,1)S(1)} collective-permute-done((bf16[96,640]{1,0:T(8,128)(2,1)S(1)}, bf16[96,640]{1,0:T(8,128)(2,1)S(1)}, u32[]{:S(2)}, u32[]{:S(2)}) %collective-permute-start.1) | collective-permute-done | bytes 122912 | tf_op jit(solution)/shard_map/ppermute | solution.py:47
  20.9 1.0 %collective-permute-start.6 = (bf16[96,640]{1,0:T(8,128)(2,1)S(1)}, bf16[96,640]{1,0:T(8,128)(2,1)S(1)}, u32[]{:S(2)}, u32[]{:S(2)}) collective-permute-start(bf16[96,640]{1,0:T(8,128)(2,1)S(1)} %collective-permute-done.3.refs_1_.refs_11_), channel_id=1, source_target_pairs={{0,16},{8,24},{16,0},{24,8},{32,48},{40,56},{48,32},{56,40},{64,80... | collective-permute-start | bytes 368648 | tf_op jit(solution)/shard_map/ppermute | solution.py:47
  21.8 1.0 %collective-permute-start.7 = (bf16[96,640]{1,0:T(8,128)(2,1)S(1)}, bf16[96,640]{1,0:T(8,128)(2,1)S(1)}, u32[]{:S(2)}, u32[]{:S(2)}) collective-permute-start(bf16[96,640]{1,0:T(8,128)(2,1)S(1)} %collective-permute-done.1.refs_0_.refs_9_), channel_id=1, source_target_pairs={{0,112},{8,120},{16,32},{24,40},{32,16},{40,24},{48,64},{56,72},{6... | collective-permute-start | bytes 368648 | tf_op jit(solution)/shard_map/ppermute | solution.py:349
  22.8 0.3 stacked.8
  23.1 0.0 copy-start
  23.1 1.2 %collective-permute-start.14 = (bf16[384,640]{1,0:T(8,128)(2,1)S(1)}, bf16[384,640]{1,0:T(8,128)(2,1)S(1)}, u32[]{:S(2)}, u32[]{:S(2)}) collective-permute-start(bf16[384,640]{1,0:T(8,128)(2,1)S(1)} %get-tuple-element.80.refs_4_), channel_id=1, source_target_pairs={{0,16},{8,24},{16,0},{24,8},{32,48},{40,56},{48,32},{56,40},{64,80... | collective-permute-start | bytes 1474568 | tf_op jit(solution)/shard_map/ppermute | solution.py:47
  24.3 1.8 %collective-permute-done.8.refs_6_ = bf16[192,640]{1,0:T(8,128)(2,1)S(1)} collective-permute-done((bf16[192,640]{1,0:T(8,128)(2,1)S(1)}, bf16[192,640]{1,0:T(8,128)(2,1)S(1)}, u32[]{:S(2)}, u32[]{:S(2)}) %collective-permute-start.8) | collective-permute-done | bytes 245792 | tf_op jit(solution)/shard_map/ppermute | solution.py:47
  26.1 0.4 collective-permute-start.12
  26.6 2.2 %collective-permute-done.6.refs_0_.refs_4_ = bf16[96,640]{1,0:T(8,128)(2,1)S(1)} collective-permute-done((bf16[96,640]{1,0:T(8,128)(2,1)S(1)}, bf16[96,640]{1,0:T(8,128)(2,1)S(1)}, u32[]{:S(2)}, u32[]{:S(2)}) %collective-permute-start.6) | collective-permute-done | bytes 122912 | tf_op jit(solution)/shard_map/ppermute | solution.py:47
  28.8 0.9 %collective-permute-start.10 = (bf16[96,640]{1,0:T(8,128)(2,1)S(1)}, bf16[96,640]{1,0:T(8,128)(2,1)S(1)}, u32[]{:S(2)}, u32[]{:S(2)}) collective-permute-start(bf16[96,640]{1,0:T(8,128)(2,1)S(1)} %collective-permute-done.6.refs_0_.refs_4_), channel_id=1, source_target_pairs={{0,112},{8,120},{16,32},{24,40},{32,16},{40,24},{48,64},{56,72},{6... | collective-permute-start | bytes 368648 | tf_op jit(solution)/shard_map/ppermute | solution.py:349
  29.7 2.2 %collective-permute-start.11 = (bf16[96,640]{1,0:T(8,128)(2,1)S(1)}, bf16[96,640]{1,0:T(8,128)(2,1)S(1)}, u32[]{:S(2)}, u32[]{:S(2)}) collective-permute-start(bf16[96,640]{1,0:T(8,128)(2,1)S(1)} %collective-permute-done.6.refs_0_.refs_4_), channel_id=1, source_target_pairs={{0,240},{8,248},{16,160},{24,168},{32,144},{40,152},{48,192},{56,2... | collective-permute-start | bytes 368648 | tf_op jit(solution)/shard_map/ppermute | solution.py:351
  31.9 0.3 stacked.9
  32.2 1.8 %collective-permute-start.13 = (bf16[192,640]{1,0:T(8,128)(2,1)S(1)}, bf16[192,640]{1,0:T(8,128)(2,1)S(1)}, u32[]{:S(2)}, u32[]{:S(2)}) collective-permute-start(bf16[192,640]{1,0:T(8,128)(2,1)S(1)} %stacked.9), channel_id=1, source_target_pairs={{0,128},{8,136},{16,144},{24,152},{32,160},{40,168},{48,176},{56,1... | collective-permute-start | bytes 737288 | tf_op jit(solution)/shard_map/ppermute | solution.py:47
  34.1 2.5 %attend_part.3 = (f32[256,640]{1,0:T(8,128)S(1)}, f32[256,128]{1,0:T(8,128)S(1)}) custom-call(bf16[384,640]{1,0:T(8,128)(2,1)S(1)} %copy-done, bf16[384,640]{1,0:T(8,128)(2,1)S(1)} %collective-permute-done.5.refs_1_, bf16[192,640]{1,0:T(8,128)(2,1)S(1)} %get-tuple-element.71.refs_2_, bf16[192,640]{1,0:T(8,128)(2,1)S(1)} %get-tuple-element.76.refs_3_, ...), custom_call_target="tpu_custom_call" | custom-call | flops 20000000000 | bytes 1 | tf_op jit(solution)/shard_map/attend_part/pallas_call | solution.py:55
  36.6 0.0 slice-start.1
  36.6 4.5 %attend_part.2 = (f32[512,640]{1,0:T(8,128)S(1)}, f32[512,128]{1,0:T(8,128)S(1)}) custom-call(bf16[384,640]{1,0:T(8,128)(2,1)S(1)} %copy-done, bf16[384,640]{1,0:T(8,128)(2,1)S(1)} %collective-permute-done.5.refs_1_, bf16[192,640]{1,0:T(8,128)(2,1)S(1)} %get-tuple-element.71.refs_2_, bf16[192,640]{1,0:T(8,128)(2,1)S(1)} %get-tuple-element.76.refs_3_, ...), custom_call_target="tpu_custom_call" | custom-call | flops 20000000000 | bytes 1 | tf_op jit(solution)/shard_map/attend_part/pallas_call | solution.py:55
  41.1 0.0 collective-permute-done.10.refs_6_
  41.1 0.0 collective-permute-done.11.refs_7_
  41.1 0.0 collective-permute-done.12.refs_8_
  41.2 0.0 collective-permute-done.14.refs_10_
  41.2 4.2 %attend_last.2 = (bf16[256,640]{1,0:T(8,128)(2,1)S(1)}, f32[256,128]{1,0:T(8,128)S(1)}, bf16[256,768]{1,0:T(8,128)(2,1)S(1)}) custom-call(bf16[384,640]{1,0:T(8,128)(2,1)S(1)} %copy-done, bf16[384,640]{1,0:T(8,128)(2,1)S(1)} %collective-permute-done.5.refs_1_, f32[512,640]{1,0:T(8,128)S(1)} %get-tuple-element.88.refs_2_, ...), custom_call_target="tpu_custom_call" | custom-call | flops 1 | bytes 1 | tf_op jit(solution)/shard_map/attend_last/pallas_call | solution.py:55
  45.4 0.3 collective-permute-start.15
  45.7 2.4 %attend_last.3 = (bf16[128,640]{1,0:T(8,128)(2,1)S(1)}, f32[128,128]{1,0:T(8,128)S(1)}, bf16[128,768]{1,0:T(8,128)(2,1)S(1)}) custom-call(bf16[384,640]{1,0:T(8,128)(2,1)S(1)} %copy-done, bf16[384,640]{1,0:T(8,128)(2,1)S(1)} %collective-permute-done.5.refs_1_, f32[256,640]{1,0:T(8,128)S(1)} %get-tuple-element.97.refs_2_, ...), custom_call_target="tpu_custom_call" | custom-call | flops 1 | bytes 1 | tf_op jit(solution)/shard_map/attend_last/pallas_call | solution.py:55
  48.2 0.6 collective-permute-start.16
  48.8 1.2 %project_send.2 = (bf16[256,640]{1,0:T(8,128)(2,1)S(1)}, bf16[256,640]{1,0:T(8,128)(2,1)S(1)}, bf16[256,640]{1,0:T(8,128)(2,1)S(1)}) custom-call(s32[1]{0:T(128)} %bitcast.place, bf16[256,640]{1,0:T(8,128)(2,1)S(1)} %get-tuple-element.93.own, f32[256,128]{1,0:T(8,128)S(1)} %get-tuple-element.94.own_log, bf16[256,768]{1,0:T(8,128)(2,1)S(1)} %collective-permute-done.15.got, ...), custom_call_target="tpu_custom_call" | custom-call | flops 1 | bytes 1 | tf_op jit(solution)/shard_map/project_send/pallas_call | solution.py:55
  50.0 0.0 collective-permute-done.16.got
  50.0 1.6 %collective-permute-start.20 = (bf16[256,640]{1,0:T(8,128)(2,1)S(1)}, bf16[256,640]{1,0:T(8,128)(2,1)S(1)}, u32[]{:S(2)}, u32[]{:S(2)}) collective-permute-start(bf16[256,640]{1,0:T(8,128)(2,1)S(1)} %get-tuple-element.116), channel_id=1, source_target_pairs={{0,2},{1,3},{2,4},{3,5},{4,6},{5,7},{6,0},{7,1},{8,10},{9,11},{10,... | collective-permute-start | bytes 983048 | tf_op jit(solution)/shard_map/ppermute | solution.py:392
  51.6 1.8 %collective-permute-start.21 = (bf16[256,640]{1,0:T(8,128)(2,1)S(1)}, bf16[256,640]{1,0:T(8,128)(2,1)S(1)}, u32[]{:S(2)}, u32[]{:S(2)}) collective-permute-start(bf16[256,640]{1,0:T(8,128)(2,1)S(1)} %get-tuple-element.117), channel_id=1, source_target_pairs={{0,6},{1,7},{2,0},{3,1},{4,2},{5,3},{6,4},{7,5},{8,14},{9,15},{10,... | collective-permute-start | bytes 983048 | tf_op jit(solution)/shard_map/ppermute | solution.py:391
  53.3 1.1 %project_send.3 = (bf16[512,640]{1,0:T(8,128)(2,1)S(1)}, bf16[128,640]{1,0:T(8,128)(2,1)S(1)}) custom-call(s32[1]{0:T(128)} %bitcast.place, bf16[128,640]{1,0:T(8,128)(2,1)S(1)} %get-tuple-element.104.own, f32[128,128]{1,0:T(8,128)S(1)} %get-tuple-element.105.own_log, bf16[128,768]{1,0:T(8,128)(2,1)S(1)} %collective-permute-done.16.got, ...), custom_call_target="tpu_custom_call" | custom-call | flops 20000000000 | bytes 1 | tf_op jit(solution)/shard_map/project_send/pallas_call | solution.py:55
  54.5 2.4 %collective-permute-start.19 = (bf16[512,640]{1,0:T(8,128)(2,1)S(1)}, bf16[512,640]{1,0:T(8,128)(2,1)S(1)}, u32[]{:S(2)}, u32[]{:S(2)}) collective-permute-start(bf16[512,640]{1,0:T(8,128)(2,1)S(1)} %get-tuple-element.114), channel_id=1, source_target_pairs={{0,1},{1,0},{2,3},{3,2},{4,5},{5,4},{6,7},{7,6},{8,9},{9,8},{10,11... | collective-permute-start | bytes 1966088 | tf_op jit(solution)/shard_map/ppermute | solution.py:47
  56.8 0.8 project_keep.3
  57.6 0.3 collective-permute-start.17
  57.9 3.0 %collective-permute-start.18 = (bf16[256,640]{1,0:T(8,128)(2,1)S(1)}, bf16[256,640]{1,0:T(8,128)(2,1)S(1)}, u32[]{:S(2)}, u32[]{:S(2)}) collective-permute-start(bf16[256,640]{1,0:T(8,128)(2,1)S(1)} %get-tuple-element.112), channel_id=1, source_target_pairs={{0,6},{1,7},{2,0},{3,1},{4,2},{5,3},{6,4},{7,5},{8,14},{9,15},{10,... | collective-permute-start | bytes 983048 | tf_op jit(solution)/shard_map/ppermute | solution.py:397
  60.9 1.3 %project_keep.4.kept = f32[1024,640]{1,0:T(8,128)S(1)} custom-call(s32[1]{0:T(128)} %bitcast.place, bf16[256,640]{1,0:T(8,128)(2,1)S(1)} %get-tuple-element.110.att, bf16[640,5120]{1,0:T(8,128)(2,1)S(1)} %bitcast.2), custom_call_target="tpu_custom_call" | custom-call | flops 1 | bytes 1 | tf_op jit(solution)/shard_map/project_keep/pallas_call | solution.py:55
  62.3 0.2 relay.1
  62.4 2.0 %collective-permute-start.22 = (bf16[256,640]{1,0:T(8,128)(2,1)S(1)}, bf16[256,640]{1,0:T(8,128)(2,1)S(1)}, u32[]{:S(2)}, u32[]{:S(2)}) collective-permute-start(bf16[256,640]{1,0:T(8,128)(2,1)S(1)} %get-tuple-element.118), channel_id=1, source_target_pairs={{0,6},{1,7},{2,0},{3,1},{4,2},{5,3},{6,4},{7,5},{8,14},{9,15},{10,... | collective-permute-start | bytes 983048 | tf_op jit(solution)/shard_map/ppermute | solution.py:404
  64.4 0.1 collective-permute-start.23
  64.5 4.8 %collective-permute-done.17.next_left = bf16[256,640]{1,0:T(8,128)(2,1)S(1)} collective-permute-done((bf16[256,640]{1,0:T(8,128)(2,1)S(1)}, bf16[256,640]{1,0:T(8,128)(2,1)S(1)}, u32[]{:S(2)}, u32[]{:S(2)}) %collective-permute-start.17) | collective-permute-done | bytes 327712 | tf_op jit(solution)/shard_map/ppermute | solution.py:396
  69.4 0.8 project_keep.5.kept
  70.2 2.0 %collective-permute-done.19.got = bf16[512,640]{1,0:T(8,128)(2,1)S(1)} collective-permute-done((bf16[512,640]{1,0:T(8,128)(2,1)S(1)}, bf16[512,640]{1,0:T(8,128)(2,1)S(1)}, u32[]{:S(2)}, u32[]{:S(2)}) %collective-permute-start.19) | collective-permute-done | bytes 655392 | tf_op jit(solution)/shard_map/ppermute | solution.py:47
  72.2 0.1 spread.1
  72.3 2.7 %collective-permute-done.22.on_left = bf16[256,640]{1,0:T(8,128)(2,1)S(1)} collective-permute-done((bf16[256,640]{1,0:T(8,128)(2,1)S(1)}, bf16[256,640]{1,0:T(8,128)(2,1)S(1)}, u32[]{:S(2)}, u32[]{:S(2)}) %collective-permute-start.22) | collective-permute-done | bytes 327712 | tf_op jit(solution)/shard_map/ppermute | solution.py:404
  75.1 0.1 turn.1
  75.2 2.4 %collective-permute-start.24 = (bf16[256,640]{1,0:T(8,128)(2,1)S(1)}, bf16[256,640]{1,0:T(8,128)(2,1)S(1)}, u32[]{:S(2)}, u32[]{:S(2)}) collective-permute-start(bf16[256,640]{1,0:T(8,128)(2,1)S(1)} %turn.1), channel_id=1, source_target_pairs={{0,1},{1,0},{2,3},{3,2},{4,5},{5,4},{6,7},{7,6},{8,9},{9,8},{10,11... | collective-permute-start | bytes 983048 | tf_op jit(solution)/shard_map/ppermute | solution.py:47
  77.6 2.7 %collective-permute-start.25 = (bf16[128,640]{1,0:T(8,128)(2,1)S(1)}, bf16[128,640]{1,0:T(8,128)(2,1)S(1)}, u32[]{:S(2)}, u32[]{:S(2)}) collective-permute-start(bf16[128,640]{1,0:T(8,128)(2,1)S(1)} %get-tuple-element.126), channel_id=1, source_target_pairs={{0,4},{1,5},{2,6},{3,7},{4,0},{5,1},{6,2},{7,3},{8,12},{9,13},{10,... | collective-permute-start | bytes 491528 | tf_op jit(solution)/shard_map/ppermute | solution.py:414
  80.3 1.1 %collective-permute-start.26 = (bf16[128,640]{1,0:T(8,128)(2,1)S(1)}, bf16[128,640]{1,0:T(8,128)(2,1)S(1)}, u32[]{:S(2)}, u32[]{:S(2)}) collective-permute-start(bf16[128,640]{1,0:T(8,128)(2,1)S(1)} %get-tuple-element.127), channel_id=1, source_target_pairs={{0,2},{1,3},{2,4},{3,5},{4,6},{5,7},{6,0},{7,1},{8,10},{9,11},{10,... | collective-permute-start | bytes 491528 | tf_op jit(solution)/shard_map/ppermute | solution.py:414
  81.4 2.2 %collective-permute-start.27 = (bf16[128,640]{1,0:T(8,128)(2,1)S(1)}, bf16[128,640]{1,0:T(8,128)(2,1)S(1)}, u32[]{:S(2)}, u32[]{:S(2)}) collective-permute-start(bf16[128,640]{1,0:T(8,128)(2,1)S(1)} %get-tuple-element.128), channel_id=1, source_target_pairs={{0,6},{1,7},{2,0},{3,1},{4,2},{5,3},{6,4},{7,5},{8,14},{9,15},{10,... | collective-permute-start | bytes 491528 | tf_op jit(solution)/shard_map/ppermute | solution.py:414
  83.6 1.8 %collective-permute-done.24.mine = bf16[256,640]{1,0:T(8,128)(2,1)S(1)} collective-permute-done((bf16[256,640]{1,0:T(8,128)(2,1)S(1)}, bf16[256,640]{1,0:T(8,128)(2,1)S(1)}, u32[]{:S(2)}, u32[]{:S(2)}) %collective-permute-start.24) | collective-permute-done | bytes 327712 | tf_op jit(solution)/shard_map/ppermute | solution.py:47
  85.4 0.2 below.1
  85.5 0.2 collective-permute-done.25.refs_0_
  85.7 2.0 %collective-permute-done.26.refs_1_ = bf16[128,640]{1,0:T(8,128)(2,1)S(1)} collective-permute-done((bf16[128,640]{1,0:T(8,128)(2,1)S(1)}, bf16[128,640]{1,0:T(8,128)(2,1)S(1)}, u32[]{:S(2)}, u32[]{:S(2)}) %collective-permute-start.26) | collective-permute-done | bytes 163872 | tf_op jit(solution)/shard_map/ppermute | solution.py:414
  87.8 0.9 last.1
  (18 shorter events, 0.0 us)
Async XLA Ops:
  0.9 9.4 %collective-permute-start = (bf16[96,640]{1,0:T(8,128)(2,1)S(1)}, bf16[96,640]{1,0:T(8,128)(2,1)S(1)}, u32[]{:S(2)}, u32[]{:S(2)}) collective-permute-start(bf16[96,640]{1,0:T(8,128)(2,1)S(1)} %stacked.5.refs_0_.refs_7_), channel_id=1, source_target_pairs={{0,112},{8,120},{16,32},{24,40},{32,16},{40,24},{48,64},{56,72},{6... | collective-permute-start | bytes 368648 | tf_op jit(solution)/shard_map/ppermute | solution.py:329
  6.8 6.2 %collective-permute-start.2 = (bf16[96,640]{1,0:T(8,128)(2,1)S(1)}, bf16[96,640]{1,0:T(8,128)(2,1)S(1)}, u32[]{:S(2)}, u32[]{:S(2)}) collective-permute-start(bf16[96,640]{1,0:T(8,128)(2,1)S(1)} %stacked.5.refs_0_.refs_7_), channel_id=1, source_target_pairs={{0,16},{8,24},{16,0},{24,8},{32,48},{40,56},{48,32},{56,40},{64,80... | collective-permute-start | bytes 368648 | tf_op jit(solution)/shard_map/ppermute | solution.py:47
  8.2 10.1 %collective-permute-start.4 = (bf16[192,640]{1,0:T(8,128)(2,1)S(1)}, bf16[192,640]{1,0:T(8,128)(2,1)S(1)}, u32[]{:S(2)}, u32[]{:S(2)}) collective-permute-start(bf16[192,640]{1,0:T(8,128)(2,1)S(1)} %get-tuple-element.71.refs_2_), channel_id=1, source_target_pairs={{0,16},{8,24},{16,0},{24,8},{32,48},{40,56},{48,32},{56,40},{64,80... | collective-permute-start | bytes 737288 | tf_op jit(solution)/shard_map/ppermute | solution.py:47
  10.3 10.6 %collective-permute-start.5 = (bf16[384,640]{1,0:T(8,128)(2,1)}, bf16[384,640]{1,0:T(8,128)(2,1)S(1)}, u32[]{:S(2)}, u32[]{:S(2)}) collective-permute-start(bf16[384,640]{1,0:T(8,128)(2,1)} %refs_0_.9), channel_id=1, source_target_pairs={{0,8},{8,0},{16,24},{24,16},{32,40},{40,32},{48,56},{56,48},{64,72... | collective-permute-start | bytes 1474568 | tf_op jit(solution)/shard_map/ppermute | solution.py:47
  10.3 10.6 %collective-permute-start.1 = (bf16[96,640]{1,0:T(8,128)(2,1)S(1)}, bf16[96,640]{1,0:T(8,128)(2,1)S(1)}, u32[]{:S(2)}, u32[]{:S(2)}) collective-permute-start(bf16[96,640]{1,0:T(8,128)(2,1)S(1)} %collective-permute-done.refs_2_.refs_10_), channel_id=1, source_target_pairs={{0,16},{8,24},{16,0},{24,8},{32,48},{40,56},{48,32},{56,40},{64,80... | collective-permute-start | bytes 368648 | tf_op jit(solution)/shard_map/ppermute | solution.py:47
  13.0 7.9 %collective-permute-start.3 = (bf16[96,640]{1,0:T(8,128)(2,1)S(1)}, bf16[96,640]{1,0:T(8,128)(2,1)S(1)}, u32[]{:S(2)}, u32[]{:S(2)}) collective-permute-start(bf16[96,640]{1,0:T(8,128)(2,1)S(1)} %collective-permute-done.2.refs_1_.refs_8_), channel_id=1, source_target_pairs={{0,112},{8,120},{16,32},{24,40},{32,16},{40,24},{48,64},{56,72},{6... | collective-permute-start | bytes 368648 | tf_op jit(solution)/shard_map/ppermute | solution.py:349
  13.6 12.6 %collective-permute-start.8 = (bf16[192,640]{1,0:T(8,128)(2,1)S(1)}, bf16[192,640]{1,0:T(8,128)(2,1)S(1)}, u32[]{:S(2)}, u32[]{:S(2)}) collective-permute-start(bf16[192,640]{1,0:T(8,128)(2,1)S(1)} %get-tuple-element.76.refs_3_), channel_id=1, source_target_pairs={{0,16},{8,24},{16,0},{24,8},{32,48},{40,56},{48,32},{56,40},{64,80... | collective-permute-start | bytes 737288 | tf_op jit(solution)/shard_map/ppermute | solution.py:47
  18.2 14.0 %collective-permute-start.9 = (bf16[288,640]{1,0:T(8,128)(2,1)S(1)}, bf16[288,640]{1,0:T(8,128)(2,1)S(1)}, u32[]{:S(2)}, u32[]{:S(2)}) collective-permute-start(bf16[288,640]{1,0:T(8,128)(2,1)S(1)} %stacked.7), channel_id=1, source_target_pairs={{0,128},{8,136},{16,144},{24,152},{32,160},{40,168},{48,176},{56,1... | collective-permute-start | bytes 1105928 | tf_op jit(solution)/shard_map/ppermute | solution.py:47
  20.9 7.9 %collective-permute-start.6 = (bf16[96,640]{1,0:T(8,128)(2,1)S(1)}, bf16[96,640]{1,0:T(8,128)(2,1)S(1)}, u32[]{:S(2)}, u32[]{:S(2)}) collective-permute-start(bf16[96,640]{1,0:T(8,128)(2,1)S(1)} %collective-permute-done.3.refs_1_.refs_11_), channel_id=1, source_target_pairs={{0,16},{8,24},{16,0},{24,8},{32,48},{40,56},{48,32},{56,40},{64,80... | collective-permute-start | bytes 368648 | tf_op jit(solution)/shard_map/ppermute | solution.py:47
  21.8 6.9 %collective-permute-start.7 = (bf16[96,640]{1,0:T(8,128)(2,1)S(1)}, bf16[96,640]{1,0:T(8,128)(2,1)S(1)}, u32[]{:S(2)}, u32[]{:S(2)}) collective-permute-start(bf16[96,640]{1,0:T(8,128)(2,1)S(1)} %collective-permute-done.1.refs_0_.refs_9_), channel_id=1, source_target_pairs={{0,112},{8,120},{16,32},{24,40},{32,16},{40,24},{48,64},{56,72},{6... | collective-permute-start | bytes 368648 | tf_op jit(solution)/shard_map/ppermute | solution.py:349
  23.1 11.0 %copy-start = (bf16[384,640]{1,0:T(8,128)(2,1)S(1)}, bf16[384,640]{1,0:T(8,128)(2,1)}, u32[]{:S(2)}) copy-start(bf16[384,640]{1,0:T(8,128)(2,1)} %refs_0_.9) | copy-start | bytes 1474564
  23.1 18.0 %collective-permute-start.14 = (bf16[384,640]{1,0:T(8,128)(2,1)S(1)}, bf16[384,640]{1,0:T(8,128)(2,1)S(1)}, u32[]{:S(2)}, u32[]{:S(2)}) collective-permute-start(bf16[384,640]{1,0:T(8,128)(2,1)S(1)} %get-tuple-element.80.refs_4_), channel_id=1, source_target_pairs={{0,16},{8,24},{16,0},{24,8},{32,48},{40,56},{48,32},{56,40},{64,80... | collective-permute-start | bytes 1474568 | tf_op jit(solution)/shard_map/ppermute | solution.py:47
  26.1 15.0 %collective-permute-start.12 = (bf16[192,640]{1,0:T(8,128)(2,1)S(1)}, bf16[192,640]{1,0:T(8,128)(2,1)S(1)}, u32[]{:S(2)}, u32[]{:S(2)}) collective-permute-start(bf16[192,640]{1,0:T(8,128)(2,1)S(1)} %stacked.8), channel_id=1, source_target_pairs={{0,128},{8,136},{16,144},{24,152},{32,160},{40,168},{48,176},{56,1... | collective-permute-start | bytes 737288 | tf_op jit(solution)/shard_map/ppermute | solution.py:47
  28.8 12.3 %collective-permute-start.10 = (bf16[96,640]{1,0:T(8,128)(2,1)S(1)}, bf16[96,640]{1,0:T(8,128)(2,1)S(1)}, u32[]{:S(2)}, u32[]{:S(2)}) collective-permute-start(bf16[96,640]{1,0:T(8,128)(2,1)S(1)} %collective-permute-done.6.refs_0_.refs_4_), channel_id=1, source_target_pairs={{0,112},{8,120},{16,32},{24,40},{32,16},{40,24},{48,64},{56,72},{6... | collective-permute-start | bytes 368648 | tf_op jit(solution)/shard_map/ppermute | solution.py:349
  29.7 11.4 %collective-permute-start.11 = (bf16[96,640]{1,0:T(8,128)(2,1)S(1)}, bf16[96,640]{1,0:T(8,128)(2,1)S(1)}, u32[]{:S(2)}, u32[]{:S(2)}) collective-permute-start(bf16[96,640]{1,0:T(8,128)(2,1)S(1)} %collective-permute-done.6.refs_0_.refs_4_), channel_id=1, source_target_pairs={{0,240},{8,248},{16,160},{24,168},{32,144},{40,152},{48,192},{56,2... | collective-permute-start | bytes 368648 | tf_op jit(solution)/shard_map/ppermute | solution.py:351
  32.2 8.9 %collective-permute-start.13 = (bf16[192,640]{1,0:T(8,128)(2,1)S(1)}, bf16[192,640]{1,0:T(8,128)(2,1)S(1)}, u32[]{:S(2)}, u32[]{:S(2)}) collective-permute-start(bf16[192,640]{1,0:T(8,128)(2,1)S(1)} %stacked.9), channel_id=1, source_target_pairs={{0,128},{8,136},{16,144},{24,152},{32,160},{40,168},{48,176},{56,1... | collective-permute-start | bytes 737288 | tf_op jit(solution)/shard_map/ppermute | solution.py:47
  34.1 14.7 %slice-start = ((s8[6553600]{0:T(1024)(128)(4,1)}), s8[4194304]{0:T(1024)(128)(4,1)S(1)}, s32[]{:S(2)}) async-start(s8[6553600]{0:T(1024)(128)(4,1)} %bitcast.1), calls=%async_computation | async-start | bytes 8388608
  36.6 12.1 %slice-start.1 = ((s8[6553600]{0:T(1024)(128)(4,1)}), s8[2359296]{0:T(1024)(128)(4,1)S(1)}, s32[]{:S(2)}) async-start(s8[6553600]{0:T(1024)(128)(4,1)} %bitcast.1), calls=%async_computation.1 | async-start | bytes 4718592
  45.4 3.4 %collective-permute-start.15 = (bf16[256,768]{1,0:T(8,128)(2,1)S(1)}, bf16[256,768]{1,0:T(8,128)(2,1)S(1)}, u32[]{:S(2)}, u32[]{:S(2)}) collective-permute-start(bf16[256,768]{1,0:T(8,128)(2,1)S(1)} %get-tuple-element.95), channel_id=1, source_target_pairs={{0,8},{8,0},{16,24},{24,16},{32,40},{40,32},{48,56},{56,48},{64,72... | collective-permute-start | bytes 1179656 | tf_op jit(solution)/shard_map/ppermute | solution.py:47
  48.2 1.8 %collective-permute-start.16 = (bf16[128,768]{1,0:T(8,128)(2,1)S(1)}, bf16[128,768]{1,0:T(8,128)(2,1)S(1)}, u32[]{:S(2)}, u32[]{:S(2)}) collective-permute-start(bf16[128,768]{1,0:T(8,128)(2,1)S(1)} %get-tuple-element.101), channel_id=1, source_target_pairs={{0,8},{8,0},{16,24},{24,16},{32,40},{40,32},{48,56},{56,48},{64,72... | collective-permute-start | bytes 589832 | tf_op jit(solution)/shard_map/ppermute | solution.py:47
  50.0 12.2 %collective-permute-start.20 = (bf16[256,640]{1,0:T(8,128)(2,1)S(1)}, bf16[256,640]{1,0:T(8,128)(2,1)S(1)}, u32[]{:S(2)}, u32[]{:S(2)}) collective-permute-start(bf16[256,640]{1,0:T(8,128)(2,1)S(1)} %get-tuple-element.116), channel_id=1, source_target_pairs={{0,2},{1,3},{2,4},{3,5},{4,6},{5,7},{6,0},{7,1},{8,10},{9,11},{10,... | collective-permute-start | bytes 983048 | tf_op jit(solution)/shard_map/ppermute | solution.py:392
  51.6 10.7 %collective-permute-start.21 = (bf16[256,640]{1,0:T(8,128)(2,1)S(1)}, bf16[256,640]{1,0:T(8,128)(2,1)S(1)}, u32[]{:S(2)}, u32[]{:S(2)}) collective-permute-start(bf16[256,640]{1,0:T(8,128)(2,1)S(1)} %get-tuple-element.117), channel_id=1, source_target_pairs={{0,6},{1,7},{2,0},{3,1},{4,2},{5,3},{6,4},{7,5},{8,14},{9,15},{10,... | collective-permute-start | bytes 983048 | tf_op jit(solution)/shard_map/ppermute | solution.py:391
  54.5 17.8 %collective-permute-start.19 = (bf16[512,640]{1,0:T(8,128)(2,1)S(1)}, bf16[512,640]{1,0:T(8,128)(2,1)S(1)}, u32[]{:S(2)}, u32[]{:S(2)}) collective-permute-start(bf16[512,640]{1,0:T(8,128)(2,1)S(1)} %get-tuple-element.114), channel_id=1, source_target_pairs={{0,1},{1,0},{2,3},{3,2},{4,5},{5,4},{6,7},{7,6},{8,9},{9,8},{10,11... | collective-permute-start | bytes 1966088 | tf_op jit(solution)/shard_map/ppermute | solution.py:47
  57.6 11.7 %collective-permute-start.17 = (bf16[256,640]{1,0:T(8,128)(2,1)S(1)}, bf16[256,640]{1,0:T(8,128)(2,1)S(1)}, u32[]{:S(2)}, u32[]{:S(2)}) collective-permute-start(bf16[256,640]{1,0:T(8,128)(2,1)S(1)} %get-tuple-element.109), channel_id=1, source_target_pairs={{0,2},{1,3},{2,4},{3,5},{4,6},{5,7},{6,0},{7,1},{8,10},{9,11},{10,... | collective-permute-start | bytes 983048 | tf_op jit(solution)/shard_map/ppermute | solution.py:396
  57.9 11.4 %collective-permute-start.18 = (bf16[256,640]{1,0:T(8,128)(2,1)S(1)}, bf16[256,640]{1,0:T(8,128)(2,1)S(1)}, u32[]{:S(2)}, u32[]{:S(2)}) collective-permute-start(bf16[256,640]{1,0:T(8,128)(2,1)S(1)} %get-tuple-element.112), channel_id=1, source_target_pairs={{0,6},{1,7},{2,0},{3,1},{4,2},{5,3},{6,4},{7,5},{8,14},{9,15},{10,... | collective-permute-start | bytes 983048 | tf_op jit(solution)/shard_map/ppermute | solution.py:397
  62.4 12.6 %collective-permute-start.22 = (bf16[256,640]{1,0:T(8,128)(2,1)S(1)}, bf16[256,640]{1,0:T(8,128)(2,1)S(1)}, u32[]{:S(2)}, u32[]{:S(2)}) collective-permute-start(bf16[256,640]{1,0:T(8,128)(2,1)S(1)} %get-tuple-element.118), channel_id=1, source_target_pairs={{0,6},{1,7},{2,0},{3,1},{4,2},{5,3},{6,4},{7,5},{8,14},{9,15},{10,... | collective-permute-start | bytes 983048 | tf_op jit(solution)/shard_map/ppermute | solution.py:404
  64.4 10.6 %collective-permute-start.23 = (bf16[256,640]{1,0:T(8,128)(2,1)S(1)}, bf16[256,640]{1,0:T(8,128)(2,1)S(1)}, u32[]{:S(2)}, u32[]{:S(2)}) collective-permute-start(bf16[256,640]{1,0:T(8,128)(2,1)S(1)} %get-tuple-element.119), channel_id=1, source_target_pairs={{0,2},{1,3},{2,4},{3,5},{4,6},{5,7},{6,0},{7,1},{8,10},{9,11},{10,... | collective-permute-start | bytes 983048 | tf_op jit(solution)/shard_map/ppermute | solution.py:403
  75.2 10.2 %collective-permute-start.24 = (bf16[256,640]{1,0:T(8,128)(2,1)S(1)}, bf16[256,640]{1,0:T(8,128)(2,1)S(1)}, u32[]{:S(2)}, u32[]{:S(2)}) collective-permute-start(bf16[256,640]{1,0:T(8,128)(2,1)S(1)} %turn.1), channel_id=1, source_target_pairs={{0,1},{1,0},{2,3},{3,2},{4,5},{5,4},{6,7},{7,6},{8,9},{9,8},{10,11... | collective-permute-start | bytes 983048 | tf_op jit(solution)/shard_map/ppermute | solution.py:47
  77.6 8.1 %collective-permute-start.25 = (bf16[128,640]{1,0:T(8,128)(2,1)S(1)}, bf16[128,640]{1,0:T(8,128)(2,1)S(1)}, u32[]{:S(2)}, u32[]{:S(2)}) collective-permute-start(bf16[128,640]{1,0:T(8,128)(2,1)S(1)} %get-tuple-element.126), channel_id=1, source_target_pairs={{0,4},{1,5},{2,6},{3,7},{4,0},{5,1},{6,2},{7,3},{8,12},{9,13},{10,... | collective-permute-start | bytes 491528 | tf_op jit(solution)/shard_map/ppermute | solution.py:414
  80.3 7.4 %collective-permute-start.26 = (bf16[128,640]{1,0:T(8,128)(2,1)S(1)}, bf16[128,640]{1,0:T(8,128)(2,1)S(1)}, u32[]{:S(2)}, u32[]{:S(2)}) collective-permute-start(bf16[128,640]{1,0:T(8,128)(2,1)S(1)} %get-tuple-element.127), channel_id=1, source_target_pairs={{0,2},{1,3},{2,4},{3,5},{4,6},{5,7},{6,0},{7,1},{8,10},{9,11},{10,... | collective-permute-start | bytes 491528 | tf_op jit(solution)/shard_map/ppermute | solution.py:414
  81.4 6.4 %collective-permute-start.27 = (bf16[128,640]{1,0:T(8,128)(2,1)S(1)}, bf16[128,640]{1,0:T(8,128)(2,1)S(1)}, u32[]{:S(2)}, u32[]{:S(2)}) collective-permute-start(bf16[128,640]{1,0:T(8,128)(2,1)S(1)} %get-tuple-element.128), channel_id=1, source_target_pairs={{0,6},{1,7},{2,0},{3,1},{4,2},{5,3},{6,4},{7,5},{8,14},{9,15},{10,... | collective-permute-start | bytes 491528 | tf_op jit(solution)/shard_map/ppermute | solution.py:414

commit v5 on v4

--- a/solution.py
+++ b/solution.py
@@ -17,7 +17,6 @@
 VMEM_LIMIT = 20 << 20
 IN_VMEM = pl.BlockSpec(memory_space=pltpu.VMEM)
 CUT = 256
-AHEAD_ROWS = 160
 LITTLE = pl.CostEstimate(flops=1, bytes_accessed=1, transcendentals=0)
 AFTER_STARTS = pl.CostEstimate(flops=20_000_000_000, bytes_accessed=1, transcendentals=0)
 
@@ -129,19 +128,16 @@
             query_ref[slot, place * rows : (place + 1) * rows, :] = queries[place][low:high, columns]
         return scores_of(query_ref[slot], key_ref[slot])
 
-    ahead = rows <= AHEAD_ROWS
     next_scores = scores_for(0)
     for head in range(heads):
         columns = slice(head * HD, (head + 1) * HD)
         slot = head % 2
         scores = next_scores
-        if ahead and head + 1 < heads:
+        if head + 1 < heads:
             next_scores = scores_for(head + 1)
         peak = jnp.max(scores, axis=1, keepdims=True)
         weights = jnp.exp2((scores - peak) * BASE2).astype(BF16)
         both = jnp.dot(weights, value_ref[slot], preferred_element_type=F32)
-        if not ahead and head + 1 < heads:
-            next_scores = scores_for(head + 1)
         summed, total = both[:, :HD], both[:, HD:]
         peak = peak * BASE2
         for place in range(2):

time: 89.9 us -> 89.2 us (level)
  no operation moved by 1% of the time
where the time goes in v5:
time: 89.2 us; the launch traced here: 88 us
  starting transfers between devices  38.2 us (43%)
  waiting for transfers between devices  26.5 us (30%)
  Pallas kernels  23 us (26%)
    pallas_call x13, Pallas kernels, local(): pl.pallas_call(kernel, in_specs=[pl.BlockSpec(memory_space=pltpu.SMEM)] *...  18.8 us
    ppermute x14, waiting for transfers between devices, swap(): lax.ppermute(value, axis, [(i, i ^ bit) for i in range(lax.axis_size(axis...  16.7 us
    ppermute x14, starting transfers between devices, swap(): lax.ppermute(value, axis, [(i, i ^ bit) for i in range(lax.axis_size(axis...  13.4 us
    ppermute x3, starting transfers between devices, body(): lax.ppermute(a, 'head', along_x(step))  5.97 us
    ppermute x1, starting transfers between devices, body(): outer = [lax.ppermute(own, 'seq', between)]  5.94 us
    ppermute x1, waiting for transfers between devices, body(): next_left = lax.ppermute(next_go_right, 'head', right_x)  4.8 us
    pallas_call x5, Pallas kernels, stacked(): pl.pallas_call(functools.partial(stack_kernel, parts, len(arrays)), in_sp...  3.31 us
    ppermute x1, starting transfers between devices, body(): next_right = lax.ppermute(next_go_left, 'head', left_x)  2.96 us
  transfers between devices with their start and end apart: 28, of which 11 were waited for; matrix products, arithmetic and copies ran while one was open for 0% of the time, Pallas kernels for 20%

profile of v5, /device:TPU:8, one launch (start us, length us, event | category | flops | bytes accessed | tf_op | source)
XLA Modules:
  0.0 88.0 jit_solution(6655526417699732446)
XLA Ops:
  0.0 0.9 stacked.5.refs_0_.refs_7_
  0.9 5.9 %collective-permute-start = (bf16[96,640]{1,0:T(8,128)(2,1)S(1)}, bf16[96,640]{1,0:T(8,128)(2,1)S(1)}, u32[]{:S(2)}, u32[]{:S(2)}) collective-permute-start(bf16[96,640]{1,0:T(8,128)(2,1)S(1)} %stacked.5.refs_0_.refs_7_), channel_id=1, source_target_pairs={{0,112},{8,120},{16,32},{24,40},{32,16},{40,24},{48,64},{56,72},{6... | collective-permute-start | bytes 368648 | tf_op jit(solution)/shard_map/ppermute | solution.py:325
  6.8 1.4 %stacked.6 = (bf16[192,640]{1,0:T(8,128)(2,1)S(1)}, bf16[192,640]{1,0:T(8,128)(2,1)S(1)}, bf16[384,640]{1,0:T(8,128)(2,1)S(1)}) custom-call(bf16[384,640]{1,0:T(8,128)(2,1)} %refs_0_.5, bf16[384,640]{1,0:T(8,128)(2,1)} %refs_1_.2), custom_call_target="tpu_custom_call" | custom-call | flops 1 | bytes 1 | tf_op jit(solution)/shard_map/stacked/pallas_call | solution.py:85
  8.2 2.1 %collective-permute-start.4 = (bf16[192,640]{1,0:T(8,128)(2,1)S(1)}, bf16[192,640]{1,0:T(8,128)(2,1)S(1)}, u32[]{:S(2)}, u32[]{:S(2)}) collective-permute-start(bf16[192,640]{1,0:T(8,128)(2,1)S(1)} %get-tuple-element.71.refs_2_), channel_id=1, source_target_pairs={{0,16},{8,24},{16,0},{24,8},{32,48},{40,56},{48,32},{56,40},{64,80... | collective-permute-start | bytes 737288 | tf_op jit(solution)/shard_map/ppermute | solution.py:46
  10.3 0.0 collective-permute-done.refs_2_.refs_10_
  10.3 0.2 collective-permute-start.1
  10.5 2.5 %collective-permute-done.2.refs_1_.refs_8_ = bf16[96,640]{1,0:T(8,128)(2,1)S(1)} collective-permute-done((bf16[96,640]{1,0:T(8,128)(2,1)S(1)}, bf16[96,640]{1,0:T(8,128)(2,1)S(1)}, u32[]{:S(2)}, u32[]{:S(2)}) %collective-permute-start.2) | collective-permute-done | bytes 122912 | tf_op jit(solution)/shard_map/ppermute | solution.py:46
  13.0 0.1 collective-permute-start.3
  13.1 0.5 stacked.7
  13.6 0.5 collective-permute-start.8
  14.1 4.2 %collective-permute-done.4.refs_5_ = bf16[192,640]{1,0:T(8,128)(2,1)S(1)} collective-permute-done((bf16[192,640]{1,0:T(8,128)(2,1)S(1)}, bf16[192,640]{1,0:T(8,128)(2,1)S(1)}, u32[]{:S(2)}, u32[]{:S(2)}) %collective-permute-start.4) | collective-permute-done | bytes 245792 | tf_op jit(solution)/shard_map/ppermute | solution.py:46
  18.2 0.4 collective-permute-start.9
  18.7 2.2 %collective-permute-done.1.refs_0_.refs_9_ = bf16[96,640]{1,0:T(8,128)(2,1)S(1)} collective-permute-done((bf16[96,640]{1,0:T(8,128)(2,1)S(1)}, bf16[96,640]{1,0:T(8,128)(2,1)S(1)}, u32[]{:S(2)}, u32[]{:S(2)}) %collective-permute-start.1) | collective-permute-done | bytes 122912 | tf_op jit(solution)/shard_map/ppermute | solution.py:46
  20.9 1.0 %collective-permute-start.6 = (bf16[96,640]{1,0:T(8,128)(2,1)S(1)}, bf16[96,640]{1,0:T(8,128)(2,1)S(1)}, u32[]{:S(2)}, u32[]{:S(2)}) collective-permute-start(bf16[96,640]{1,0:T(8,128)(2,1)S(1)} %collective-permute-done.3.refs_1_.refs_11_), channel_id=1, source_target_pairs={{0,16},{8,24},{16,0},{24,8},{32,48},{40,56},{48,32},{56,40},{64,80... | collective-permute-start | bytes 368648 | tf_op jit(solution)/shard_map/ppermute | solution.py:46
  21.8 1.0 %collective-permute-start.7 = (bf16[96,640]{1,0:T(8,128)(2,1)S(1)}, bf16[96,640]{1,0:T(8,128)(2,1)S(1)}, u32[]{:S(2)}, u32[]{:S(2)}) collective-permute-start(bf16[96,640]{1,0:T(8,128)(2,1)S(1)} %collective-permute-done.1.refs_0_.refs_9_), channel_id=1, source_target_pairs={{0,112},{8,120},{16,32},{24,40},{32,16},{40,24},{48,64},{56,72},{6... | collective-permute-start | bytes 368648 | tf_op jit(solution)/shard_map/ppermute | solution.py:345
  22.8 0.3 stacked.8
  23.1 0.0 copy-start
  23.1 1.2 %collective-permute-start.14 = (bf16[384,640]{1,0:T(8,128)(2,1)S(1)}, bf16[384,640]{1,0:T(8,128)(2,1)S(1)}, u32[]{:S(2)}, u32[]{:S(2)}) collective-permute-start(bf16[384,640]{1,0:T(8,128)(2,1)S(1)} %get-tuple-element.80.refs_4_), channel_id=1, source_target_pairs={{0,16},{8,24},{16,0},{24,8},{32,48},{40,56},{48,32},{56,40},{64,80... | collective-permute-start | bytes 1474568 | tf_op jit(solution)/shard_map/ppermute | solution.py:46
  24.3 1.8 %collective-permute-done.8.refs_6_ = bf16[192,640]{1,0:T(8,128)(2,1)S(1)} collective-permute-done((bf16[192,640]{1,0:T(8,128)(2,1)S(1)}, bf16[192,640]{1,0:T(8,128)(2,1)S(1)}, u32[]{:S(2)}, u32[]{:S(2)}) %collective-permute-start.8) | collective-permute-done | bytes 245792 | tf_op jit(solution)/shard_map/ppermute | solution.py:46
  26.1 0.4 collective-permute-start.12
  26.6 2.2 %collective-permute-done.6.refs_0_.refs_4_ = bf16[96,640]{1,0:T(8,128)(2,1)S(1)} collective-permute-done((bf16[96,640]{1,0:T(8,128)(2,1)S(1)}, bf16[96,640]{1,0:T(8,128)(2,1)S(1)}, u32[]{:S(2)}, u32[]{:S(2)}) %collective-permute-start.6) | collective-permute-done | bytes 122912 | tf_op jit(solution)/shard_map/ppermute | solution.py:46
  28.8 0.9 %collective-permute-start.10 = (bf16[96,640]{1,0:T(8,128)(2,1)S(1)}, bf16[96,640]{1,0:T(8,128)(2,1)S(1)}, u32[]{:S(2)}, u32[]{:S(2)}) collective-permute-start(bf16[96,640]{1,0:T(8,128)(2,1)S(1)} %collective-permute-done.6.refs_0_.refs_4_), channel_id=1, source_target_pairs={{0,112},{8,120},{16,32},{24,40},{32,16},{40,24},{48,64},{56,72},{6... | collective-permute-start | bytes 368648 | tf_op jit(solution)/shard_map/ppermute | solution.py:345
  29.7 2.2 %collective-permute-start.11 = (bf16[96,640]{1,0:T(8,128)(2,1)S(1)}, bf16[96,640]{1,0:T(8,128)(2,1)S(1)}, u32[]{:S(2)}, u32[]{:S(2)}) collective-permute-start(bf16[96,640]{1,0:T(8,128)(2,1)S(1)} %collective-permute-done.6.refs_0_.refs_4_), channel_id=1, source_target_pairs={{0,240},{8,248},{16,160},{24,168},{32,144},{40,152},{48,192},{56,2... | collective-permute-start | bytes 368648 | tf_op jit(solution)/shard_map/ppermute | solution.py:347
  31.9 0.3 stacked.9
  32.2 1.8 %collective-permute-start.13 = (bf16[192,640]{1,0:T(8,128)(2,1)S(1)}, bf16[192,640]{1,0:T(8,128)(2,1)S(1)}, u32[]{:S(2)}, u32[]{:S(2)}) collective-permute-start(bf16[192,640]{1,0:T(8,128)(2,1)S(1)} %stacked.9), channel_id=1, source_target_pairs={{0,128},{8,136},{16,144},{24,152},{32,160},{40,168},{48,176},{56,1... | collective-permute-start | bytes 737288 | tf_op jit(solution)/shard_map/ppermute | solution.py:46
  34.1 2.5 %attend_part.3 = (f32[256,640]{1,0:T(8,128)S(1)}, f32[256,128]{1,0:T(8,128)S(1)}) custom-call(bf16[384,640]{1,0:T(8,128)(2,1)S(1)} %copy-done, bf16[384,640]{1,0:T(8,128)(2,1)S(1)} %collective-permute-done.5.refs_1_, bf16[192,640]{1,0:T(8,128)(2,1)S(1)} %get-tuple-element.71.refs_2_, bf16[192,640]{1,0:T(8,128)(2,1)S(1)} %get-tuple-element.76.refs_3_, ...), custom_call_target="tpu_custom_call" | custom-call | flops 20000000000 | bytes 1 | tf_op jit(solution)/shard_map/attend_part/pallas_call | solution.py:54
  36.6 0.0 slice-start.1
  36.6 4.1 %attend_part.2 = (f32[512,640]{1,0:T(8,128)S(1)}, f32[512,128]{1,0:T(8,128)S(1)}) custom-call(bf16[384,640]{1,0:T(8,128)(2,1)S(1)} %copy-done, bf16[384,640]{1,0:T(8,128)(2,1)S(1)} %collective-permute-done.5.refs_1_, bf16[192,640]{1,0:T(8,128)(2,1)S(1)} %get-tuple-element.71.refs_2_, bf16[192,640]{1,0:T(8,128)(2,1)S(1)} %get-tuple-element.76.refs_3_, ...), custom_call_target="tpu_custom_call" | custom-call | flops 20000000000 | bytes 1 | tf_op jit(solution)/shard_map/attend_part/pallas_call | solution.py:54
  40.7 0.0 collective-permute-done.10.refs_6_
  40.7 0.0 collective-permute-done.11.refs_7_
  40.8 0.0 collective-permute-done.14.refs_10_
  40.8 4.0 %attend_last.2 = (bf16[256,640]{1,0:T(8,128)(2,1)S(1)}, f32[256,128]{1,0:T(8,128)S(1)}, bf16[256,768]{1,0:T(8,128)(2,1)S(1)}) custom-call(bf16[384,640]{1,0:T(8,128)(2,1)S(1)} %copy-done, bf16[384,640]{1,0:T(8,128)(2,1)S(1)} %collective-permute-done.5.refs_1_, f32[512,640]{1,0:T(8,128)S(1)} %get-tuple-element.88.refs_2_, ...), custom_call_target="tpu_custom_call" | custom-call | flops 1 | bytes 1 | tf_op jit(solution)/shard_map/attend_last/pallas_call | solution.py:54
  44.7 0.3 collective-permute-start.15
  45.1 2.4 %attend_last.3 = (bf16[128,640]{1,0:T(8,128)(2,1)S(1)}, f32[128,128]{1,0:T(8,128)S(1)}, bf16[128,768]{1,0:T(8,128)(2,1)S(1)}) custom-call(bf16[384,640]{1,0:T(8,128)(2,1)S(1)} %copy-done, bf16[384,640]{1,0:T(8,128)(2,1)S(1)} %collective-permute-done.5.refs_1_, f32[256,640]{1,0:T(8,128)S(1)} %get-tuple-element.97.refs_2_, ...), custom_call_target="tpu_custom_call" | custom-call | flops 1 | bytes 1 | tf_op jit(solution)/shard_map/attend_last/pallas_call | solution.py:54
  47.5 0.6 collective-permute-start.16
  48.1 0.0 collective-permute-done.15.got
  48.1 1.2 %project_send.2 = (bf16[256,640]{1,0:T(8,128)(2,1)S(1)}, bf16[256,640]{1,0:T(8,128)(2,1)S(1)}, bf16[256,640]{1,0:T(8,128)(2,1)S(1)}) custom-call(s32[1]{0:T(128)} %bitcast.place, bf16[256,640]{1,0:T(8,128)(2,1)S(1)} %get-tuple-element.93.own, f32[256,128]{1,0:T(8,128)S(1)} %get-tuple-element.94.own_log, bf16[256,768]{1,0:T(8,128)(2,1)S(1)} %collective-permute-done.15.got, ...), custom_call_target="tpu_custom_call" | custom-call | flops 1 | bytes 1 | tf_op jit(solution)/shard_map/project_send/pallas_call | solution.py:54
  49.4 0.0 collective-permute-done.16.got
  49.4 1.6 %collective-permute-start.20 = (bf16[256,640]{1,0:T(8,128)(2,1)S(1)}, bf16[256,640]{1,0:T(8,128)(2,1)S(1)}, u32[]{:S(2)}, u32[]{:S(2)}) collective-permute-start(bf16[256,640]{1,0:T(8,128)(2,1)S(1)} %get-tuple-element.116), channel_id=1, source_target_pairs={{0,2},{1,3},{2,4},{3,5},{4,6},{5,7},{6,0},{7,1},{8,10},{9,11},{10,... | collective-permute-start | bytes 983048 | tf_op jit(solution)/shard_map/ppermute | solution.py:388
  50.9 1.8 %collective-permute-start.21 = (bf16[256,640]{1,0:T(8,128)(2,1)S(1)}, bf16[256,640]{1,0:T(8,128)(2,1)S(1)}, u32[]{:S(2)}, u32[]{:S(2)}) collective-permute-start(bf16[256,640]{1,0:T(8,128)(2,1)S(1)} %get-tuple-element.117), channel_id=1, source_target_pairs={{0,6},{1,7},{2,0},{3,1},{4,2},{5,3},{6,4},{7,5},{8,14},{9,15},{10,... | collective-permute-start | bytes 983048 | tf_op jit(solution)/shard_map/ppermute | solution.py:387
  52.7 1.1 %project_send.3 = (bf16[512,640]{1,0:T(8,128)(2,1)S(1)}, bf16[128,640]{1,0:T(8,128)(2,1)S(1)}) custom-call(s32[1]{0:T(128)} %bitcast.place, bf16[128,640]{1,0:T(8,128)(2,1)S(1)} %get-tuple-element.104.own, f32[128,128]{1,0:T(8,128)S(1)} %get-tuple-element.105.own_log, bf16[128,768]{1,0:T(8,128)(2,1)S(1)} %collective-permute-done.16.got, ...), custom_call_target="tpu_custom_call" | custom-call | flops 20000000000 | bytes 1 | tf_op jit(solution)/shard_map/project_send/pallas_call | solution.py:54
  53.8 2.4 %collective-permute-start.19 = (bf16[512,640]{1,0:T(8,128)(2,1)S(1)}, bf16[512,640]{1,0:T(8,128)(2,1)S(1)}, u32[]{:S(2)}, u32[]{:S(2)}) collective-permute-start(bf16[512,640]{1,0:T(8,128)(2,1)S(1)} %get-tuple-element.114), channel_id=1, source_target_pairs={{0,1},{1,0},{2,3},{3,2},{4,5},{5,4},{6,7},{7,6},{8,9},{9,8},{10,11... | collective-permute-start | bytes 1966088 | tf_op jit(solution)/shard_map/ppermute | solution.py:46
  56.2 0.8 project_keep.3
  57.0 0.3 collective-permute-start.17
  57.3 3.0 %collective-permute-start.18 = (bf16[256,640]{1,0:T(8,128)(2,1)S(1)}, bf16[256,640]{1,0:T(8,128)(2,1)S(1)}, u32[]{:S(2)}, u32[]{:S(2)}) collective-permute-start(bf16[256,640]{1,0:T(8,128)(2,1)S(1)} %get-tuple-element.112), channel_id=1, source_target_pairs={{0,6},{1,7},{2,0},{3,1},{4,2},{5,3},{6,4},{7,5},{8,14},{9,15},{10,... | collective-permute-start | bytes 983048 | tf_op jit(solution)/shard_map/ppermute | solution.py:393
  60.3 1.3 %project_keep.4.kept = f32[1024,640]{1,0:T(8,128)S(1)} custom-call(s32[1]{0:T(128)} %bitcast.place, bf16[256,640]{1,0:T(8,128)(2,1)S(1)} %get-tuple-element.110.att, bf16[640,5120]{1,0:T(8,128)(2,1)S(1)} %bitcast.2), custom_call_target="tpu_custom_call" | custom-call | flops 1 | bytes 1 | tf_op jit(solution)/shard_map/project_keep/pallas_call | solution.py:54
  61.6 0.2 relay.1
  61.8 2.0 %collective-permute-start.22 = (bf16[256,640]{1,0:T(8,128)(2,1)S(1)}, bf16[256,640]{1,0:T(8,128)(2,1)S(1)}, u32[]{:S(2)}, u32[]{:S(2)}) collective-permute-start(bf16[256,640]{1,0:T(8,128)(2,1)S(1)} %get-tuple-element.118), channel_id=1, source_target_pairs={{0,6},{1,7},{2,0},{3,1},{4,2},{5,3},{6,4},{7,5},{8,14},{9,15},{10,... | collective-permute-start | bytes 983048 | tf_op jit(solution)/shard_map/ppermute | solution.py:400
  63.8 0.1 collective-permute-start.23
  63.9 4.8 %collective-permute-done.17.next_left = bf16[256,640]{1,0:T(8,128)(2,1)S(1)} collective-permute-done((bf16[256,640]{1,0:T(8,128)(2,1)S(1)}, bf16[256,640]{1,0:T(8,128)(2,1)S(1)}, u32[]{:S(2)}, u32[]{:S(2)}) %collective-permute-start.17) | collective-permute-done | bytes 327712 | tf_op jit(solution)/shard_map/ppermute | solution.py:392
  68.7 0.8 project_keep.5.kept
  69.5 2.0 %collective-permute-done.19.got = bf16[512,640]{1,0:T(8,128)(2,1)S(1)} collective-permute-done((bf16[512,640]{1,0:T(8,128)(2,1)S(1)}, bf16[512,640]{1,0:T(8,128)(2,1)S(1)}, u32[]{:S(2)}, u32[]{:S(2)}) %collective-permute-start.19) | collective-permute-done | bytes 655392 | tf_op jit(solution)/shard_map/ppermute | solution.py:46
  71.6 0.1 spread.1
  71.7 2.7 %collective-permute-done.22.on_left = bf16[256,640]{1,0:T(8,128)(2,1)S(1)} collective-permute-done((bf16[256,640]{1,0:T(8,128)(2,1)S(1)}, bf16[256,640]{1,0:T(8,128)(2,1)S(1)}, u32[]{:S(2)}, u32[]{:S(2)}) %collective-permute-start.22) | collective-permute-done | bytes 327712 | tf_op jit(solution)/shard_map/ppermute | solution.py:400
  74.4 0.1 turn.1
  74.5 2.4 %collective-permute-start.24 = (bf16[256,640]{1,0:T(8,128)(2,1)S(1)}, bf16[256,640]{1,0:T(8,128)(2,1)S(1)}, u32[]{:S(2)}, u32[]{:S(2)}) collective-permute-start(bf16[256,640]{1,0:T(8,128)(2,1)S(1)} %turn.1), channel_id=1, source_target_pairs={{0,1},{1,0},{2,3},{3,2},{4,5},{5,4},{6,7},{7,6},{8,9},{9,8},{10,11... | collective-permute-start | bytes 983048 | tf_op jit(solution)/shard_map/ppermute | solution.py:46
  76.9 2.7 %collective-permute-start.25 = (bf16[128,640]{1,0:T(8,128)(2,1)S(1)}, bf16[128,640]{1,0:T(8,128)(2,1)S(1)}, u32[]{:S(2)}, u32[]{:S(2)}) collective-permute-start(bf16[128,640]{1,0:T(8,128)(2,1)S(1)} %get-tuple-element.126), channel_id=1, source_target_pairs={{0,4},{1,5},{2,6},{3,7},{4,0},{5,1},{6,2},{7,3},{8,12},{9,13},{10,... | collective-permute-start | bytes 491528 | tf_op jit(solution)/shard_map/ppermute | solution.py:410
  79.7 1.1 %collective-permute-start.26 = (bf16[128,640]{1,0:T(8,128)(2,1)S(1)}, bf16[128,640]{1,0:T(8,128)(2,1)S(1)}, u32[]{:S(2)}, u32[]{:S(2)}) collective-permute-start(bf16[128,640]{1,0:T(8,128)(2,1)S(1)} %get-tuple-element.127), channel_id=1, source_target_pairs={{0,2},{1,3},{2,4},{3,5},{4,6},{5,7},{6,0},{7,1},{8,10},{9,11},{10,... | collective-permute-start | bytes 491528 | tf_op jit(solution)/shard_map/ppermute | solution.py:410
  80.7 2.2 %collective-permute-start.27 = (bf16[128,640]{1,0:T(8,128)(2,1)S(1)}, bf16[128,640]{1,0:T(8,128)(2,1)S(1)}, u32[]{:S(2)}, u32[]{:S(2)}) collective-permute-start(bf16[128,640]{1,0:T(8,128)(2,1)S(1)} %get-tuple-element.128), channel_id=1, source_target_pairs={{0,6},{1,7},{2,0},{3,1},{4,2},{5,3},{6,4},{7,5},{8,14},{9,15},{10,... | collective-permute-start | bytes 491528 | tf_op jit(solution)/shard_map/ppermute | solution.py:410
  82.9 1.8 %collective-permute-done.24.mine = bf16[256,640]{1,0:T(8,128)(2,1)S(1)} collective-permute-done((bf16[256,640]{1,0:T(8,128)(2,1)S(1)}, bf16[256,640]{1,0:T(8,128)(2,1)S(1)}, u32[]{:S(2)}, u32[]{:S(2)}) %collective-permute-start.24) | collective-permute-done | bytes 327712 | tf_op jit(solution)/shard_map/ppermute | solution.py:46
  84.7 0.2 below.1
  84.9 0.2 collective-permute-done.25.refs_0_
  85.1 2.0 %collective-permute-done.26.refs_1_ = bf16[128,640]{1,0:T(8,128)(2,1)S(1)} collective-permute-done((bf16[128,640]{1,0:T(8,128)(2,1)S(1)}, bf16[128,640]{1,0:T(8,128)(2,1)S(1)}, u32[]{:S(2)}, u32[]{:S(2)}) %collective-permute-start.26) | collective-permute-done | bytes 163872 | tf_op jit(solution)/shard_map/ppermute | solution.py:410
  87.1 0.9 last.1
  (18 shorter events, 0.0 us)
Async XLA Ops:
  0.9 9.4 %collective-permute-start = (bf16[96,640]{1,0:T(8,128)(2,1)S(1)}, bf16[96,640]{1,0:T(8,128)(2,1)S(1)}, u32[]{:S(2)}, u32[]{:S(2)}) collective-permute-start(bf16[96,640]{1,0:T(8,128)(2,1)S(1)} %stacked.5.refs_0_.refs_7_), channel_id=1, source_target_pairs={{0,112},{8,120},{16,32},{24,40},{32,16},{40,24},{48,64},{56,72},{6... | collective-permute-start | bytes 368648 | tf_op jit(solution)/shard_map/ppermute | solution.py:325
  6.8 6.2 %collective-permute-start.2 = (bf16[96,640]{1,0:T(8,128)(2,1)S(1)}, bf16[96,640]{1,0:T(8,128)(2,1)S(1)}, u32[]{:S(2)}, u32[]{:S(2)}) collective-permute-start(bf16[96,640]{1,0:T(8,128)(2,1)S(1)} %stacked.5.refs_0_.refs_7_), channel_id=1, source_target_pairs={{0,16},{8,24},{16,0},{24,8},{32,48},{40,56},{48,32},{56,40},{64,80... | collective-permute-start | bytes 368648 | tf_op jit(solution)/shard_map/ppermute | solution.py:46
  8.2 10.1 %collective-permute-start.4 = (bf16[192,640]{1,0:T(8,128)(2,1)S(1)}, bf16[192,640]{1,0:T(8,128)(2,1)S(1)}, u32[]{:S(2)}, u32[]{:S(2)}) collective-permute-start(bf16[192,640]{1,0:T(8,128)(2,1)S(1)} %get-tuple-element.71.refs_2_), channel_id=1, source_target_pairs={{0,16},{8,24},{16,0},{24,8},{32,48},{40,56},{48,32},{56,40},{64,80... | collective-permute-start | bytes 737288 | tf_op jit(solution)/shard_map/ppermute | solution.py:46
  10.3 10.6 %collective-permute-start.5 = (bf16[384,640]{1,0:T(8,128)(2,1)}, bf16[384,640]{1,0:T(8,128)(2,1)S(1)}, u32[]{:S(2)}, u32[]{:S(2)}) collective-permute-start(bf16[384,640]{1,0:T(8,128)(2,1)} %refs_0_.9), channel_id=1, source_target_pairs={{0,8},{8,0},{16,24},{24,16},{32,40},{40,32},{48,56},{56,48},{64,72... | collective-permute-start | bytes 1474568 | tf_op jit(solution)/shard_map/ppermute | solution.py:46
  10.3 10.6 %collective-permute-start.1 = (bf16[96,640]{1,0:T(8,128)(2,1)S(1)}, bf16[96,640]{1,0:T(8,128)(2,1)S(1)}, u32[]{:S(2)}, u32[]{:S(2)}) collective-permute-start(bf16[96,640]{1,0:T(8,128)(2,1)S(1)} %collective-permute-done.refs_2_.refs_10_), channel_id=1, source_target_pairs={{0,16},{8,24},{16,0},{24,8},{32,48},{40,56},{48,32},{56,40},{64,80... | collective-permute-start | bytes 368648 | tf_op jit(solution)/shard_map/ppermute | solution.py:46
  13.0 7.9 %collective-permute-start.3 = (bf16[96,640]{1,0:T(8,128)(2,1)S(1)}, bf16[96,640]{1,0:T(8,128)(2,1)S(1)}, u32[]{:S(2)}, u32[]{:S(2)}) collective-permute-start(bf16[96,640]{1,0:T(8,128)(2,1)S(1)} %collective-permute-done.2.refs_1_.refs_8_), channel_id=1, source_target_pairs={{0,112},{8,120},{16,32},{24,40},{32,16},{40,24},{48,64},{56,72},{6... | collective-permute-start | bytes 368648 | tf_op jit(solution)/shard_map/ppermute | solution.py:345
  13.6 12.6 %collective-permute-start.8 = (bf16[192,640]{1,0:T(8,128)(2,1)S(1)}, bf16[192,640]{1,0:T(8,128)(2,1)S(1)}, u32[]{:S(2)}, u32[]{:S(2)}) collective-permute-start(bf16[192,640]{1,0:T(8,128)(2,1)S(1)} %get-tuple-element.76.refs_3_), channel_id=1, source_target_pairs={{0,16},{8,24},{16,0},{24,8},{32,48},{40,56},{48,32},{56,40},{64,80... | collective-permute-start | bytes 737288 | tf_op jit(solution)/shard_map/ppermute | solution.py:46
  18.2 14.0 %collective-permute-start.9 = (bf16[288,640]{1,0:T(8,128)(2,1)S(1)}, bf16[288,640]{1,0:T(8,128)(2,1)S(1)}, u32[]{:S(2)}, u32[]{:S(2)}) collective-permute-start(bf16[288,640]{1,0:T(8,128)(2,1)S(1)} %stacked.7), channel_id=1, source_target_pairs={{0,128},{8,136},{16,144},{24,152},{32,160},{40,168},{48,176},{56,1... | collective-permute-start | bytes 1105928 | tf_op jit(solution)/shard_map/ppermute | solution.py:46
  20.9 7.9 %collective-permute-start.6 = (bf16[96,640]{1,0:T(8,128)(2,1)S(1)}, bf16[96,640]{1,0:T(8,128)(2,1)S(1)}, u32[]{:S(2)}, u32[]{:S(2)}) collective-permute-start(bf16[96,640]{1,0:T(8,128)(2,1)S(1)} %collective-permute-done.3.refs_1_.refs_11_), channel_id=1, source_target_pairs={{0,16},{8,24},{16,0},{24,8},{32,48},{40,56},{48,32},{56,40},{64,80... | collective-permute-start | bytes 368648 | tf_op jit(solution)/shard_map/ppermute | solution.py:46
  21.8 6.9 %collective-permute-start.7 = (bf16[96,640]{1,0:T(8,128)(2,1)S(1)}, bf16[96,640]{1,0:T(8,128)(2,1)S(1)}, u32[]{:S(2)}, u32[]{:S(2)}) collective-permute-start(bf16[96,640]{1,0:T(8,128)(2,1)S(1)} %collective-permute-done.1.refs_0_.refs_9_), channel_id=1, source_target_pairs={{0,112},{8,120},{16,32},{24,40},{32,16},{40,24},{48,64},{56,72},{6... | collective-permute-start | bytes 368648 | tf_op jit(solution)/shard_map/ppermute | solution.py:345
  23.1 11.0 %copy-start = (bf16[384,640]{1,0:T(8,128)(2,1)S(1)}, bf16[384,640]{1,0:T(8,128)(2,1)}, u32[]{:S(2)}) copy-start(bf16[384,640]{1,0:T(8,128)(2,1)} %refs_0_.9) | copy-start | bytes 1474564
  23.1 17.6 %collective-permute-start.14 = (bf16[384,640]{1,0:T(8,128)(2,1)S(1)}, bf16[384,640]{1,0:T(8,128)(2,1)S(1)}, u32[]{:S(2)}, u32[]{:S(2)}) collective-permute-start(bf16[384,640]{1,0:T(8,128)(2,1)S(1)} %get-tuple-element.80.refs_4_), channel_id=1, source_target_pairs={{0,16},{8,24},{16,0},{24,8},{32,48},{40,56},{48,32},{56,40},{64,80... | collective-permute-start | bytes 1474568 | tf_op jit(solution)/shard_map/ppermute | solution.py:46
  26.1 14.6 %collective-permute-start.12 = (bf16[192,640]{1,0:T(8,128)(2,1)S(1)}, bf16[192,640]{1,0:T(8,128)(2,1)S(1)}, u32[]{:S(2)}, u32[]{:S(2)}) collective-permute-start(bf16[192,640]{1,0:T(8,128)(2,1)S(1)} %stacked.8), channel_id=1, source_target_pairs={{0,128},{8,136},{16,144},{24,152},{32,160},{40,168},{48,176},{56,1... | collective-permute-start | bytes 737288 | tf_op jit(solution)/shard_map/ppermute | solution.py:46
  28.8 11.9 %collective-permute-start.10 = (bf16[96,640]{1,0:T(8,128)(2,1)S(1)}, bf16[96,640]{1,0:T(8,128)(2,1)S(1)}, u32[]{:S(2)}, u32[]{:S(2)}) collective-permute-start(bf16[96,640]{1,0:T(8,128)(2,1)S(1)} %collective-permute-done.6.refs_0_.refs_4_), channel_id=1, source_target_pairs={{0,112},{8,120},{16,32},{24,40},{32,16},{40,24},{48,64},{56,72},{6... | collective-permute-start | bytes 368648 | tf_op jit(solution)/shard_map/ppermute | solution.py:345
  29.7 11.0 %collective-permute-start.11 = (bf16[96,640]{1,0:T(8,128)(2,1)S(1)}, bf16[96,640]{1,0:T(8,128)(2,1)S(1)}, u32[]{:S(2)}, u32[]{:S(2)}) collective-permute-start(bf16[96,640]{1,0:T(8,128)(2,1)S(1)} %collective-permute-done.6.refs_0_.refs_4_), channel_id=1, source_target_pairs={{0,240},{8,248},{16,160},{24,168},{32,144},{40,152},{48,192},{56,2... | collective-permute-start | bytes 368648 | tf_op jit(solution)/shard_map/ppermute | solution.py:347
  32.2 8.5 %collective-permute-start.13 = (bf16[192,640]{1,0:T(8,128)(2,1)S(1)}, bf16[192,640]{1,0:T(8,128)(2,1)S(1)}, u32[]{:S(2)}, u32[]{:S(2)}) collective-permute-start(bf16[192,640]{1,0:T(8,128)(2,1)S(1)} %stacked.9), channel_id=1, source_target_pairs={{0,128},{8,136},{16,144},{24,152},{32,160},{40,168},{48,176},{56,1... | collective-permute-start | bytes 737288 | tf_op jit(solution)/shard_map/ppermute | solution.py:46
  34.1 14.0 %slice-start = ((s8[6553600]{0:T(1024)(128)(4,1)}), s8[4194304]{0:T(1024)(128)(4,1)S(1)}, s32[]{:S(2)}) async-start(s8[6553600]{0:T(1024)(128)(4,1)} %bitcast.1), calls=%async_computation | async-start | bytes 8388608
  36.6 11.5 %slice-start.1 = ((s8[6553600]{0:T(1024)(128)(4,1)}), s8[2359296]{0:T(1024)(128)(4,1)S(1)}, s32[]{:S(2)}) async-start(s8[6553600]{0:T(1024)(128)(4,1)} %bitcast.1), calls=%async_computation.1 | async-start | bytes 4718592
  44.7 3.4 %collective-permute-start.15 = (bf16[256,768]{1,0:T(8,128)(2,1)S(1)}, bf16[256,768]{1,0:T(8,128)(2,1)S(1)}, u32[]{:S(2)}, u32[]{:S(2)}) collective-permute-start(bf16[256,768]{1,0:T(8,128)(2,1)S(1)} %get-tuple-element.95), channel_id=1, source_target_pairs={{0,8},{8,0},{16,24},{24,16},{32,40},{40,32},{48,56},{56,48},{64,72... | collective-permute-start | bytes 1179656 | tf_op jit(solution)/shard_map/ppermute | solution.py:46
  47.5 1.8 %collective-permute-start.16 = (bf16[128,768]{1,0:T(8,128)(2,1)S(1)}, bf16[128,768]{1,0:T(8,128)(2,1)S(1)}, u32[]{:S(2)}, u32[]{:S(2)}) collective-permute-start(bf16[128,768]{1,0:T(8,128)(2,1)S(1)} %get-tuple-element.101), channel_id=1, source_target_pairs={{0,8},{8,0},{16,24},{24,16},{32,40},{40,32},{48,56},{56,48},{64,72... | collective-permute-start | bytes 589832 | tf_op jit(solution)/shard_map/ppermute | solution.py:46
  49.4 12.2 %collective-permute-start.20 = (bf16[256,640]{1,0:T(8,128)(2,1)S(1)}, bf16[256,640]{1,0:T(8,128)(2,1)S(1)}, u32[]{:S(2)}, u32[]{:S(2)}) collective-permute-start(bf16[256,640]{1,0:T(8,128)(2,1)S(1)} %get-tuple-element.116), channel_id=1, source_target_pairs={{0,2},{1,3},{2,4},{3,5},{4,6},{5,7},{6,0},{7,1},{8,10},{9,11},{10,... | collective-permute-start | bytes 983048 | tf_op jit(solution)/shard_map/ppermute | solution.py:388
  50.9 10.7 %collective-permute-start.21 = (bf16[256,640]{1,0:T(8,128)(2,1)S(1)}, bf16[256,640]{1,0:T(8,128)(2,1)S(1)}, u32[]{:S(2)}, u32[]{:S(2)}) collective-permute-start(bf16[256,640]{1,0:T(8,128)(2,1)S(1)} %get-tuple-element.117), channel_id=1, source_target_pairs={{0,6},{1,7},{2,0},{3,1},{4,2},{5,3},{6,4},{7,5},{8,14},{9,15},{10,... | collective-permute-start | bytes 983048 | tf_op jit(solution)/shard_map/ppermute | solution.py:387
  53.8 17.8 %collective-permute-start.19 = (bf16[512,640]{1,0:T(8,128)(2,1)S(1)}, bf16[512,640]{1,0:T(8,128)(2,1)S(1)}, u32[]{:S(2)}, u32[]{:S(2)}) collective-permute-start(bf16[512,640]{1,0:T(8,128)(2,1)S(1)} %get-tuple-element.114), channel_id=1, source_target_pairs={{0,1},{1,0},{2,3},{3,2},{4,5},{5,4},{6,7},{7,6},{8,9},{9,8},{10,11... | collective-permute-start | bytes 1966088 | tf_op jit(solution)/shard_map/ppermute | solution.py:46
  57.0 11.7 %collective-permute-start.17 = (bf16[256,640]{1,0:T(8,128)(2,1)S(1)}, bf16[256,640]{1,0:T(8,128)(2,1)S(1)}, u32[]{:S(2)}, u32[]{:S(2)}) collective-permute-start(bf16[256,640]{1,0:T(8,128)(2,1)S(1)} %get-tuple-element.109), channel_id=1, source_target_pairs={{0,2},{1,3},{2,4},{3,5},{4,6},{5,7},{6,0},{7,1},{8,10},{9,11},{10,... | collective-permute-start | bytes 983048 | tf_op jit(solution)/shard_map/ppermute | solution.py:392
  57.3 11.4 %collective-permute-start.18 = (bf16[256,640]{1,0:T(8,128)(2,1)S(1)}, bf16[256,640]{1,0:T(8,128)(2,1)S(1)}, u32[]{:S(2)}, u32[]{:S(2)}) collective-permute-start(bf16[256,640]{1,0:T(8,128)(2,1)S(1)} %get-tuple-element.112), channel_id=1, source_target_pairs={{0,6},{1,7},{2,0},{3,1},{4,2},{5,3},{6,4},{7,5},{8,14},{9,15},{10,... | collective-permute-start | bytes 983048 | tf_op jit(solution)/shard_map/ppermute | solution.py:393
  61.8 12.6 %collective-permute-start.22 = (bf16[256,640]{1,0:T(8,128)(2,1)S(1)}, bf16[256,640]{1,0:T(8,128)(2,1)S(1)}, u32[]{:S(2)}, u32[]{:S(2)}) collective-permute-start(bf16[256,640]{1,0:T(8,128)(2,1)S(1)} %get-tuple-element.118), channel_id=1, source_target_pairs={{0,6},{1,7},{2,0},{3,1},{4,2},{5,3},{6,4},{7,5},{8,14},{9,15},{10,... | collective-permute-start | bytes 983048 | tf_op jit(solution)/shard_map/ppermute | solution.py:400
  63.8 10.6 %collective-permute-start.23 = (bf16[256,640]{1,0:T(8,128)(2,1)S(1)}, bf16[256,640]{1,0:T(8,128)(2,1)S(1)}, u32[]{:S(2)}, u32[]{:S(2)}) collective-permute-start(bf16[256,640]{1,0:T(8,128)(2,1)S(1)} %get-tuple-element.119), channel_id=1, source_target_pairs={{0,2},{1,3},{2,4},{3,5},{4,6},{5,7},{6,0},{7,1},{8,10},{9,11},{10,... | collective-permute-start | bytes 983048 | tf_op jit(solution)/shard_map/ppermute | solution.py:399
  74.5 10.2 %collective-permute-start.24 = (bf16[256,640]{1,0:T(8,128)(2,1)S(1)}, bf16[256,640]{1,0:T(8,128)(2,1)S(1)}, u32[]{:S(2)}, u32[]{:S(2)}) collective-permute-start(bf16[256,640]{1,0:T(8,128)(2,1)S(1)} %turn.1), channel_id=1, source_target_pairs={{0,1},{1,0},{2,3},{3,2},{4,5},{5,4},{6,7},{7,6},{8,9},{9,8},{10,11... | collective-permute-start | bytes 983048 | tf_op jit(solution)/shard_map/ppermute | solution.py:46
  76.9 8.1 %collective-permute-start.25 = (bf16[128,640]{1,0:T(8,128)(2,1)S(1)}, bf16[128,640]{1,0:T(8,128)(2,1)S(1)}, u32[]{:S(2)}, u32[]{:S(2)}) collective-permute-start(bf16[128,640]{1,0:T(8,128)(2,1)S(1)} %get-tuple-element.126), channel_id=1, source_target_pairs={{0,4},{1,5},{2,6},{3,7},{4,0},{5,1},{6,2},{7,3},{8,12},{9,13},{10,... | collective-permute-start | bytes 491528 | tf_op jit(solution)/shard_map/ppermute | solution.py:410
  79.7 7.4 %collective-permute-start.26 = (bf16[128,640]{1,0:T(8,128)(2,1)S(1)}, bf16[128,640]{1,0:T(8,128)(2,1)S(1)}, u32[]{:S(2)}, u32[]{:S(2)}) collective-permute-start(bf16[128,640]{1,0:T(8,128)(2,1)S(1)} %get-tuple-element.127), channel_id=1, source_target_pairs={{0,2},{1,3},{2,4},{3,5},{4,6},{5,7},{6,0},{7,1},{8,10},{9,11},{10,... | collective-permute-start | bytes 491528 | tf_op jit(solution)/shard_map/ppermute | solution.py:410
  80.7 6.4 %collective-permute-start.27 = (bf16[128,640]{1,0:T(8,128)(2,1)S(1)}, bf16[128,640]{1,0:T(8,128)(2,1)S(1)}, u32[]{:S(2)}, u32[]{:S(2)}) collective-permute-start(bf16[128,640]{1,0:T(8,128)(2,1)S(1)} %get-tuple-element.128), channel_id=1, source_target_pairs={{0,6},{1,7},{2,0},{3,1},{4,2},{5,3},{6,4},{7,5},{8,14},{9,15},{10,... | collective-permute-start | bytes 491528 | tf_op jit(solution)/shard_map/ppermute | solution.py:410

commit v6 on v5

--- a/solution.py
+++ b/solution.py
@@ -407,7 +407,8 @@
     *spread, rest = local(
         spread_kernel, [(part, BF16)] * 3 + [(part, F32)], last_kept, got_across, name="spread"
     )
-    others = [lax.ppermute(a, "head", along_x(step)) for a, step in zip(spread, (2, 1, X - 1))]
+    sends = tuple(zip(spread, (2, 1, X - 1)))
+    others = [lax.ppermute(a, "head", along_x(step)) for a, step in (*sends[1:], sends[0])]
     kept, rest, on_left, on_right = lax.optimization_barrier((kept, rest, on_left, on_right))
     (turned,) = local(
         turn_kernel, [((CUT, width), BF16)], kept, next_left, on_left, cost=AFTER_STARTS, name="turn"

time: 89.2 us -> 89.2 us (level)
  waiting for transfers between devices: 26.5 us -> 28.2 us
  starting transfers between devices: 38.2 us -> 37 us
    ppermute x14, waiting for transfers between devices: 16.7 us -> 17.9 us  [swap(): lax.ppermute(value, axis, [(i, i ^ bit) for i in range(lax.axis_size(axis...]
    ppermute x3, starting transfers between devices: 5.97 us -> 4.76 us  [body(): lax.ppermute(a, 'head', along_x(step))]
  transfers between devices with their start and end apart: 28 -> 28, of which waited for: 11 -> 11; matrix products, arithmetic and copies ran while one was open for 0% -> 0% of each run, Pallas kernels for 20% -> 19%
where the time goes in v6:
time: 89.2 us; the launch traced here: 88.5 us
  starting transfers between devices  37 us (41%)
  waiting for transfers between devices  28.2 us (32%)
  Pallas kernels  23 us (26%)
    pallas_call x13, Pallas kernels, local(): pl.pallas_call(kernel, in_specs=[pl.BlockSpec(memory_space=pltpu.SMEM)] *...  18.8 us
    ppermute x14, waiting for transfers between devices, swap(): lax.ppermute(value, axis, [(i, i ^ bit) for i in range(lax.axis_size(axis...  17.9 us
    ppermute x14, starting transfers between devices, swap(): lax.ppermute(value, axis, [(i, i ^ bit) for i in range(lax.axis_size(axis...  13.4 us
    ppermute x1, starting transfers between devices, body(): outer = [lax.ppermute(own, 'seq', between)]  5.94 us
    ppermute x1, waiting for transfers between devices, body(): next_left = lax.ppermute(next_go_right, 'head', right_x)  4.8 us
    ppermute x3, starting transfers between devices, body(): lax.ppermute(a, 'head', along_x(step))  4.76 us
    pallas_call x5, Pallas kernels, stacked(): pl.pallas_call(functools.partial(stack_kernel, parts, len(arrays)), in_sp...  3.31 us
    ppermute x1, starting transfers between devices, body(): next_right = lax.ppermute(next_go_left, 'head', left_x)  2.96 us
  transfers between devices with their start and end apart: 28, of which 11 were waited for; matrix products, arithmetic and copies ran while one was open for 0% of the time, Pallas kernels for 19%

profile of v6, /device:TPU:8, one launch (start us, length us, event | category | flops | bytes accessed | tf_op | source)
XLA Modules:
  0.0 88.5 jit_solution(15243724005335199678)
XLA Ops:
  0.0 0.9 stacked.5.refs_0_.refs_7_
  0.9 5.9 %collective-permute-start = (bf16[96,640]{1,0:T(8,128)(2,1)S(1)}, bf16[96,640]{1,0:T(8,128)(2,1)S(1)}, u32[]{:S(2)}, u32[]{:S(2)}) collective-permute-start(bf16[96,640]{1,0:T(8,128)(2,1)S(1)} %stacked.5.refs_0_.refs_7_), channel_id=1, source_target_pairs={{0,112},{8,120},{16,32},{24,40},{32,16},{40,24},{48,64},{56,72},{6... | collective-permute-start | bytes 368648 | tf_op jit(solution)/shard_map/ppermute | solution.py:325
  6.8 0.0 collective-permute-start.2
  6.8 1.4 %stacked.6 = (bf16[192,640]{1,0:T(8,128)(2,1)S(1)}, bf16[192,640]{1,0:T(8,128)(2,1)S(1)}, bf16[384,640]{1,0:T(8,128)(2,1)S(1)}) custom-call(bf16[384,640]{1,0:T(8,128)(2,1)} %refs_0_.5, bf16[384,640]{1,0:T(8,128)(2,1)} %refs_1_.2), custom_call_target="tpu_custom_call" | custom-call | flops 1 | bytes 1 | tf_op jit(solution)/shard_map/stacked/pallas_call | solution.py:85
  8.2 2.1 %collective-permute-start.4 = (bf16[192,640]{1,0:T(8,128)(2,1)S(1)}, bf16[192,640]{1,0:T(8,128)(2,1)S(1)}, u32[]{:S(2)}, u32[]{:S(2)}) collective-permute-start(bf16[192,640]{1,0:T(8,128)(2,1)S(1)} %get-tuple-element.71.refs_2_), channel_id=1, source_target_pairs={{0,16},{8,24},{16,0},{24,8},{32,48},{40,56},{48,32},{56,40},{64,80... | collective-permute-start | bytes 737288 | tf_op jit(solution)/shard_map/ppermute | solution.py:46
  10.3 0.2 collective-permute-start.1
  10.5 2.5 %collective-permute-done.2.refs_1_.refs_8_ = bf16[96,640]{1,0:T(8,128)(2,1)S(1)} collective-permute-done((bf16[96,640]{1,0:T(8,128)(2,1)S(1)}, bf16[96,640]{1,0:T(8,128)(2,1)S(1)}, u32[]{:S(2)}, u32[]{:S(2)}) %collective-permute-start.2) | collective-permute-done | bytes 122912 | tf_op jit(solution)/shard_map/ppermute | solution.py:46
  13.0 0.1 collective-permute-start.3
  13.1 0.5 stacked.7
  13.6 0.5 collective-permute-start.8
  14.1 4.2 %collective-permute-done.4.refs_5_ = bf16[192,640]{1,0:T(8,128)(2,1)S(1)} collective-permute-done((bf16[192,640]{1,0:T(8,128)(2,1)S(1)}, bf16[192,640]{1,0:T(8,128)(2,1)S(1)}, u32[]{:S(2)}, u32[]{:S(2)}) %collective-permute-start.4) | collective-permute-done | bytes 245792 | tf_op jit(solution)/shard_map/ppermute | solution.py:46
  18.2 0.4 collective-permute-start.9
  18.7 2.2 %collective-permute-done.1.refs_0_.refs_9_ = bf16[96,640]{1,0:T(8,128)(2,1)S(1)} collective-permute-done((bf16[96,640]{1,0:T(8,128)(2,1)S(1)}, bf16[96,640]{1,0:T(8,128)(2,1)S(1)}, u32[]{:S(2)}, u32[]{:S(2)}) %collective-permute-start.1) | collective-permute-done | bytes 122912 | tf_op jit(solution)/shard_map/ppermute | solution.py:46
  20.9 0.0 collective-permute-done.3.refs_1_.refs_11_
  20.9 1.0 %collective-permute-start.6 = (bf16[96,640]{1,0:T(8,128)(2,1)S(1)}, bf16[96,640]{1,0:T(8,128)(2,1)S(1)}, u32[]{:S(2)}, u32[]{:S(2)}) collective-permute-start(bf16[96,640]{1,0:T(8,128)(2,1)S(1)} %collective-permute-done.3.refs_1_.refs_11_), channel_id=1, source_target_pairs={{0,16},{8,24},{16,0},{24,8},{32,48},{40,56},{48,32},{56,40},{64,80... | collective-permute-start | bytes 368648 | tf_op jit(solution)/shard_map/ppermute | solution.py:46
  21.8 1.0 %collective-permute-start.7 = (bf16[96,640]{1,0:T(8,128)(2,1)S(1)}, bf16[96,640]{1,0:T(8,128)(2,1)S(1)}, u32[]{:S(2)}, u32[]{:S(2)}) collective-permute-start(bf16[96,640]{1,0:T(8,128)(2,1)S(1)} %collective-permute-done.1.refs_0_.refs_9_), channel_id=1, source_target_pairs={{0,112},{8,120},{16,32},{24,40},{32,16},{40,24},{48,64},{56,72},{6... | collective-permute-start | bytes 368648 | tf_op jit(solution)/shard_map/ppermute | solution.py:345
  22.8 0.3 stacked.8
  23.1 0.0 copy-start
  23.1 1.2 %collective-permute-start.14 = (bf16[384,640]{1,0:T(8,128)(2,1)S(1)}, bf16[384,640]{1,0:T(8,128)(2,1)S(1)}, u32[]{:S(2)}, u32[]{:S(2)}) collective-permute-start(bf16[384,640]{1,0:T(8,128)(2,1)S(1)} %get-tuple-element.80.refs_4_), channel_id=1, source_target_pairs={{0,16},{8,24},{16,0},{24,8},{32,48},{40,56},{48,32},{56,40},{64,80... | collective-permute-start | bytes 1474568 | tf_op jit(solution)/shard_map/ppermute | solution.py:46
  24.3 1.8 %collective-permute-done.8.refs_6_ = bf16[192,640]{1,0:T(8,128)(2,1)S(1)} collective-permute-done((bf16[192,640]{1,0:T(8,128)(2,1)S(1)}, bf16[192,640]{1,0:T(8,128)(2,1)S(1)}, u32[]{:S(2)}, u32[]{:S(2)}) %collective-permute-start.8) | collective-permute-done | bytes 245792 | tf_op jit(solution)/shard_map/ppermute | solution.py:46
  26.1 0.4 collective-permute-start.12
  26.6 2.2 %collective-permute-done.6.refs_0_.refs_4_ = bf16[96,640]{1,0:T(8,128)(2,1)S(1)} collective-permute-done((bf16[96,640]{1,0:T(8,128)(2,1)S(1)}, bf16[96,640]{1,0:T(8,128)(2,1)S(1)}, u32[]{:S(2)}, u32[]{:S(2)}) %collective-permute-start.6) | collective-permute-done | bytes 122912 | tf_op jit(solution)/shard_map/ppermute | solution.py:46
  28.8 0.0 collective-permute-done.7.refs_1_.refs_5_
  28.8 0.9 %collective-permute-start.10 = (bf16[96,640]{1,0:T(8,128)(2,1)S(1)}, bf16[96,640]{1,0:T(8,128)(2,1)S(1)}, u32[]{:S(2)}, u32[]{:S(2)}) collective-permute-start(bf16[96,640]{1,0:T(8,128)(2,1)S(1)} %collective-permute-done.6.refs_0_.refs_4_), channel_id=1, source_target_pairs={{0,112},{8,120},{16,32},{24,40},{32,16},{40,24},{48,64},{56,72},{6... | collective-permute-start | bytes 368648 | tf_op jit(solution)/shard_map/ppermute | solution.py:345
  29.7 2.2 %collective-permute-start.11 = (bf16[96,640]{1,0:T(8,128)(2,1)S(1)}, bf16[96,640]{1,0:T(8,128)(2,1)S(1)}, u32[]{:S(2)}, u32[]{:S(2)}) collective-permute-start(bf16[96,640]{1,0:T(8,128)(2,1)S(1)} %collective-permute-done.6.refs_0_.refs_4_), channel_id=1, source_target_pairs={{0,240},{8,248},{16,160},{24,168},{32,144},{40,152},{48,192},{56,2... | collective-permute-start | bytes 368648 | tf_op jit(solution)/shard_map/ppermute | solution.py:347
  31.9 0.3 stacked.9
  32.2 0.0 collective-permute-done.9.refs_12_
  32.2 1.8 %collective-permute-start.13 = (bf16[192,640]{1,0:T(8,128)(2,1)S(1)}, bf16[192,640]{1,0:T(8,128)(2,1)S(1)}, u32[]{:S(2)}, u32[]{:S(2)}) collective-permute-start(bf16[192,640]{1,0:T(8,128)(2,1)S(1)} %stacked.9), channel_id=1, source_target_pairs={{0,128},{8,136},{16,144},{24,152},{32,160},{40,168},{48,176},{56,1... | collective-permute-start | bytes 737288 | tf_op jit(solution)/shard_map/ppermute | solution.py:46
  34.1 2.5 %attend_part.3 = (f32[256,640]{1,0:T(8,128)S(1)}, f32[256,128]{1,0:T(8,128)S(1)}) custom-call(bf16[384,640]{1,0:T(8,128)(2,1)S(1)} %copy-done, bf16[384,640]{1,0:T(8,128)(2,1)S(1)} %collective-permute-done.5.refs_1_, bf16[192,640]{1,0:T(8,128)(2,1)S(1)} %get-tuple-element.71.refs_2_, bf16[192,640]{1,0:T(8,128)(2,1)S(1)} %get-tuple-element.76.refs_3_, ...), custom_call_target="tpu_custom_call" | custom-call | flops 20000000000 | bytes 1 | tf_op jit(solution)/shard_map/attend_part/pallas_call | solution.py:54
  36.6 0.0 slice-start.1
  36.6 4.1 %attend_part.2 = (f32[512,640]{1,0:T(8,128)S(1)}, f32[512,128]{1,0:T(8,128)S(1)}) custom-call(bf16[384,640]{1,0:T(8,128)(2,1)S(1)} %copy-done, bf16[384,640]{1,0:T(8,128)(2,1)S(1)} %collective-permute-done.5.refs_1_, bf16[192,640]{1,0:T(8,128)(2,1)S(1)} %get-tuple-element.71.refs_2_, bf16[192,640]{1,0:T(8,128)(2,1)S(1)} %get-tuple-element.76.refs_3_, ...), custom_call_target="tpu_custom_call" | custom-call | flops 20000000000 | bytes 1 | tf_op jit(solution)/shard_map/attend_part/pallas_call | solution.py:54
  40.7 0.0 collective-permute-done.10.refs_6_
  40.7 0.0 collective-permute-done.13.refs_9_
  40.8 4.0 %attend_last.2 = (bf16[256,640]{1,0:T(8,128)(2,1)S(1)}, f32[256,128]{1,0:T(8,128)S(1)}, bf16[256,768]{1,0:T(8,128)(2,1)S(1)}) custom-call(bf16[384,640]{1,0:T(8,128)(2,1)S(1)} %copy-done, bf16[384,640]{1,0:T(8,128)(2,1)S(1)} %collective-permute-done.5.refs_1_, f32[512,640]{1,0:T(8,128)S(1)} %get-tuple-element.88.refs_2_, ...), custom_call_target="tpu_custom_call" | custom-call | flops 1 | bytes 1 | tf_op jit(solution)/shard_map/attend_last/pallas_call | solution.py:54
  44.7 0.3 collective-permute-start.15
  45.1 2.4 %attend_last.3 = (bf16[128,640]{1,0:T(8,128)(2,1)S(1)}, f32[128,128]{1,0:T(8,128)S(1)}, bf16[128,768]{1,0:T(8,128)(2,1)S(1)}) custom-call(bf16[384,640]{1,0:T(8,128)(2,1)S(1)} %copy-done, bf16[384,640]{1,0:T(8,128)(2,1)S(1)} %collective-permute-done.5.refs_1_, f32[256,640]{1,0:T(8,128)S(1)} %get-tuple-element.97.refs_2_, ...), custom_call_target="tpu_custom_call" | custom-call | flops 1 | bytes 1 | tf_op jit(solution)/shard_map/attend_last/pallas_call | solution.py:54
  47.5 0.6 collective-permute-start.16
  48.1 1.2 %project_send.2 = (bf16[256,640]{1,0:T(8,128)(2,1)S(1)}, bf16[256,640]{1,0:T(8,128)(2,1)S(1)}, bf16[256,640]{1,0:T(8,128)(2,1)S(1)}) custom-call(s32[1]{0:T(128)} %bitcast.place, bf16[256,640]{1,0:T(8,128)(2,1)S(1)} %get-tuple-element.93.own, f32[256,128]{1,0:T(8,128)S(1)} %get-tuple-element.94.own_log, bf16[256,768]{1,0:T(8,128)(2,1)S(1)} %collective-permute-done.15.got, ...), custom_call_target="tpu_custom_call" | custom-call | flops 1 | bytes 1 | tf_op jit(solution)/shard_map/project_send/pallas_call | solution.py:54
  49.4 1.6 %collective-permute-start.20 = (bf16[256,640]{1,0:T(8,128)(2,1)S(1)}, bf16[256,640]{1,0:T(8,128)(2,1)S(1)}, u32[]{:S(2)}, u32[]{:S(2)}) collective-permute-start(bf16[256,640]{1,0:T(8,128)(2,1)S(1)} %get-tuple-element.116), channel_id=1, source_target_pairs={{0,2},{1,3},{2,4},{3,5},{4,6},{5,7},{6,0},{7,1},{8,10},{9,11},{10,... | collective-permute-start | bytes 983048 | tf_op jit(solution)/shard_map/ppermute | solution.py:388
  50.9 1.8 %collective-permute-start.21 = (bf16[256,640]{1,0:T(8,128)(2,1)S(1)}, bf16[256,640]{1,0:T(8,128)(2,1)S(1)}, u32[]{:S(2)}, u32[]{:S(2)}) collective-permute-start(bf16[256,640]{1,0:T(8,128)(2,1)S(1)} %get-tuple-element.117), channel_id=1, source_target_pairs={{0,6},{1,7},{2,0},{3,1},{4,2},{5,3},{6,4},{7,5},{8,14},{9,15},{10,... | collective-permute-start | bytes 983048 | tf_op jit(solution)/shard_map/ppermute | solution.py:387
  52.7 1.1 %project_send.3 = (bf16[512,640]{1,0:T(8,128)(2,1)S(1)}, bf16[128,640]{1,0:T(8,128)(2,1)S(1)}) custom-call(s32[1]{0:T(128)} %bitcast.place, bf16[128,640]{1,0:T(8,128)(2,1)S(1)} %get-tuple-element.104.own, f32[128,128]{1,0:T(8,128)S(1)} %get-tuple-element.105.own_log, bf16[128,768]{1,0:T(8,128)(2,1)S(1)} %collective-permute-done.16.got, ...), custom_call_target="tpu_custom_call" | custom-call | flops 20000000000 | bytes 1 | tf_op jit(solution)/shard_map/project_send/pallas_call | solution.py:54
  53.8 2.4 %collective-permute-start.19 = (bf16[512,640]{1,0:T(8,128)(2,1)S(1)}, bf16[512,640]{1,0:T(8,128)(2,1)S(1)}, u32[]{:S(2)}, u32[]{:S(2)}) collective-permute-start(bf16[512,640]{1,0:T(8,128)(2,1)S(1)} %get-tuple-element.114), channel_id=1, source_target_pairs={{0,1},{1,0},{2,3},{3,2},{4,5},{5,4},{6,7},{7,6},{8,9},{9,8},{10,11... | collective-permute-start | bytes 1966088 | tf_op jit(solution)/shard_map/ppermute | solution.py:46
  56.2 0.8 project_keep.3
  57.0 0.3 collective-permute-start.17
  57.3 3.0 %collective-permute-start.18 = (bf16[256,640]{1,0:T(8,128)(2,1)S(1)}, bf16[256,640]{1,0:T(8,128)(2,1)S(1)}, u32[]{:S(2)}, u32[]{:S(2)}) collective-permute-start(bf16[256,640]{1,0:T(8,128)(2,1)S(1)} %get-tuple-element.112), channel_id=1, source_target_pairs={{0,6},{1,7},{2,0},{3,1},{4,2},{5,3},{6,4},{7,5},{8,14},{9,15},{10,... | collective-permute-start | bytes 983048 | tf_op jit(solution)/shard_map/ppermute | solution.py:393
  60.3 1.3 %project_keep.4.kept = f32[1024,640]{1,0:T(8,128)S(1)} custom-call(s32[1]{0:T(128)} %bitcast.place, bf16[256,640]{1,0:T(8,128)(2,1)S(1)} %get-tuple-element.110.att, bf16[640,5120]{1,0:T(8,128)(2,1)S(1)} %bitcast.2), custom_call_target="tpu_custom_call" | custom-call | flops 1 | bytes 1 | tf_op jit(solution)/shard_map/project_keep/pallas_call | solution.py:54
  61.6 0.2 relay.1
  61.8 2.0 %collective-permute-start.22 = (bf16[256,640]{1,0:T(8,128)(2,1)S(1)}, bf16[256,640]{1,0:T(8,128)(2,1)S(1)}, u32[]{:S(2)}, u32[]{:S(2)}) collective-permute-start(bf16[256,640]{1,0:T(8,128)(2,1)S(1)} %get-tuple-element.118), channel_id=1, source_target_pairs={{0,6},{1,7},{2,0},{3,1},{4,2},{5,3},{6,4},{7,5},{8,14},{9,15},{10,... | collective-permute-start | bytes 983048 | tf_op jit(solution)/shard_map/ppermute | solution.py:400
  63.8 0.1 collective-permute-start.23
  63.9 4.8 %collective-permute-done.17.next_left = bf16[256,640]{1,0:T(8,128)(2,1)S(1)} collective-permute-done((bf16[256,640]{1,0:T(8,128)(2,1)S(1)}, bf16[256,640]{1,0:T(8,128)(2,1)S(1)}, u32[]{:S(2)}, u32[]{:S(2)}) %collective-permute-start.17) | collective-permute-done | bytes 327712 | tf_op jit(solution)/shard_map/ppermute | solution.py:392
  68.7 0.8 project_keep.5.kept
  69.5 2.0 %collective-permute-done.19.got = bf16[512,640]{1,0:T(8,128)(2,1)S(1)} collective-permute-done((bf16[512,640]{1,0:T(8,128)(2,1)S(1)}, bf16[512,640]{1,0:T(8,128)(2,1)S(1)}, u32[]{:S(2)}, u32[]{:S(2)}) %collective-permute-start.19) | collective-permute-done | bytes 655392 | tf_op jit(solution)/shard_map/ppermute | solution.py:46
  71.6 0.1 spread.1
  71.7 2.7 %collective-permute-done.22.on_left = bf16[256,640]{1,0:T(8,128)(2,1)S(1)} collective-permute-done((bf16[256,640]{1,0:T(8,128)(2,1)S(1)}, bf16[256,640]{1,0:T(8,128)(2,1)S(1)}, u32[]{:S(2)}, u32[]{:S(2)}) %collective-permute-start.22) | collective-permute-done | bytes 327712 | tf_op jit(solution)/shard_map/ppermute | solution.py:400
  74.4 0.1 turn.1
  74.5 2.4 %collective-permute-start.24 = (bf16[256,640]{1,0:T(8,128)(2,1)S(1)}, bf16[256,640]{1,0:T(8,128)(2,1)S(1)}, u32[]{:S(2)}, u32[]{:S(2)}) collective-permute-start(bf16[256,640]{1,0:T(8,128)(2,1)S(1)} %turn.1), channel_id=1, source_target_pairs={{0,1},{1,0},{2,3},{3,2},{4,5},{5,4},{6,7},{7,6},{8,9},{9,8},{10,11... | collective-permute-start | bytes 983048 | tf_op jit(solution)/shard_map/ppermute | solution.py:46
  76.9 1.5 %collective-permute-start.25 = (bf16[128,640]{1,0:T(8,128)(2,1)S(1)}, bf16[128,640]{1,0:T(8,128)(2,1)S(1)}, u32[]{:S(2)}, u32[]{:S(2)}) collective-permute-start(bf16[128,640]{1,0:T(8,128)(2,1)S(1)} %get-tuple-element.126), channel_id=1, source_target_pairs={{0,2},{1,3},{2,4},{3,5},{4,6},{5,7},{6,0},{7,1},{8,10},{9,11},{10,... | collective-permute-start | bytes 491528 | tf_op jit(solution)/shard_map/ppermute | solution.py:411
  78.4 1.7 %collective-permute-start.26 = (bf16[128,640]{1,0:T(8,128)(2,1)S(1)}, bf16[128,640]{1,0:T(8,128)(2,1)S(1)}, u32[]{:S(2)}, u32[]{:S(2)}) collective-permute-start(bf16[128,640]{1,0:T(8,128)(2,1)S(1)} %get-tuple-element.127), channel_id=1, source_target_pairs={{0,6},{1,7},{2,0},{3,1},{4,2},{5,3},{6,4},{7,5},{8,14},{9,15},{10,... | collective-permute-start | bytes 491528 | tf_op jit(solution)/shard_map/ppermute | solution.py:411
  80.2 1.5 %collective-permute-start.27 = (bf16[128,640]{1,0:T(8,128)(2,1)S(1)}, bf16[128,640]{1,0:T(8,128)(2,1)S(1)}, u32[]{:S(2)}, u32[]{:S(2)}) collective-permute-start(bf16[128,640]{1,0:T(8,128)(2,1)S(1)} %get-tuple-element.128), channel_id=1, source_target_pairs={{0,4},{1,5},{2,6},{3,7},{4,0},{5,1},{6,2},{7,3},{8,12},{9,13},{10,... | collective-permute-start | bytes 491528 | tf_op jit(solution)/shard_map/ppermute | solution.py:411
  81.7 3.0 %collective-permute-done.24.mine = bf16[256,640]{1,0:T(8,128)(2,1)S(1)} collective-permute-done((bf16[256,640]{1,0:T(8,128)(2,1)S(1)}, bf16[256,640]{1,0:T(8,128)(2,1)S(1)}, u32[]{:S(2)}, u32[]{:S(2)}) %collective-permute-start.24) | collective-permute-done | bytes 327712 | tf_op jit(solution)/shard_map/ppermute | solution.py:46
  84.7 0.2 below.1
  84.9 0.1 collective-permute-done.25.refs_0_
  85.0 2.6 %collective-permute-done.27.refs_2_ = bf16[128,640]{1,0:T(8,128)(2,1)S(1)} collective-permute-done((bf16[128,640]{1,0:T(8,128)(2,1)S(1)}, bf16[128,640]{1,0:T(8,128)(2,1)S(1)}, u32[]{:S(2)}, u32[]{:S(2)}) %collective-permute-start.27) | collective-permute-done | bytes 163872 | tf_op jit(solution)/shard_map/ppermute | solution.py:411
  87.6 0.9 last.1
  (18 shorter events, 0.0 us)
Async XLA Ops:
  0.9 9.4 %collective-permute-start = (bf16[96,640]{1,0:T(8,128)(2,1)S(1)}, bf16[96,640]{1,0:T(8,128)(2,1)S(1)}, u32[]{:S(2)}, u32[]{:S(2)}) collective-permute-start(bf16[96,640]{1,0:T(8,128)(2,1)S(1)} %stacked.5.refs_0_.refs_7_), channel_id=1, source_target_pairs={{0,112},{8,120},{16,32},{24,40},{32,16},{40,24},{48,64},{56,72},{6... | collective-permute-start | bytes 368648 | tf_op jit(solution)/shard_map/ppermute | solution.py:325
  6.8 6.2 %collective-permute-start.2 = (bf16[96,640]{1,0:T(8,128)(2,1)S(1)}, bf16[96,640]{1,0:T(8,128)(2,1)S(1)}, u32[]{:S(2)}, u32[]{:S(2)}) collective-permute-start(bf16[96,640]{1,0:T(8,128)(2,1)S(1)} %stacked.5.refs_0_.refs_7_), channel_id=1, source_target_pairs={{0,16},{8,24},{16,0},{24,8},{32,48},{40,56},{48,32},{56,40},{64,80... | collective-permute-start | bytes 368648 | tf_op jit(solution)/shard_map/ppermute | solution.py:46
  8.2 10.1 %collective-permute-start.4 = (bf16[192,640]{1,0:T(8,128)(2,1)S(1)}, bf16[192,640]{1,0:T(8,128)(2,1)S(1)}, u32[]{:S(2)}, u32[]{:S(2)}) collective-permute-start(bf16[192,640]{1,0:T(8,128)(2,1)S(1)} %get-tuple-element.71.refs_2_), channel_id=1, source_target_pairs={{0,16},{8,24},{16,0},{24,8},{32,48},{40,56},{48,32},{56,40},{64,80... | collective-permute-start | bytes 737288 | tf_op jit(solution)/shard_map/ppermute | solution.py:46
  10.3 10.6 %collective-permute-start.5 = (bf16[384,640]{1,0:T(8,128)(2,1)}, bf16[384,640]{1,0:T(8,128)(2,1)S(1)}, u32[]{:S(2)}, u32[]{:S(2)}) collective-permute-start(bf16[384,640]{1,0:T(8,128)(2,1)} %refs_0_.9), channel_id=1, source_target_pairs={{0,8},{8,0},{16,24},{24,16},{32,40},{40,32},{48,56},{56,48},{64,72... | collective-permute-start | bytes 1474568 | tf_op jit(solution)/shard_map/ppermute | solution.py:46
  10.3 10.6 %collective-permute-start.1 = (bf16[96,640]{1,0:T(8,128)(2,1)S(1)}, bf16[96,640]{1,0:T(8,128)(2,1)S(1)}, u32[]{:S(2)}, u32[]{:S(2)}) collective-permute-start(bf16[96,640]{1,0:T(8,128)(2,1)S(1)} %collective-permute-done.refs_2_.refs_10_), channel_id=1, source_target_pairs={{0,16},{8,24},{16,0},{24,8},{32,48},{40,56},{48,32},{56,40},{64,80... | collective-permute-start | bytes 368648 | tf_op jit(solution)/shard_map/ppermute | solution.py:46
  13.0 7.9 %collective-permute-start.3 = (bf16[96,640]{1,0:T(8,128)(2,1)S(1)}, bf16[96,640]{1,0:T(8,128)(2,1)S(1)}, u32[]{:S(2)}, u32[]{:S(2)}) collective-permute-start(bf16[96,640]{1,0:T(8,128)(2,1)S(1)} %collective-permute-done.2.refs_1_.refs_8_), channel_id=1, source_target_pairs={{0,112},{8,120},{16,32},{24,40},{32,16},{40,24},{48,64},{56,72},{6... | collective-permute-start | bytes 368648 | tf_op jit(solution)/shard_map/ppermute | solution.py:345
  13.6 12.6 %collective-permute-start.8 = (bf16[192,640]{1,0:T(8,128)(2,1)S(1)}, bf16[192,640]{1,0:T(8,128)(2,1)S(1)}, u32[]{:S(2)}, u32[]{:S(2)}) collective-permute-start(bf16[192,640]{1,0:T(8,128)(2,1)S(1)} %get-tuple-element.76.refs_3_), channel_id=1, source_target_pairs={{0,16},{8,24},{16,0},{24,8},{32,48},{40,56},{48,32},{56,40},{64,80... | collective-permute-start | bytes 737288 | tf_op jit(solution)/shard_map/ppermute | solution.py:46
  18.2 14.0 %collective-permute-start.9 = (bf16[288,640]{1,0:T(8,128)(2,1)S(1)}, bf16[288,640]{1,0:T(8,128)(2,1)S(1)}, u32[]{:S(2)}, u32[]{:S(2)}) collective-permute-start(bf16[288,640]{1,0:T(8,128)(2,1)S(1)} %stacked.7), channel_id=1, source_target_pairs={{0,128},{8,136},{16,144},{24,152},{32,160},{40,168},{48,176},{56,1... | collective-permute-start | bytes 1105928 | tf_op jit(solution)/shard_map/ppermute | solution.py:46
  20.9 7.9 %collective-permute-start.6 = (bf16[96,640]{1,0:T(8,128)(2,1)S(1)}, bf16[96,640]{1,0:T(8,128)(2,1)S(1)}, u32[]{:S(2)}, u32[]{:S(2)}) collective-permute-start(bf16[96,640]{1,0:T(8,128)(2,1)S(1)} %collective-permute-done.3.refs_1_.refs_11_), channel_id=1, source_target_pairs={{0,16},{8,24},{16,0},{24,8},{32,48},{40,56},{48,32},{56,40},{64,80... | collective-permute-start | bytes 368648 | tf_op jit(solution)/shard_map/ppermute | solution.py:46
  21.8 6.9 %collective-permute-start.7 = (bf16[96,640]{1,0:T(8,128)(2,1)S(1)}, bf16[96,640]{1,0:T(8,128)(2,1)S(1)}, u32[]{:S(2)}, u32[]{:S(2)}) collective-permute-start(bf16[96,640]{1,0:T(8,128)(2,1)S(1)} %collective-permute-done.1.refs_0_.refs_9_), channel_id=1, source_target_pairs={{0,112},{8,120},{16,32},{24,40},{32,16},{40,24},{48,64},{56,72},{6... | collective-permute-start | bytes 368648 | tf_op jit(solution)/shard_map/ppermute | solution.py:345
  23.1 11.0 %copy-start = (bf16[384,640]{1,0:T(8,128)(2,1)S(1)}, bf16[384,640]{1,0:T(8,128)(2,1)}, u32[]{:S(2)}) copy-start(bf16[384,640]{1,0:T(8,128)(2,1)} %refs_0_.9) | copy-start | bytes 1474564
  23.1 17.6 %collective-permute-start.14 = (bf16[384,640]{1,0:T(8,128)(2,1)S(1)}, bf16[384,640]{1,0:T(8,128)(2,1)S(1)}, u32[]{:S(2)}, u32[]{:S(2)}) collective-permute-start(bf16[384,640]{1,0:T(8,128)(2,1)S(1)} %get-tuple-element.80.refs_4_), channel_id=1, source_target_pairs={{0,16},{8,24},{16,0},{24,8},{32,48},{40,56},{48,32},{56,40},{64,80... | collective-permute-start | bytes 1474568 | tf_op jit(solution)/shard_map/ppermute | solution.py:46
  26.1 14.6 %collective-permute-start.12 = (bf16[192,640]{1,0:T(8,128)(2,1)S(1)}, bf16[192,640]{1,0:T(8,128)(2,1)S(1)}, u32[]{:S(2)}, u32[]{:S(2)}) collective-permute-start(bf16[192,640]{1,0:T(8,128)(2,1)S(1)} %stacked.8), channel_id=1, source_target_pairs={{0,128},{8,136},{16,144},{24,152},{32,160},{40,168},{48,176},{56,1... | collective-permute-start | bytes 737288 | tf_op jit(solution)/shard_map/ppermute | solution.py:46
  28.8 11.9 %collective-permute-start.10 = (bf16[96,640]{1,0:T(8,128)(2,1)S(1)}, bf16[96,640]{1,0:T(8,128)(2,1)S(1)}, u32[]{:S(2)}, u32[]{:S(2)}) collective-permute-start(bf16[96,640]{1,0:T(8,128)(2,1)S(1)} %collective-permute-done.6.refs_0_.refs_4_), channel_id=1, source_target_pairs={{0,112},{8,120},{16,32},{24,40},{32,16},{40,24},{48,64},{56,72},{6... | collective-permute-start | bytes 368648 | tf_op jit(solution)/shard_map/ppermute | solution.py:345
  29.7 11.0 %collective-permute-start.11 = (bf16[96,640]{1,0:T(8,128)(2,1)S(1)}, bf16[96,640]{1,0:T(8,128)(2,1)S(1)}, u32[]{:S(2)}, u32[]{:S(2)}) collective-permute-start(bf16[96,640]{1,0:T(8,128)(2,1)S(1)} %collective-permute-done.6.refs_0_.refs_4_), channel_id=1, source_target_pairs={{0,240},{8,248},{16,160},{24,168},{32,144},{40,152},{48,192},{56,2... | collective-permute-start | bytes 368648 | tf_op jit(solution)/shard_map/ppermute | solution.py:347
  32.2 8.5 %collective-permute-start.13 = (bf16[192,640]{1,0:T(8,128)(2,1)S(1)}, bf16[192,640]{1,0:T(8,128)(2,1)S(1)}, u32[]{:S(2)}, u32[]{:S(2)}) collective-permute-start(bf16[192,640]{1,0:T(8,128)(2,1)S(1)} %stacked.9), channel_id=1, source_target_pairs={{0,128},{8,136},{16,144},{24,152},{32,160},{40,168},{48,176},{56,1... | collective-permute-start | bytes 737288 | tf_op jit(solution)/shard_map/ppermute | solution.py:46
  34.1 14.0 %slice-start = ((s8[6553600]{0:T(1024)(128)(4,1)}), s8[4194304]{0:T(1024)(128)(4,1)S(1)}, s32[]{:S(2)}) async-start(s8[6553600]{0:T(1024)(128)(4,1)} %bitcast.1), calls=%async_computation | async-start | bytes 8388608
  36.6 11.5 %slice-start.1 = ((s8[6553600]{0:T(1024)(128)(4,1)}), s8[2359296]{0:T(1024)(128)(4,1)S(1)}, s32[]{:S(2)}) async-start(s8[6553600]{0:T(1024)(128)(4,1)} %bitcast.1), calls=%async_computation.1 | async-start | bytes 4718592
  44.7 3.4 %collective-permute-start.15 = (bf16[256,768]{1,0:T(8,128)(2,1)S(1)}, bf16[256,768]{1,0:T(8,128)(2,1)S(1)}, u32[]{:S(2)}, u32[]{:S(2)}) collective-permute-start(bf16[256,768]{1,0:T(8,128)(2,1)S(1)} %get-tuple-element.95), channel_id=1, source_target_pairs={{0,8},{8,0},{16,24},{24,16},{32,40},{40,32},{48,56},{56,48},{64,72... | collective-permute-start | bytes 1179656 | tf_op jit(solution)/shard_map/ppermute | solution.py:46
  47.5 1.8 %collective-permute-start.16 = (bf16[128,768]{1,0:T(8,128)(2,1)S(1)}, bf16[128,768]{1,0:T(8,128)(2,1)S(1)}, u32[]{:S(2)}, u32[]{:S(2)}) collective-permute-start(bf16[128,768]{1,0:T(8,128)(2,1)S(1)} %get-tuple-element.101), channel_id=1, source_target_pairs={{0,8},{8,0},{16,24},{24,16},{32,40},{40,32},{48,56},{56,48},{64,72... | collective-permute-start | bytes 589832 | tf_op jit(solution)/shard_map/ppermute | solution.py:46
  49.4 12.2 %collective-permute-start.20 = (bf16[256,640]{1,0:T(8,128)(2,1)S(1)}, bf16[256,640]{1,0:T(8,128)(2,1)S(1)}, u32[]{:S(2)}, u32[]{:S(2)}) collective-permute-start(bf16[256,640]{1,0:T(8,128)(2,1)S(1)} %get-tuple-element.116), channel_id=1, source_target_pairs={{0,2},{1,3},{2,4},{3,5},{4,6},{5,7},{6,0},{7,1},{8,10},{9,11},{10,... | collective-permute-start | bytes 983048 | tf_op jit(solution)/shard_map/ppermute | solution.py:388
  50.9 10.7 %collective-permute-start.21 = (bf16[256,640]{1,0:T(8,128)(2,1)S(1)}, bf16[256,640]{1,0:T(8,128)(2,1)S(1)}, u32[]{:S(2)}, u32[]{:S(2)}) collective-permute-start(bf16[256,640]{1,0:T(8,128)(2,1)S(1)} %get-tuple-element.117), channel_id=1, source_target_pairs={{0,6},{1,7},{2,0},{3,1},{4,2},{5,3},{6,4},{7,5},{8,14},{9,15},{10,... | collective-permute-start | bytes 983048 | tf_op jit(solution)/shard_map/ppermute | solution.py:387
  53.8 17.8 %collective-permute-start.19 = (bf16[512,640]{1,0:T(8,128)(2,1)S(1)}, bf16[512,640]{1,0:T(8,128)(2,1)S(1)}, u32[]{:S(2)}, u32[]{:S(2)}) collective-permute-start(bf16[512,640]{1,0:T(8,128)(2,1)S(1)} %get-tuple-element.114), channel_id=1, source_target_pairs={{0,1},{1,0},{2,3},{3,2},{4,5},{5,4},{6,7},{7,6},{8,9},{9,8},{10,11... | collective-permute-start | bytes 1966088 | tf_op jit(solution)/shard_map/ppermute | solution.py:46
  57.0 11.7 %collective-permute-start.17 = (bf16[256,640]{1,0:T(8,128)(2,1)S(1)}, bf16[256,640]{1,0:T(8,128)(2,1)S(1)}, u32[]{:S(2)}, u32[]{:S(2)}) collective-permute-start(bf16[256,640]{1,0:T(8,128)(2,1)S(1)} %get-tuple-element.109), channel_id=1, source_target_pairs={{0,2},{1,3},{2,4},{3,5},{4,6},{5,7},{6,0},{7,1},{8,10},{9,11},{10,... | collective-permute-start | bytes 983048 | tf_op jit(solution)/shard_map/ppermute | solution.py:392
  57.3 11.4 %collective-permute-start.18 = (bf16[256,640]{1,0:T(8,128)(2,1)S(1)}, bf16[256,640]{1,0:T(8,128)(2,1)S(1)}, u32[]{:S(2)}, u32[]{:S(2)}) collective-permute-start(bf16[256,640]{1,0:T(8,128)(2,1)S(1)} %get-tuple-element.112), channel_id=1, source_target_pairs={{0,6},{1,7},{2,0},{3,1},{4,2},{5,3},{6,4},{7,5},{8,14},{9,15},{10,... | collective-permute-start | bytes 983048 | tf_op jit(solution)/shard_map/ppermute | solution.py:393
  61.8 12.6 %collective-permute-start.22 = (bf16[256,640]{1,0:T(8,128)(2,1)S(1)}, bf16[256,640]{1,0:T(8,128)(2,1)S(1)}, u32[]{:S(2)}, u32[]{:S(2)}) collective-permute-start(bf16[256,640]{1,0:T(8,128)(2,1)S(1)} %get-tuple-element.118), channel_id=1, source_target_pairs={{0,6},{1,7},{2,0},{3,1},{4,2},{5,3},{6,4},{7,5},{8,14},{9,15},{10,... | collective-permute-start | bytes 983048 | tf_op jit(solution)/shard_map/ppermute | solution.py:400
  63.8 10.6 %collective-permute-start.23 = (bf16[256,640]{1,0:T(8,128)(2,1)S(1)}, bf16[256,640]{1,0:T(8,128)(2,1)S(1)}, u32[]{:S(2)}, u32[]{:S(2)}) collective-permute-start(bf16[256,640]{1,0:T(8,128)(2,1)S(1)} %get-tuple-element.119), channel_id=1, source_target_pairs={{0,2},{1,3},{2,4},{3,5},{4,6},{5,7},{6,0},{7,1},{8,10},{9,11},{10,... | collective-permute-start | bytes 983048 | tf_op jit(solution)/shard_map/ppermute | solution.py:399
  74.5 10.2 %collective-permute-start.24 = (bf16[256,640]{1,0:T(8,128)(2,1)S(1)}, bf16[256,640]{1,0:T(8,128)(2,1)S(1)}, u32[]{:S(2)}, u32[]{:S(2)}) collective-permute-start(bf16[256,640]{1,0:T(8,128)(2,1)S(1)} %turn.1), channel_id=1, source_target_pairs={{0,1},{1,0},{2,3},{3,2},{4,5},{5,4},{6,7},{7,6},{8,9},{9,8},{10,11... | collective-permute-start | bytes 983048 | tf_op jit(solution)/shard_map/ppermute | solution.py:46
  76.9 8.1 %collective-permute-start.25 = (bf16[128,640]{1,0:T(8,128)(2,1)S(1)}, bf16[128,640]{1,0:T(8,128)(2,1)S(1)}, u32[]{:S(2)}, u32[]{:S(2)}) collective-permute-start(bf16[128,640]{1,0:T(8,128)(2,1)S(1)} %get-tuple-element.126), channel_id=1, source_target_pairs={{0,2},{1,3},{2,4},{3,5},{4,6},{5,7},{6,0},{7,1},{8,10},{9,11},{10,... | collective-permute-start | bytes 491528 | tf_op jit(solution)/shard_map/ppermute | solution.py:411
  78.4 6.6 %collective-permute-start.26 = (bf16[128,640]{1,0:T(8,128)(2,1)S(1)}, bf16[128,640]{1,0:T(8,128)(2,1)S(1)}, u32[]{:S(2)}, u32[]{:S(2)}) collective-permute-start(bf16[128,640]{1,0:T(8,128)(2,1)S(1)} %get-tuple-element.127), channel_id=1, source_target_pairs={{0,6},{1,7},{2,0},{3,1},{4,2},{5,3},{6,4},{7,5},{8,14},{9,15},{10,... | collective-permute-start | bytes 491528 | tf_op jit(solution)/shard_map/ppermute | solution.py:411
  80.2 7.5 %collective-permute-start.27 = (bf16[128,640]{1,0:T(8,128)(2,1)S(1)}, bf16[128,640]{1,0:T(8,128)(2,1)S(1)}, u32[]{:S(2)}, u32[]{:S(2)}) collective-permute-start(bf16[128,640]{1,0:T(8,128)(2,1)S(1)} %get-tuple-element.128), channel_id=1, source_target_pairs={{0,4},{1,5},{2,6},{3,7},{4,0},{5,1},{6,2},{7,3},{8,12},{9,13},{10,... | collective-permute-start | bytes 491528 | tf_op jit(solution)/shard_map/ppermute | solution.py:411
